TPU v7x, 32 devices: a whole 2x2x4 slice. The times are simulated.
32 devices in a mesh: row: 4 (over z), col: 8 (over y, x, core).
Axes of the slice: x: 2, y: 2, z: 4, core: 2. Of those that a mesh axis runs over, the one named last changes fastest.
Arguments:
- ingest_features: bfloat16 [8192, 1536], P(('row', 'col')), may hold values from -40 to 40
- node_map: int32 [8192], P(('row', 'col')), may hold values from 0 to 4095, as said below
- unit_rows: int32 [32], P(('row', 'col')), may hold values from 0 to 256, as said below
- tile_ids: int32 [768, 2], P(('row', 'col')), may hold values from 0 to 32, as said below
- tile_values: bfloat16 [768, 128, 128], P(('row', 'col')), may hold values from -40 to 40
- mix_in: bfloat16 [128, 128], replicated, may hold values from -0.5 to 0.5
- mix_out: bfloat16 [128, 128], replicated, may hold values from -0.5 to 0.5
Outputs:
- residual: float32 [4096, 1536], P(('row', 'col'))
Inputs may be any that keep to these rules, and one draw needn't show every extreme that they name: `node_map`: for every unit u the first unit_rows[u] of its 256 slots name distinct nodes, and all units' such slots together name every node exactly once; at most 8 of them of one unit name nodes of one partition (nodes k * 128 to (k + 1) * 128 - 1), and one unit names exactly 8 in every partition. Entries of the other slots are arbitrary nodes. `unit_rows`: one unit delivers 256 rows. `tile_ids`: slots k * 24 to (k + 1) * 24 - 1 hold first some distinct tiles whose row tile lies in row block k // 8 (tile rows (8 times that) onward) and whose column tile lies in column block k % 8, then padding slots whose row tile and column tile are both 4096 // 128. Some blocks have no padding slot.
All inputs are finite; a program needn't handle non-finite values.
Results may differ from a plain program's by a relative error of at most 0.0095.
Values may be sent and summed in bfloat16 or wider, within the bound.
No kernel may reach another device: no remote copies, remote signals or barrier semaphores. Data moves between devices by JAX's collectives and lax.ppermute only.
A program may use at most 64 MiB of HBM per device.

v0:
```python
import jax
import jax.numpy as jnp
from jax import lax
from jax.sharding import PartitionSpec as P

CH = 128
TILE = 128
PIECE = 128


epsilon = 1e-05


def normalize(values):
    groups = values.reshape(-1, CH)
    power = jnp.mean(groups * groups, axis=-1, keepdims=True)
    return (groups * lax.rsqrt(power + epsilon)).astype(jnp.bfloat16)


def encode(totals, mix_in):
    row_total = totals.shape[0]
    mixed = jnp.dot(normalize(totals), mix_in, preferred_element_type=jnp.float32)
    return jax.nn.gelu(mixed, approximate=False).astype(jnp.bfloat16).reshape(row_total, -1)


def dense_block(tile_ids, tile_values, row_index, col_index, row_tiles, col_tiles):
    local_rows = tile_ids[:, 0] - row_index * row_tiles
    local_cols = tile_ids[:, 1] - col_index * col_tiles
    tile_edge = tile_values.shape[1]
    tile_grid = jnp.zeros((row_tiles, col_tiles, tile_edge, tile_edge), tile_values.dtype)
    tile_grid = tile_grid.at[local_rows, local_cols].set(tile_values, mode="drop")
    return tile_grid.transpose(0, 2, 1, 3).reshape(row_tiles * tile_edge, col_tiles * tile_edge)


def local(ingest_features, node_map, unit_rows, tile_ids, tile_values, mix_in, mix_out):
    row_count = lax.axis_size("row")
    col_count = lax.axis_size("col")
    unit_count = row_count * col_count
    slots_held = node_map.shape[0]
    per_pair = slots_held // unit_count
    feature_width = ingest_features.shape[1]
    owner = node_map // PIECE
    live = jnp.arange(slots_held, dtype=jnp.int32) < unit_rows[0]
    member = (
        (owner[:, None] == jnp.arange(unit_count, dtype=jnp.int32)[None, :]) & live[:, None]
    ).astype(jnp.int32)
    earlier = jnp.cumsum(member, axis=0) - member
    rank_within = jnp.sum(earlier * member, axis=1)
    target = jnp.where(live, owner * per_pair + rank_within, unit_count * per_pair)
    outgoing = (
        jnp.zeros((unit_count * per_pair, feature_width), jnp.bfloat16)
        .at[target]
        .set(ingest_features, mode="drop")
    )
    placing = (
        jnp.full((unit_count * per_pair,), -1, jnp.int32)
        .at[target]
        .set(node_map % PIECE, mode="drop")
    )
    arrived, arrived_at = (
        lax.all_to_all(
            outgoing.reshape(unit_count, per_pair, feature_width),
            ("row", "col"),
            split_axis=0,
            concat_axis=0,
            tiled=True,
        ),
        lax.all_to_all(
            placing.reshape(unit_count, per_pair),
            ("row", "col"),
            split_axis=0,
            concat_axis=0,
            tiled=True,
        ),
    )
    arrived = arrived.reshape(-1, feature_width)
    arrived_at = arrived_at.reshape(-1)
    landing = jnp.where(arrived_at >= 0, arrived_at, PIECE)
    features = jnp.zeros((PIECE, feature_width), jnp.bfloat16).at[landing].set(arrived, mode="drop")
    row_tiles = col_count * PIECE // TILE
    col_tiles = row_count * PIECE // TILE
    block = dense_block(
        tile_ids, tile_values, lax.axis_index("row"), lax.axis_index("col"), row_tiles, col_tiles
    )
    strip = block
    back_part = lax.dot_general(
        strip,
        lax.all_gather(features, "col", axis=0, tiled=True),
        (((0,), (0,)), ((), ())),
        preferred_element_type=jnp.float32,
    )
    back_own = lax.psum_scatter(
        back_part.astype(jnp.bfloat16), "row", scatter_dimension=0, tiled=True
    ).astype(jnp.float32)
    hidden = lax.all_gather(encode(back_own, mix_in), "row", axis=0, tiled=True)
    strip = block
    forward_sum = lax.psum_scatter(
        jnp.dot(strip, hidden, preferred_element_type=jnp.float32).astype(jnp.bfloat16),
        "col",
        scatter_dimension=0,
        tiled=True,
    ).astype(jnp.float32)
    recon = jnp.dot(normalize(forward_sum), mix_out, preferred_element_type=jnp.float32).reshape(
        PIECE, feature_width
    )
    return features.astype(jnp.float32) - recon


def solution(mesh):
    return jax.shard_map(
        local,
        mesh=mesh,
        in_specs=(
            P(("row", "col"), None),
            P(("row", "col")),
            P(("row", "col")),
            P(("row", "col"), None),
            P(("row", "col"), None, None),
            P(),
            P(),
        ),
        out_specs=P(("row", "col"), None),
        check_vma=False,
    )
```

profile of v0, /device:TPU:0, one launch (start us, length us, event | category | flops | bytes accessed | tf_op | source)
XLA Modules:
  0.0 224.5 jit_solution(14874546171349204794)
XLA Ops:
  7.3 0.7 and_select_fusion
  8.9 1.4 scatter_custom_fusion
  10.3 0.7 all_to_all.9
  11.0 7.3 %all-to-all-start = ((s32[32,1,8]{2,1,0:T(1,128)}), s32[32,1,8]{2,1,0:T(1,128)S(1)}, u32[]{:S(2)}, u32[]{:S(2)}) async-start(s32[32,1,8]{2,1,0:T(1,128)} %bitcast.3), calls=%async_computation | async-start | bytes 32768 | tf_op jit(solution)/shard_map/all_to_all | solution.py:68
  18.3 3.3 %scatter_custom_fusion.1 = bf16[256,1536]{1,0:T(8,128)(2,1)} fusion(s32[256]{0:T(256)S(1)} %compare_select_fusion.2, bf16[256,1536]{1,0:T(8,128)(2,1)} %param.7, bf16[]{:T(256)} %constant.44.clone.1), kind=kCustom, calls=%fused_computation.40 | custom fusion | bytes 786944 | tf_op jit(solution)/shard_map/scatter | solution.py:53
  21.6 3.9 %all-to-all-done = s32[32,1,8]{2,1,0:T(1,128)S(1)} async-done(((s32[32,1,8]{2,1,0:T(1,128)}), s32[32,1,8]{2,1,0:T(1,128)S(1)}, u32[]{:S(2)}, u32[]{:S(2)}) %all-to-all-start) | async-done | bytes 1056 | tf_op jit(solution)/shard_map/all_to_all | solution.py:68
  25.5 2.6 %all-to-all-start.1 = ((bf16[32,8,1536]{2,1,0:T(8,128)(2,1)}), bf16[32,8,1536]{2,1,0:T(8,128)(2,1)S(1)}, u32[]{:S(2)}, u32[]{:S(2)}) async-start(bf16[32,8,1536]{2,1,0:T(8,128)(2,1)} %bitcast.5), calls=%async_computation.1 | async-start | bytes 1572864 | tf_op jit(solution)/shard_map/all_to_all | solution.py:61
  28.2 0.6 broadcast.176
  28.7 0.7 reduce.5
  29.6 19.1 %all-to-all-done.1 = bf16[32,8,1536]{2,1,0:T(8,128)(2,1)S(1)} async-done(((bf16[32,8,1536]{2,1,0:T(8,128)(2,1)}), bf16[32,8,1536]{2,1,0:T(8,128)(2,1)S(1)}, u32[]{:S(2)}, u32[]{:S(2)}) %all-to-all-start.1) | async-done | bytes 786464 | tf_op jit(solution)/shard_map/all_to_all | solution.py:61
  48.7 2.5 %scatter_custom_fusion.2 = bf16[128,1536]{1,0:T(8,128)(2,1)} fusion(s32[256]{0:T(256)S(1)} %bitcast.54, bf16[32,8,1536]{2,1,0:T(8,128)(2,1)S(1)} %all-to-all-done.1, bf16[]{:T(256)} %constant.44.clone.1), kind=kCustom, calls=%fused_computation.14 | custom fusion | bytes 1179650 | tf_op jit(solution)/shard_map/scatter | solution.py:79
  51.5 2.0 scatter_fusion
  53.6 0.7 copy.12
  54.3 28.3 %all-gather.3.cloned.1.call-done = bf16[1024,1536]{1,0:T(8,128)(2,1)} async-done(((bf16[128,1536]{1,0:T(8,128)(2,1)}), bf16[1024,1536]{1,0:T(8,128)(2,1)}) %all-gather.3.cloned.1.call-update) | async-done | bytes 3145744 | tf_op jit(solution)/shard_map/all_gather | solution.py:88
  82.6 4.8 %convolution_convert_fusion.1 = bf16[512,1536]{1,0:T(8,128)(2,1)} fusion(bf16[1024,1536]{1,0:T(8,128)(2,1)} %all-gather.3.cloned.1.call-done, bf16[64,8,8,128]{3,2,1,0:T(8,128)(2,1)S(1)} %bitcast.51), kind=kOutput, calls=%fused_computation.5 | convolution fusion | flops 1611399168 | bytes 5767168 | tf_op jit(solution)/shard_map/dot_general | solution.py:86
  87.5 35.4 %reduce-scatter.3.cloned.1.call-done = bf16[128,1536]{1,0:T(8,128)(2,1)} async-done(((bf16[512,1536]{1,0:T(8,128)(2,1)}), bf16[128,1536]{1,0:T(8,128)(2,1)}) %reduce-scatter.3.cloned.1.call-update) | async-done | bytes 393232 | tf_op jit(solution)/shard_map/reduce_scatter | solution.py:92
  122.9 1.4 reshape.117
  124.7 2.4 %fusion.6 = bf16[1536,128]{1,0:T(8,128)(2,1)S(1)} fusion(bf16[128,128]{1,0:T(8,128)(2,1)S(1)} %copy-done, f32[1536,128]{1,0:T(8,128)S(1)} %reshape.117, f32[1536]{0:T(1024)S(1)} %add_rsqrt_fusion.1), kind=kOutput, calls=%fused_computation.13 | convolution fusion | flops 63504384 | bytes 1218560 | tf_op jit(solution)/shard_map/dot_general | solution.py:22
  127.1 1.2 reshape.112
  128.5 36.0 %all-gather.5.cloned.1.call-done = bf16[512,1536]{1,0:T(8,128)(2,1)} async-done(((bf16[128,1536]{1,0:T(8,128)(2,1)}), bf16[512,1536]{1,0:T(8,128)(2,1)}) %all-gather.5.cloned.1.call-update) | async-done | bytes 1572880 | tf_op jit(solution)/shard_map/all_gather | solution.py:95
  164.5 4.9 %convolution_convert_fusion = bf16[1024,1536]{1,0:T(8,128)(2,1)} fusion(bf16[512,1536]{1,0:T(8,128)(2,1)} %all-gather.5.cloned.1.call-done, bf16[64,8,8,128]{3,2,1,0:T(8,128)(2,1)S(1)} %bitcast.52), kind=kOutput, calls=%fused_computation.4 | convolution fusion | flops 1612185600 | bytes 5767168 | tf_op jit(solution)/shard_map/dot_general | solution.py:98
  169.5 45.3 %reduce-scatter.5.cloned.1.call-done = bf16[128,1536]{1,0:T(8,128)(2,1)} async-done(((bf16[1024,1536]{1,0:T(8,128)(2,1)}), bf16[128,1536]{1,0:T(8,128)(2,1)}) %reduce-scatter.5.cloned.1.call-update) | async-done | bytes 393232 | tf_op jit(solution)/shard_map/reduce_scatter | solution.py:97
  214.7 1.4 reshape.119
  217.0 1.0 convert_subtract_fusion
  (37 shorter events, 2.8 us)
Async XLA Ops:
  6.5 118.1 %copy-start = (bf16[128,128]{1,0:T(8,128)(2,1)S(1)}, bf16[128,128]{1,0:T(8,128)(2,1)}, u32[]{:S(2)}) copy-start(bf16[128,128]{1,0:T(8,128)(2,1)} %param.12) | copy-start | bytes 98308
  6.5 44.7 %copy-start.4 = (s32[24,2]{0,1:T(2,128)S(1)}, s32[24,2]{0,1:T(2,128)}, u32[]{:S(2)}) copy-start(s32[24,2]{0,1:T(2,128)} %param.10) | copy-start | bytes 580
  6.5 45.0 %copy-start.2 = (bf16[24,128,128]{2,1,0:T(8,128)(2,1)S(1)}, bf16[24,128,128]{2,1,0:T(8,128)(2,1)}, u32[]{:S(2)}) copy-start(bf16[24,128,128]{2,1,0:T(8,128)(2,1)} %param.11) | copy-start | bytes 2359300
  11.0 14.4 %all-to-all-start = ((s32[32,1,8]{2,1,0:T(1,128)}), s32[32,1,8]{2,1,0:T(1,128)S(1)}, u32[]{:S(2)}, u32[]{:S(2)}) async-start(s32[32,1,8]{2,1,0:T(1,128)} %bitcast.3), calls=%async_computation | async-start | bytes 32768 | tf_op jit(solution)/shard_map/all_to_all | solution.py:68
  25.5 23.2 %all-to-all-start.1 = ((bf16[32,8,1536]{2,1,0:T(8,128)(2,1)}), bf16[32,8,1536]{2,1,0:T(8,128)(2,1)S(1)}, u32[]{:S(2)}, u32[]{:S(2)}) async-start(bf16[32,8,1536]{2,1,0:T(8,128)(2,1)} %bitcast.5), calls=%async_computation.1 | async-start | bytes 1572864 | tf_op jit(solution)/shard_map/all_to_all | solution.py:61
  28.1 54.5 %all-gather.3.cloned.1.call-start = ((), (), s32[]{:S(2)}) async-start(), calls=%async_computation.4 | async-start | bytes 3538944 | tf_op jit(solution)/shard_map/all_gather | solution.py:88
  51.2 71.7 %reduce-scatter.3.cloned.1.call-start = ((), (), s32[]{:S(2)}) async-start(), calls=%async_computation.5 | async-start | bytes 1966080 | tf_op jit(solution)/shard_map/reduce_scatter | solution.py:92
  87.5 77.0 %all-gather.5.cloned.1.call-start = ((), (), s32[]{:S(2)}) async-start(), calls=%async_computation.6 | async-start | bytes 1966080 | tf_op jit(solution)/shard_map/all_gather | solution.py:95
  128.3 86.4 %reduce-scatter.5.cloned.1.call-start = ((), (), s32[]{:S(2)}) async-start(), calls=%async_computation.7 | async-start | bytes 3538944 | tf_op jit(solution)/shard_map/reduce_scatter | solution.py:97
  169.4 47.0 %copy-start.3 = (bf16[128,128]{1,0:T(8,128)(2,1)S(1)}, bf16[128,128]{1,0:T(8,128)(2,1)}, u32[]{:S(2)}) copy-start(bf16[128,128]{1,0:T(8,128)(2,1)} %param.13) | copy-start | bytes 98308
  169.4 47.5 %copy-start.1 = (bf16[128,1536]{1,0:T(8,128)(2,1)S(1)}, bf16[128,1536]{1,0:T(8,128)(2,1)}, u32[]{:S(2)}) copy-start(bf16[128,1536]{1,0:T(8,128)(2,1)} %scatter_custom_fusion.2) | copy-start | bytes 1179652
Sparse Core Ops, SparseCore 0:
  51.3 31.2 all-gather.2
  87.6 35.2 reduce-scatter.2
  128.4 36.0 all-gather.4
  169.6 45.0 reduce-scatter.4
where the time goes:
time: 225 us; the launch traced here: 224 us
  waiting for transfers between devices  168 us (75%)
  local copies, waits for them, and re-layouts  15.9 us (7%)
  between operations  14.1 us (6%)
  matrix products  12.5 us (6%)
  starting transfers between devices  10.3 us (5%)
  other arithmetic  3.72 us (2%)
    reduce_scatter x1, waiting for transfers between devices, local(): lax.psum_scatter(jnp.dot(strip, hidden, preferred_element_type=jnp.float3...  45.3 us
    all_gather x1, waiting for transfers between devices, local(): hidden = lax.all_gather(encode(back_own, mix_in), 'row', axis=0, tiled=True)  36 us
    reduce_scatter x1, waiting for transfers between devices, local(): lax.psum_scatter(back_part.astype(jnp.bfloat16), 'row', scatter_dimension...  35.4 us
    all_gather x1, waiting for transfers between devices, local(): lax.all_gather(features, 'col', axis=0, tiled=True)  28.3 us
    all_to_all x1, waiting for transfers between devices, local(): lax.all_to_all(outgoing.reshape(unit_count, per_pair, feature_width), ('r...  19.1 us
    all_to_all x1, starting transfers between devices, local(): lax.all_to_all(placing.reshape(unit_count, per_pair), ('row', 'col'), spl...  7.3 us
    dot_general x1, matrix products, local(): jnp.dot(strip, hidden, preferred_element_type=jnp.float32)  4.91 us
    dot_general x1, matrix products, local(): lax.dot_general(strip, lax.all_gather(features, 'col', axis=0, tiled=True...  4.82 us
  transfers between devices with their start and end apart: 6, of which 6 were waited for; matrix products, arithmetic and copies ran while one was open for 3% of the time, Pallas kernels for 0%

commit v1 on v0

v1 whole, which is shorter than its diff:
```python
import functools

import jax
import jax.numpy as jnp
from jax import lax
from jax.experimental import pallas as pl
from jax.experimental.pallas import tpu as pltpu
from jax.sharding import PartitionSpec as P

CH = 128
TILE = 128
PIECE = 128
QUARTERS = 4
VMEM_LIMIT = 56 * 1024 * 1024

epsilon = 1e-05

BF16 = jnp.bfloat16
F32 = jnp.float32
VM = pl.BlockSpec(memory_space=pltpu.VMEM)
SM = pl.BlockSpec(memory_space=pltpu.SMEM)


def iota(shape, axis):
    return lax.broadcasted_iota(jnp.int32, shape, axis)


def call(kernel, out_shape, in_specs, out_specs=None, flops=0, bytes_accessed=0, **kw):
    many = isinstance(out_shape, (list, tuple))
    if out_specs is None:
        out_specs = [VM] * len(out_shape) if many else VM
    return pl.pallas_call(
        kernel,
        out_shape=out_shape,
        in_specs=in_specs,
        out_specs=out_specs,
        compiler_params=pltpu.CompilerParams(vmem_limit_bytes=VMEM_LIMIT),
        cost_estimate=pl.CostEstimate(
            flops=flops, bytes_accessed=bytes_accessed, transcendentals=0
        ),
        **kw,
    )


class Layout:
    def __init__(self, rows, cols, slots, width):
        self.R, self.C = rows, cols
        self.R2, self.chips = rows // 2, cols // 2
        self.U = rows * cols
        self.slots = slots
        self.pair = slots // self.U
        self.slab = 4 * self.pair
        self.upl = CH // self.slab
        self.groups = width // CH // QUARTERS
        self.qw = self.groups * CH
        self.blocks = self.R2 * self.chips
        self.own = 4 * PIECE
        self.chip_cols = 2 * rows * TILE
        self.tpl = 2 * rows // self.R2
        self.pay = self.groups * self.slab + 8

    def split_z(self, z):
        return z // self.R2, z % self.R2

    def join_z(self, h, l):
        return h * self.R2 + l


def pack_kernel(lay, me, node, feats, out):
    unit, count = me[0], me[1]
    n = lay.slots
    row = node[...]
    slot = iota((1, n), 1)
    live = slot < count
    p = row // PIECE
    h, l = lay.split_z(p // lay.C)
    c = p % lay.C
    block = l * lay.chips + c // 2
    part = h * 2 + c % 2
    p = jnp.where(live, p, -1)
    across = jnp.broadcast_to(p, (n, n))
    down = jnp.transpose(across)
    before = (across == down) & (iota((n, n), 0) < iota((n, n), 1))
    rank = jnp.sum(jnp.where(before, 1, 0), axis=0, keepdims=True)
    target = jnp.where(live, (block * 4 + part) * lay.pair + rank, -1)
    pick = jnp.where(iota((n, n), 0) == target, 1.0, 0.0).astype(BF16)
    sorted_rows = jnp.dot(pick, feats[...], preferred_element_type=F32).astype(BF16)
    place = jnp.where(live, row % PIECE + 1, 0).astype(F32).astype(BF16)
    place = jnp.broadcast_to(place, (16, n))
    lane = iota((lay.blocks * CH, n), 0)
    inner = lane % CH - (unit % lay.upl) * lay.slab
    wanted = (lane // CH) * lay.slab + inner
    wanted = jnp.where((inner >= 0) & (inner < lay.slab), wanted, -2)
    spread = jnp.where(wanted == target, 1.0, 0.0).astype(BF16)
    places = lax.dot_general(
        place, spread, (((1,), (1,)), ((), ())), preferred_element_type=F32
    ).astype(BF16)
    for z in range(lay.R):
        dh, dl = lay.split_z(z)
        for c in range(lay.C):
            b = dl * lay.chips + c // 2
            q = dh * 2 + c % 2
            d = z * lay.C + c
            for g in range(lay.groups):
                lo = q * lay.qw + g * CH
                out[d, g * lay.slab : (g + 1) * lay.slab, :] = sorted_rows[
                    b * lay.slab : (b + 1) * lay.slab, lo : lo + CH
                ]
            out[d, lay.groups * lay.slab : lay.pay, :] = places[0:8, b * CH : (b + 1) * CH]


def land_kernel(lay, chunks, me, got, *outs):
    mine = me[2]
    lane = iota((1, CH), 1)
    part = (lane % lay.slab) // lay.pair
    base = (part ^ mine) * PIECE - 1
    rows = iota((lay.own, CH), 0)
    picks = []
    for j in range(lay.U // lay.upl):
        total = jnp.zeros((8, CH), F32)
        for i in range(lay.upl):
            total = total + got[j * lay.upl + i, lay.groups * lay.slab : lay.pay, :].astype(F32)
        place = total[0:1, :].astype(jnp.int32)
        spot = jnp.where(place > 0, base + place, -1)
        picks.append(jnp.where(rows == spot, 1.0, 0.0).astype(BF16))
    pick = jnp.concatenate(picks, axis=1)
    for out, (first, many) in zip(outs, chunks):
        for g in range(many):
            lo = (first + g) * lay.slab
            block = got[:, lo : lo + lay.slab, :].reshape(lay.U * lay.slab, CH)
            out[:, g * CH : (g + 1) * CH] = jnp.dot(
                pick, block, preferred_element_type=F32
            ).astype(BF16)


def dense_kernel(lay, step_rows, me, i0, i1, i2, i3, v0, v1, v2, v3, a, at):
    h, l, chip, core = me[3], me[4], me[5], me[6]
    first = pl.program_id(0) * step_rows
    a[...] = jnp.zeros_like(a)
    at[...] = jnp.zeros_like(at)
    tiles = step_rows // TILE
    for ids, values in ((i0, v0), (i1, v1), (i2, v2), (i3, v3)):

        def body(t, carry, ids=ids, values=values):
            rt, ct = ids[2 * t], ids[2 * t + 1]
            zh, zl = lay.split_z(rt // lay.C)
            c = rt % lay.C
            r = ((c // 2) ^ chip) * 4 + (zh ^ h) * 2 + ((c % 2) ^ core) - first // TILE
            cc = ct // lay.R
            j = (cc % 2) * lay.R + ct % lay.R
            k = ((j // lay.tpl) ^ l) * lay.tpl + j % lay.tpl

            @pl.when((rt < lay.U) & (r >= 0) & (r < tiles))
            def _():
                rr = pl.multiple_of(r * TILE, TILE)
                kk = pl.multiple_of(k * TILE, TILE)
                tile = values[t]
                a[pl.ds(rr, TILE), pl.ds(kk, TILE)] = tile
                at[pl.ds(kk, TILE), pl.ds(rr, TILE)] = jnp.transpose(tile)

            return carry

        lax.fori_loop(0, values.shape[0], body, 0)


def product_kernel(parts, *refs):
    lhs, rhs, out = refs[0], refs[1 : 1 + parts], refs[1 + parts]
    total = None
    at = 0
    for ref in rhs:
        depth = ref.shape[0]
        one = jnp.dot(lhs[:, at : at + depth], ref[...], preferred_element_type=F32)
        total = one if total is None else total + one
        at += depth
    out[...] = total.astype(out.dtype)


def product(lhs, rhs, first, rows, block=256):
    depth, width = lhs.shape[1], rhs[0].shape[1]
    skip = first // block
    return call(
        functools.partial(product_kernel, len(rhs)),
        jax.ShapeDtypeStruct((rows, width), BF16),
        [pl.BlockSpec((block, depth), lambda i: (skip + i, 0))]
        + [pl.BlockSpec(r.shape, lambda i: (0, 0)) for r in rhs],
        pl.BlockSpec((block, width), lambda i: (i, 0)),
        grid=(rows // block,),
        flops=2 * rows * depth * width,
        bytes_accessed=2 * (rows * depth + depth * width + rows * width),
    )(lhs, *rhs)


def unit_groups(total):
    power = jnp.mean(total * total, axis=-1, keepdims=True)
    return (total * lax.rsqrt(power + epsilon)).astype(BF16)


def encode_kernel(mix, *refs):
    parts, out = refs[:-1], refs[-1]
    for g in range(out.shape[1] // CH):
        span = slice(g * CH, (g + 1) * CH)
        total = parts[0][:, span].astype(F32)
        for ref in parts[1:]:
            total = total + ref[:, span].astype(F32)
        v = jnp.dot(unit_groups(total), mix[...], preferred_element_type=F32)
        out[:, span] = (0.5 * v * (1.0 + lax.erf(v * (0.5**0.5)))).astype(BF16)


def decode_kernel(parts, mix, x, *refs):
    sums, outs = refs[:parts], refs[parts:]
    for g in range(x.shape[1] // CH):
        span = slice(g * CH, (g + 1) * CH)
        total = sums[0][:, span].astype(F32)
        for ref in sums[1:]:
            total = total + ref[:, span].astype(F32)
        recon = jnp.dot(unit_groups(total), mix[...], preferred_element_type=F32)
        left = x[:, span].astype(F32) - recon
        for i, out in enumerate(outs):
            out[:, span] = left[i * PIECE : (i + 1) * PIECE, :].astype(out.dtype)


def join_kernel(lay, chunks, me, *refs):
    out = refs[-1]
    mine = me[2]
    for n, (first, many) in enumerate(chunks):
        for rel in range(4):
            at = pl.multiple_of((mine ^ rel) * lay.qw + first * CH, CH)
            out[:, pl.ds(at, many * CH)] = refs[n * 4 + rel][...].astype(F32)


CHUNKS = ((0, 3),)


def local(lay, ingest_features, node_map, unit_rows, tile_ids, tile_values, mix_in, mix_out):
    z, c = lax.axis_index("row"), lax.axis_index("col")
    h, l = lay.split_z(z)
    me = jnp.stack(
        [z * lay.C + c, unit_rows[0], h * 2 + c % 2, h, l, c // 2, c % 2]
    ).astype(jnp.int32)

    def exchange(x, dh=0, dl=0, chip=0, core=0):
        pairs = []
        for zz in range(lay.R):
            hh, ll = lay.split_z(zz)
            for cc in range(lay.C):
                to = lay.join_z(hh ^ dh, ll ^ dl) * lay.C + (cc ^ (chip * 2 + core))
                pairs.append((zz * lay.C + cc, to))
        return lax.ppermute(x, ("row", "col"), pairs)

    chunks = tuple((f, min(m, lay.groups - f)) for f, m in CHUNKS)

    outgoing = call(
        functools.partial(pack_kernel, lay),
        jax.ShapeDtypeStruct((lay.U, lay.pay, CH), BF16),
        [SM, VM, VM],
    )(me, node_map.reshape(1, lay.slots), ingest_features)
    got = lax.all_to_all(outgoing, ("row", "col"), split_axis=0, concat_axis=0, tiled=True)

    ids0 = tile_ids.reshape(-1)
    ids1, val1 = exchange(ids0, dh=1), exchange(tile_values, dh=1)
    ids2, val2 = exchange(ids0, core=1), exchange(tile_values, core=1)
    ids3, val3 = exchange(ids1, core=1), exchange(val1, core=1)

    depth = lay.chips * lay.own
    step_rows = depth if depth * lay.chip_cols <= 2048 * 1024 else lay.own
    held = pl.BlockSpec(tile_values.shape, lambda i: (0, 0, 0))
    a, at = call(
        functools.partial(dense_kernel, lay, step_rows),
        [
            jax.ShapeDtypeStruct((depth, lay.chip_cols), BF16),
            jax.ShapeDtypeStruct((lay.chip_cols, depth), BF16),
        ],
        [SM] * 5 + [held] * 4,
        [
            pl.BlockSpec((step_rows, lay.chip_cols), lambda i: (i, 0)),
            pl.BlockSpec((lay.chip_cols, step_rows), lambda i: (0, i)),
        ],
        grid=(depth // step_rows,),
    )(me, ids0, ids1, ids2, ids3, tile_values, val1, val2, val3)

    own = call(
        functools.partial(land_kernel, lay, chunks),
        [jax.ShapeDtypeStruct((lay.own, m * CH), BF16) for _, m in chunks],
        [SM, VM],
    )(me, got)

    share = lay.chip_cols // lay.R2
    pieces = []
    for x in own:
        width = x.shape[1]
        xs = [x] + [exchange(x, chip=s) for s in range(1, lay.chips)]
        back = [
            exchange(product(at, xs, s * share, share), dl=s) for s in range(1, lay.R2)
        ]
        back = [product(at, xs, 0, share)] + back
        hidden = call(
            encode_kernel,
            jax.ShapeDtypeStruct((share, width), BF16),
            [VM] * (1 + lay.R2),
        )(mix_in, *back)
        hs = [hidden] + [exchange(hidden, dl=s) for s in range(1, lay.R2)]
        forward = [
            exchange(product(a, hs, s * lay.own, lay.own), chip=s)
            for s in range(1, lay.chips)
        ]
        forward = [product(a, hs, 0, lay.own)] + forward
        left = call(
            functools.partial(decode_kernel, lay.chips),
            [
                jax.ShapeDtypeStruct((PIECE, width), F32 if i == 0 else BF16)
                for i in range(4)
            ],
            [VM] * (2 + lay.chips),
        )(mix_out, x, *forward)
        pieces += [
            left[0],
            exchange(left[1], core=1),
            exchange(left[2], dh=1),
            exchange(left[3], dh=1, core=1),
        ]
    return call(
        functools.partial(join_kernel, lay, chunks),
        jax.ShapeDtypeStruct((PIECE, QUARTERS * lay.qw), F32),
        [SM] + [VM] * len(pieces),
    )(me, *pieces)


def solution(mesh):
    rows, cols = mesh.shape["row"], mesh.shape["col"]

    def run(ingest_features, node_map, *rest):
        lay = Layout(
            rows, cols, node_map.shape[0] // (rows * cols), ingest_features.shape[1]
        )
        return jax.shard_map(
            functools.partial(local, lay),
            mesh=mesh,
            in_specs=(
                P(("row", "col"), None),
                P(("row", "col")),
                P(("row", "col")),
                P(("row", "col"), None),
                P(("row", "col"), None, None),
                P(),
                P(),
            ),
            out_specs=P(("row", "col"), None),
            check_vma=False,
        )(ingest_features, node_map, *rest)

    return run
```

time: 225 us -> 167 us (0.74)
  waiting for transfers between devices: 168 us -> 91.6 us
  Pallas kernels: 0 us -> 44.9 us
  between operations: 14.1 us -> 0.79 us
  matrix products: 12.5 us -> 0 us
  starting transfers between devices: 10.3 us -> 20.7 us
  local copies, waits for them, and re-layouts: 15.9 us -> 8.5 us
  other arithmetic: 3.72 us -> 0 us
    ppermute x0 -> x17, waiting for transfers between devices: none -> 91.6 us  [exchange(): return lax.ppermute(x, ('row', 'col'), pairs)]
    reduce_scatter x2 -> x0, waiting for transfers between devices: 80.6 us -> none  [the longest x1 45.3 us: local(): lax.psum_scatter(jnp.dot(strip, hidden, preferred_element_type=jnp.float3...]
    all_gather x2 -> x0, waiting for transfers between devices: 64.3 us -> none  [the longest x1 36 us: local(): hidden = lax.all_gather(encode(back_own, mix_in), 'row', axis=0, tiled=True)]
    pallas_call x0 -> x12, Pallas kernels: none -> 44.9 us  [the longest x6 19 us: product(): call(functools.partial(product_kernel, len(rhs)), jax.ShapeDtypeStruct((r...]
    all_to_all x2 -> x1, waiting for transfers between devices: 23 us -> 0.01 us  [local(): lax.all_to_all(outgoing, ('row', 'col'), split_axis=0, concat_axis=0, til...]
    ppermute x0 -> x17, starting transfers between devices: none -> 13.4 us  [exchange(): return lax.ppermute(x, ('row', 'col'), pairs)]
    dot_general x4 -> x0, matrix products: 12.5 us -> none  [the longest x1 4.91 us: local(): jnp.dot(strip, hidden, preferred_element_type=jnp.float32)]
    scatter x4 -> x0, local copies, waits for them, and re-layouts: 9.21 us -> none  [the longest x1 3.29 us: local(): outgoing = jnp.zeros((unit_count * per_pair, feature_width), jnp.bfloat16...]
  transfers between devices with their start and end apart: 6 -> 18, of which waited for: 6 -> 9; matrix products, arithmetic and copies ran while one was open for 3% -> 1% of each run, Pallas kernels for 0% -> 17%
where the time goes in v1:
time: 167 us; the launch traced here: 166 us
  waiting for transfers between devices  91.6 us (55%)
  Pallas kernels  44.9 us (27%)
  starting transfers between devices  20.7 us (12%)
  local copies, waits for them, and re-layouts  8.5 us (5%)
    ppermute x17, waiting for transfers between devices, exchange(): return lax.ppermute(x, ('row', 'col'), pairs)  91.6 us
    pallas_call x6, Pallas kernels, product(): call(functools.partial(product_kernel, len(rhs)), jax.ShapeDtypeStruct((r...  19 us
    ppermute x17, starting transfers between devices, exchange(): return lax.ppermute(x, ('row', 'col'), pairs)  13.4 us
    pallas_call x1, Pallas kernels, local(): call(functools.partial(dense_kernel, lay, step_rows), [jax.ShapeDtypeStru...  13.3 us
    unnamed x39, local copies, waits for them, and re-layouts  7.84 us
    all_to_all x1, starting transfers between devices, local(): lax.all_to_all(outgoing, ('row', 'col'), split_axis=0, concat_axis=0, til...  7.3 us
  transfers between devices with their start and end apart: 18, of which 9 were waited for; matrix products, arithmetic and copies ran while one was open for 1% of the time, Pallas kernels for 17%

profile of v1, /device:TPU:0, one launch (start us, length us, event | category | flops | bytes accessed | tf_op | source)
XLA Modules:
  0.0 166.4 jit_solution(5277807718597003756)
XLA Ops:
  1.2 2.7 %shard_map.73 = bf16[32,104,128]{2,1,0:T(8,128)(2,1)} custom-call(s32[7]{0:T(128)} %stack.27.me, s32[1,256]{1,0:T(1,128)} %bitcast.7, bf16[256,1536]{1,0:T(8,128)(2,1)} %feats.1), custom_call_target="tpu_custom_call" | custom-call | tf_op jit(solution)/shard_map/pallas_call | solution.py:252
  3.9 7.3 %all-to-all-start = ((bf16[32,104,128]{2,1,0:T(8,128)(2,1)}), bf16[32,104,128]{2,1,0:T(8,128)(2,1)S(1)}, u32[]{:S(2)}, u32[]{:S(2)}) async-start(bf16[32,104,128]{2,1,0:T(8,128)(2,1)} %shard_map.73), calls=%async_computation | async-start | bytes 1703936 | tf_op jit(solution)/shard_map/all_to_all | solution.py:257
  11.2 2.7 %collective-permute-start.3 = (bf16[24,128,128]{2,1,0:T(8,128)(2,1)}, bf16[24,128,128]{2,1,0:T(8,128)(2,1)S(1)}, u32[]{:S(2)}, u32[]{:S(2)}) collective-permute-start(bf16[24,128,128]{2,1,0:T(8,128)(2,1)} %v0.1), channel_id=1, source_target_pairs={{0,16},{1,17},{2,18},{3,19},{4,20},{5,21},{6,22},{7,23},{8,24},{9,... | collective-permute-start | bytes 2359304 | tf_op jit(solution)/shard_map/ppermute | solution.py:248
  13.9 53.0 %collective-permute-done.3.v1 = bf16[24,128,128]{2,1,0:T(8,128)(2,1)S(1)} collective-permute-done((bf16[24,128,128]{2,1,0:T(8,128)(2,1)}, bf16[24,128,128]{2,1,0:T(8,128)(2,1)S(1)}, u32[]{:S(2)}, u32[]{:S(2)}) %collective-permute-start.3) | collective-permute-done | bytes 786464 | tf_op jit(solution)/shard_map/ppermute | solution.py:248
  68.4 3.9 %collective-permute-done.i1 = s32[48]{0:T(128)S(1)} collective-permute-done((s32[48]{0:T(128)S(1)}, s32[48]{0:T(128)S(1)}, u32[]{:S(2)}, u32[]{:S(2)}) %collective-permute-start) | collective-permute-done | bytes 224 | tf_op jit(solution)/shard_map/ppermute | solution.py:248
  73.2 2.9 %shard_map.74.refs_1_.x = bf16[512,384]{1,0:T(8,128)(2,1)} custom-call(s32[7]{0:T(128)} %stack.27.me, bf16[32,104,128]{2,1,0:T(8,128)(2,1)} %copy-done.1), custom_call_target="tpu_custom_call" | custom-call | tf_op jit(solution)/shard_map/pallas_call | solution.py:281
  77.6 1.5 collective-permute-start.7
  81.4 13.3 %shard_map.75 = (bf16[2048,1024]{1,0:T(8,128)(2,1)}, bf16[1024,2048]{1,0:T(8,128)(2,1)}) custom-call(s32[7]{0:T(128)} %stack.27.me, s32[48]{0:T(128)} %copy-done.15, s32[48]{0:T(128)} %copy-done.16, s32[48]{0:T(128)} %copy-done.17, s32[48]{0:T(128)} %copy-done.18, bf16[24,128,128]{2,1,0:T(8,128)(2,1)} %v0.1, bf16[24,128,128]{2,1,0:T(8,128)(2,1)} %copy-done.5, ...), custom_call_target="tpu_custom_call" | custom-call | tf_op jit(solution)/shard_map/pallas_call | solution.py:267
  94.7 2.8 %collective-permute-done.7.refs_3_ = bf16[512,384]{1,0:T(8,128)(2,1)S(1)} collective-permute-done((bf16[512,384]{1,0:T(8,128)(2,1)}, bf16[512,384]{1,0:T(8,128)(2,1)S(1)}, u32[]{:S(2)}, u32[]{:S(2)}) %collective-permute-start.7) | collective-permute-done | bytes 393248 | tf_op jit(solution)/shard_map/ppermute | solution.py:248
  98.4 3.8 %shard_map.77 = bf16[512,384]{1,0:T(8,128)(2,1)} custom-call(bf16[1024,2048]{1,0:T(8,128)(2,1)} %get-tuple-element.12.refs_0_, bf16[512,384]{1,0:T(8,128)(2,1)} %shard_map.74.refs_1_.x, bf16[512,384]{1,0:T(8,128)(2,1)} %copy-done.2, bf16[512,384]{1,0:T(8,128)(2,1)} %copy-done.3, bf16[512,384]{1,0:T(8,128)(2,1)} %copy-done.4), custom_call_target="tpu_custom_call" | custom-call | flops 805306368 | bytes 4063232 | tf_op jit(solution)/shard_map/pallas_call | solution.py:181
  102.2 3.8 %shard_map.76.refs_0_ = bf16[512,384]{1,0:T(8,128)(2,1)} custom-call(bf16[1024,2048]{1,0:T(8,128)(2,1)} %get-tuple-element.12.refs_0_, bf16[512,384]{1,0:T(8,128)(2,1)} %shard_map.74.refs_1_.x, bf16[512,384]{1,0:T(8,128)(2,1)} %copy-done.2, bf16[512,384]{1,0:T(8,128)(2,1)} %copy-done.3, bf16[512,384]{1,0:T(8,128)(2,1)} %copy-done.4), custom_call_target="tpu_custom_call" | custom-call | flops 805306368 | bytes 4063232 | tf_op jit(solution)/shard_map/pallas_call | solution.py:181
  106.0 6.8 %collective-permute-done.9.refs_1_ = bf16[512,384]{1,0:T(8,128)(2,1)S(1)} collective-permute-done((bf16[512,384]{1,0:T(8,128)(2,1)}, bf16[512,384]{1,0:T(8,128)(2,1)S(1)}, u32[]{:S(2)}, u32[]{:S(2)}) %collective-permute-start.9) | collective-permute-done | bytes 393248 | tf_op jit(solution)/shard_map/ppermute | solution.py:248
  113.6 2.3 %shard_map.78.refs_1_ = bf16[512,384]{1,0:T(8,128)(2,1)} custom-call(bf16[128,128]{1,0:T(8,128)(2,1)} %mix.2, bf16[512,384]{1,0:T(8,128)(2,1)} %shard_map.76.refs_0_, bf16[512,384]{1,0:T(8,128)(2,1)} %copy-done.8), custom_call_target="tpu_custom_call" | custom-call | tf_op jit(solution)/shard_map/pallas_call | solution.py:296
  116.2 9.4 %collective-permute-done.10.refs_2_ = bf16[512,384]{1,0:T(8,128)(2,1)S(1)} collective-permute-done((bf16[512,384]{1,0:T(8,128)(2,1)}, bf16[512,384]{1,0:T(8,128)(2,1)S(1)}, u32[]{:S(2)}, u32[]{:S(2)}) %collective-permute-start.10) | collective-permute-done | bytes 393248 | tf_op jit(solution)/shard_map/ppermute | solution.py:248
  126.4 2.8 %shard_map.82 = bf16[512,384]{1,0:T(8,128)(2,1)} custom-call(bf16[2048,1024]{1,0:T(8,128)(2,1)} %get-tuple-element.11.refs_0_, bf16[512,384]{1,0:T(8,128)(2,1)} %shard_map.78.refs_1_, bf16[512,384]{1,0:T(8,128)(2,1)} %copy-done), custom_call_target="tpu_custom_call" | custom-call | flops 402653184 | bytes 2228224 | tf_op jit(solution)/shard_map/pallas_call | solution.py:181
  130.5 2.8 %shard_map.81 = bf16[512,384]{1,0:T(8,128)(2,1)} custom-call(bf16[2048,1024]{1,0:T(8,128)(2,1)} %get-tuple-element.11.refs_0_, bf16[512,384]{1,0:T(8,128)(2,1)} %shard_map.78.refs_1_, bf16[512,384]{1,0:T(8,128)(2,1)} %copy-done), custom_call_target="tpu_custom_call" | custom-call | flops 402653184 | bytes 2228224 | tf_op jit(solution)/shard_map/pallas_call | solution.py:181
  133.4 1.9 %collective-permute-start.12 = (bf16[512,384]{1,0:T(8,128)(2,1)}, bf16[512,384]{1,0:T(8,128)(2,1)S(1)}, u32[]{:S(2)}, u32[]{:S(2)}) collective-permute-start(bf16[512,384]{1,0:T(8,128)(2,1)} %shard_map.81), channel_id=1, source_target_pairs={{0,4},{1,5},{2,6},{3,7},{4,0},{5,1},{6,2},{7,3},{8,12},{9,13},{10,... | collective-permute-start | bytes 1179656 | tf_op jit(solution)/shard_map/ppermute | solution.py:248
  135.3 2.9 %shard_map.80 = bf16[512,384]{1,0:T(8,128)(2,1)} custom-call(bf16[2048,1024]{1,0:T(8,128)(2,1)} %get-tuple-element.11.refs_0_, bf16[512,384]{1,0:T(8,128)(2,1)} %shard_map.78.refs_1_, bf16[512,384]{1,0:T(8,128)(2,1)} %copy-done), custom_call_target="tpu_custom_call" | custom-call | flops 402653184 | bytes 2228224 | tf_op jit(solution)/shard_map/pallas_call | solution.py:181
  138.4 2.9 %shard_map.79.refs_0_ = bf16[512,384]{1,0:T(8,128)(2,1)} custom-call(bf16[2048,1024]{1,0:T(8,128)(2,1)} %get-tuple-element.11.refs_0_, bf16[512,384]{1,0:T(8,128)(2,1)} %shard_map.78.refs_1_, bf16[512,384]{1,0:T(8,128)(2,1)} %copy-done), custom_call_target="tpu_custom_call" | custom-call | flops 402653184 | bytes 2228224 | tf_op jit(solution)/shard_map/pallas_call | solution.py:181
  141.3 6.1 %collective-permute-done.12.refs_2_ = bf16[512,384]{1,0:T(8,128)(2,1)S(1)} collective-permute-done((bf16[512,384]{1,0:T(8,128)(2,1)}, bf16[512,384]{1,0:T(8,128)(2,1)S(1)}, u32[]{:S(2)}, u32[]{:S(2)}) %collective-permute-start.12) | collective-permute-done | bytes 393248 | tf_op jit(solution)/shard_map/ppermute | solution.py:248
  148.8 2.6 %shard_map.83 = (f32[128,384]{1,0:T(8,128)}, bf16[128,384]{1,0:T(8,128)(2,1)}, bf16[128,384]{1,0:T(8,128)(2,1)}, bf16[128,384]{1,0:T(8,128)(2,1)}) custom-call(bf16[128,128]{1,0:T(8,128)(2,1)} %mix.3, bf16[512,384]{1,0:T(8,128)(2,1)} %shard_map.74.refs_1_.x, bf16[512,384]{1,0:T(8,128)(2,1)} %shard_map.79.refs_0_, bf16[512,384]{1,0:T(8,128)(2,1)} %copy-done.11, ...), custom_call_target="tpu_custom_call" | custom-call | tf_op jit(solution)/shard_map/pallas_call | solution.py:307
  152.7 1.5 collective-permute-start.16
  154.2 8.1 %collective-permute-done.15.refs_2_ = bf16[128,384]{1,0:T(8,128)(2,1)S(1)} collective-permute-done((bf16[128,384]{1,0:T(8,128)(2,1)}, bf16[128,384]{1,0:T(8,128)(2,1)S(1)}, u32[]{:S(2)}, u32[]{:S(2)}) %collective-permute-start.15) | collective-permute-done | bytes 98336 | tf_op jit(solution)/shard_map/ppermute | solution.py:248
  164.4 2.0 %shard_map.84 = f32[128,1536]{1,0:T(8,128)} custom-call(s32[7]{0:T(128)} %stack.27.me, f32[128,384]{1,0:T(8,128)} %get-tuple-element.13.refs_0_, bf16[128,384]{1,0:T(8,128)(2,1)} %copy-done.12, bf16[128,384]{1,0:T(8,128)(2,1)} %copy-done.13, bf16[128,384]{1,0:T(8,128)(2,1)} %copy-done.14), custom_call_target="tpu_custom_call" | custom-call | tf_op jit(solution)/shard_map/pallas_call | solution.py:321
  (65 shorter events, 15.7 us)
Async XLA Ops:
  3.9 68.4 %all-to-all-start = ((bf16[32,104,128]{2,1,0:T(8,128)(2,1)}), bf16[32,104,128]{2,1,0:T(8,128)(2,1)S(1)}, u32[]{:S(2)}, u32[]{:S(2)}) async-start(bf16[32,104,128]{2,1,0:T(8,128)(2,1)} %shard_map.73), calls=%async_computation | async-start | bytes 1703936 | tf_op jit(solution)/shard_map/all_to_all | solution.py:257
  11.2 55.7 %collective-permute-start.3 = (bf16[24,128,128]{2,1,0:T(8,128)(2,1)}, bf16[24,128,128]{2,1,0:T(8,128)(2,1)S(1)}, u32[]{:S(2)}, u32[]{:S(2)}) collective-permute-start(bf16[24,128,128]{2,1,0:T(8,128)(2,1)} %v0.1), channel_id=1, source_target_pairs={{0,16},{1,17},{2,18},{3,19},{4,20},{5,21},{6,22},{7,23},{8,24},{9,... | collective-permute-start | bytes 2359304 | tf_op jit(solution)/shard_map/ppermute | solution.py:248
  13.9 65.7 %collective-permute-start.4 = (bf16[24,128,128]{2,1,0:T(8,128)(2,1)}, bf16[24,128,128]{2,1,0:T(8,128)(2,1)S(1)}, u32[]{:S(2)}, u32[]{:S(2)}) collective-permute-start(bf16[24,128,128]{2,1,0:T(8,128)(2,1)} %v0.1), channel_id=1, source_target_pairs={{0,1},{1,0},{2,3},{3,2},{4,5},{5,4},{6,7},{7,6},{8,9},{9,8},{10,11... | collective-permute-start | bytes 2359304 | tf_op jit(solution)/shard_map/ppermute | solution.py:248
  66.9 12.7 %copy-start.5 = (bf16[24,128,128]{2,1,0:T(8,128)(2,1)}, bf16[24,128,128]{2,1,0:T(8,128)(2,1)S(1)}, u32[]{:S(2)}) copy-start(bf16[24,128,128]{2,1,0:T(8,128)(2,1)S(1)} %collective-permute-done.3.v1) | copy-start | bytes 2359300
  66.9 12.7 %collective-permute-start.5 = (bf16[24,128,128]{2,1,0:T(8,128)(2,1)S(1)}, bf16[24,128,128]{2,1,0:T(8,128)(2,1)S(1)}, u32[]{:S(2)}, u32[]{:S(2)}) collective-permute-start(bf16[24,128,128]{2,1,0:T(8,128)(2,1)S(1)} %collective-permute-done.3.v1), channel_id=1, source_target_pairs={{0,1},{1,0},{2,3},{3,2},{4,5},{5,4},{6,7},{7,6},{8,9},{9,8},{10,11... | collective-permute-start | bytes 2359304 | tf_op jit(solution)/shard_map/ppermute | solution.py:248
  67.8 11.9 %copy-start.15 = (s32[48]{0:T(128)}, s32[48]{0:T(128)S(1)}, u32[]{:S(2)}) copy-start(s32[48]{0:T(128)S(1)} %reshape.7.i0) | copy-start | bytes 580
  67.8 4.5 %collective-permute-start = (s32[48]{0:T(128)S(1)}, s32[48]{0:T(128)S(1)}, u32[]{:S(2)}, u32[]{:S(2)}) collective-permute-start(s32[48]{0:T(128)S(1)} %reshape.7.i0), channel_id=1, source_target_pairs={{0,16},{1,17},{2,18},{3,19},{4,20},{5,21},{6,22},{7,23},{8,24},{9,... | collective-permute-start | bytes 584 | tf_op jit(solution)/shard_map/ppermute | solution.py:248
  67.9 9.7 %collective-permute-start.1 = (s32[48]{0:T(128)S(1)}, s32[48]{0:T(128)S(1)}, u32[]{:S(2)}, u32[]{:S(2)}) collective-permute-start(s32[48]{0:T(128)S(1)} %reshape.7.i0), channel_id=1, source_target_pairs={{0,1},{1,0},{2,3},{3,2},{4,5},{5,4},{6,7},{7,6},{8,9},{9,8},{10,11... | collective-permute-start | bytes 584 | tf_op jit(solution)/shard_map/ppermute | solution.py:248
  72.3 7.4 %copy-start.16 = (s32[48]{0:T(128)}, s32[48]{0:T(128)S(1)}, u32[]{:S(2)}) copy-start(s32[48]{0:T(128)S(1)} %collective-permute-done.i1) | copy-start | bytes 580
  72.3 6.8 %collective-permute-start.2 = (s32[48]{0:T(128)S(1)}, s32[48]{0:T(128)S(1)}, u32[]{:S(2)}, u32[]{:S(2)}) collective-permute-start(s32[48]{0:T(128)S(1)} %collective-permute-done.i1), channel_id=1, source_target_pairs={{0,1},{1,0},{2,3},{3,2},{4,5},{5,4},{6,7},{7,6},{8,9},{9,8},{10,11... | collective-permute-start | bytes 584 | tf_op jit(solution)/shard_map/ppermute | solution.py:248
  76.1 18.6 %collective-permute-start.6 = (bf16[512,384]{1,0:T(8,128)(2,1)}, bf16[512,384]{1,0:T(8,128)(2,1)S(1)}, u32[]{:S(2)}, u32[]{:S(2)}) collective-permute-start(bf16[512,384]{1,0:T(8,128)(2,1)} %shard_map.74.refs_1_.x), channel_id=1, source_target_pairs={{0,2},{1,3},{2,0},{3,1},{4,6},{5,7},{6,4},{7,5},{8,10},{9,11},{10,... | collective-permute-start | bytes 1179656 | tf_op jit(solution)/shard_map/ppermute | solution.py:248
  77.6 19.9 %collective-permute-start.7 = (bf16[512,384]{1,0:T(8,128)(2,1)}, bf16[512,384]{1,0:T(8,128)(2,1)S(1)}, u32[]{:S(2)}, u32[]{:S(2)}) collective-permute-start(bf16[512,384]{1,0:T(8,128)(2,1)} %shard_map.74.refs_1_.x), channel_id=1, source_target_pairs={{0,4},{1,5},{2,6},{3,7},{4,0},{5,1},{6,2},{7,3},{8,12},{9,13},{10,... | collective-permute-start | bytes 1179656 | tf_op jit(solution)/shard_map/ppermute | solution.py:248
  79.1 18.4 %collective-permute-start.8 = (bf16[512,384]{1,0:T(8,128)(2,1)}, bf16[512,384]{1,0:T(8,128)(2,1)S(1)}, u32[]{:S(2)}, u32[]{:S(2)}) collective-permute-start(bf16[512,384]{1,0:T(8,128)(2,1)} %shard_map.74.refs_1_.x), channel_id=1, source_target_pairs={{0,6},{1,7},{2,4},{3,5},{4,2},{5,3},{6,0},{7,1},{8,14},{9,15},{10,... | collective-permute-start | bytes 1179656 | tf_op jit(solution)/shard_map/ppermute | solution.py:248
  94.7 2.8 %copy-start.2 = (bf16[512,384]{1,0:T(8,128)(2,1)}, bf16[512,384]{1,0:T(8,128)(2,1)S(1)}, u32[]{:S(2)}) copy-start(bf16[512,384]{1,0:T(8,128)(2,1)S(1)} %collective-permute-done.6.refs_2_) | copy-start | bytes 1179652
  102.2 10.6 %collective-permute-start.9 = (bf16[512,384]{1,0:T(8,128)(2,1)}, bf16[512,384]{1,0:T(8,128)(2,1)S(1)}, u32[]{:S(2)}, u32[]{:S(2)}) collective-permute-start(bf16[512,384]{1,0:T(8,128)(2,1)} %shard_map.77), channel_id=1, source_target_pairs={{0,8},{1,9},{2,10},{3,11},{4,12},{5,13},{6,14},{7,15},{8,0},{9,1},... | collective-permute-start | bytes 1179656 | tf_op jit(solution)/shard_map/ppermute | solution.py:248
  115.9 9.7 %collective-permute-start.10 = (bf16[512,384]{1,0:T(8,128)(2,1)}, bf16[512,384]{1,0:T(8,128)(2,1)S(1)}, u32[]{:S(2)}, u32[]{:S(2)}) collective-permute-start(bf16[512,384]{1,0:T(8,128)(2,1)} %shard_map.78.refs_1_), channel_id=1, source_target_pairs={{0,8},{1,9},{2,10},{3,11},{4,12},{5,13},{6,14},{7,15},{8,0},{9,1},... | collective-permute-start | bytes 1179656 | tf_op jit(solution)/shard_map/ppermute | solution.py:248
  129.2 12.0 %collective-permute-start.13 = (bf16[512,384]{1,0:T(8,128)(2,1)}, bf16[512,384]{1,0:T(8,128)(2,1)S(1)}, u32[]{:S(2)}, u32[]{:S(2)}) collective-permute-start(bf16[512,384]{1,0:T(8,128)(2,1)} %shard_map.82), channel_id=1, source_target_pairs={{0,6},{1,7},{2,4},{3,5},{4,2},{5,3},{6,0},{7,1},{8,14},{9,15},{10,... | collective-permute-start | bytes 1179656 | tf_op jit(solution)/shard_map/ppermute | solution.py:248
  133.4 14.0 %collective-permute-start.12 = (bf16[512,384]{1,0:T(8,128)(2,1)}, bf16[512,384]{1,0:T(8,128)(2,1)S(1)}, u32[]{:S(2)}, u32[]{:S(2)}) collective-permute-start(bf16[512,384]{1,0:T(8,128)(2,1)} %shard_map.81), channel_id=1, source_target_pairs={{0,4},{1,5},{2,6},{3,7},{4,0},{5,1},{6,2},{7,3},{8,12},{9,13},{10,... | collective-permute-start | bytes 1179656 | tf_op jit(solution)/shard_map/ppermute | solution.py:248
  138.1 9.3 %collective-permute-start.11 = (bf16[512,384]{1,0:T(8,128)(2,1)}, bf16[512,384]{1,0:T(8,128)(2,1)S(1)}, u32[]{:S(2)}, u32[]{:S(2)}) collective-permute-start(bf16[512,384]{1,0:T(8,128)(2,1)} %shard_map.80), channel_id=1, source_target_pairs={{0,2},{1,3},{2,0},{3,1},{4,6},{5,7},{6,4},{7,5},{8,10},{9,11},{10,... | collective-permute-start | bytes 1179656 | tf_op jit(solution)/shard_map/ppermute | solution.py:248
  141.3 6.2 %copy-start.9 = (bf16[512,384]{1,0:T(8,128)(2,1)}, bf16[512,384]{1,0:T(8,128)(2,1)S(1)}, u32[]{:S(2)}) copy-start(bf16[512,384]{1,0:T(8,128)(2,1)S(1)} %collective-permute-done.13.refs_3_) | copy-start | bytes 1179652
  151.5 2.8 %collective-permute-start.14 = (bf16[128,384]{1,0:T(8,128)(2,1)}, bf16[128,384]{1,0:T(8,128)(2,1)S(1)}, u32[]{:S(2)}, u32[]{:S(2)}) collective-permute-start(bf16[128,384]{1,0:T(8,128)(2,1)} %get-tuple-element.14), channel_id=1, source_target_pairs={{0,1},{1,0},{2,3},{3,2},{4,5},{5,4},{6,7},{7,6},{8,9},{9,8},{10,11... | collective-permute-start | bytes 294920 | tf_op jit(solution)/shard_map/ppermute | solution.py:248
  151.5 10.9 %collective-permute-start.15 = (bf16[128,384]{1,0:T(8,128)(2,1)}, bf16[128,384]{1,0:T(8,128)(2,1)S(1)}, u32[]{:S(2)}, u32[]{:S(2)}) collective-permute-start(bf16[128,384]{1,0:T(8,128)(2,1)} %get-tuple-element.15), channel_id=1, source_target_pairs={{0,16},{1,17},{2,18},{3,19},{4,20},{5,21},{6,22},{7,23},{8,24},{9,... | collective-permute-start | bytes 294920 | tf_op jit(solution)/shard_map/ppermute | solution.py:248
  152.7 11.0 %collective-permute-start.16 = (bf16[128,384]{1,0:T(8,128)(2,1)}, bf16[128,384]{1,0:T(8,128)(2,1)S(1)}, u32[]{:S(2)}, u32[]{:S(2)}) collective-permute-start(bf16[128,384]{1,0:T(8,128)(2,1)} %get-tuple-element.16), channel_id=1, source_target_pairs={{0,17},{1,16},{2,19},{3,18},{4,21},{5,20},{6,23},{7,22},{8,25},{9,... | collective-permute-start | bytes 294920 | tf_op jit(solution)/shard_map/ppermute | solution.py:248
  154.2 9.5 %copy-start.12 = (bf16[128,384]{1,0:T(8,128)(2,1)}, bf16[128,384]{1,0:T(8,128)(2,1)S(1)}, u32[]{:S(2)}) copy-start(bf16[128,384]{1,0:T(8,128)(2,1)S(1)} %collective-permute-done.14.refs_1_) | copy-start | bytes 294916
  (13 other events, 12.0 us)

commit v2 on v1

v2 whole, which is shorter than its diff:
```python
import functools

import jax
import jax.numpy as jnp
from jax import lax
from jax.experimental import pallas as pl
from jax.experimental.pallas import tpu as pltpu
from jax.sharding import PartitionSpec as P

CH = 128
TILE = 128
PIECE = 128
QUARTERS = 4
VMEM_LIMIT = [16 * 1024 * 1024]

epsilon = 1e-05

BF16 = jnp.bfloat16
F32 = jnp.float32
VM = pl.BlockSpec(memory_space=pltpu.VMEM)
SM = pl.BlockSpec(memory_space=pltpu.SMEM)


def over(x, n):
    assert n & (n - 1) == 0
    return x >> (n.bit_length() - 1)


def rest(x, n):
    assert n & (n - 1) == 0
    return x & (n - 1)


def iota(shape, axis):
    return lax.broadcasted_iota(jnp.int32, shape, axis)


def call(kernel, out_shape, in_specs, behind=(), flops=0):
    count, many = len(in_specs), len(out_shape)

    def body(*refs):
        kernel(*refs[:count], *refs[count + len(behind) : -1])
        refs[-1][...] = jnp.zeros_like(refs[-1])

    run = pl.pallas_call(
        body,
        out_shape=list(out_shape) + [jax.ShapeDtypeStruct((8, CH), F32)],
        in_specs=list(in_specs) + [VM] * len(behind),
        out_specs=[VM] * (many + 1),
        compiler_params=pltpu.CompilerParams(vmem_limit_bytes=VMEM_LIMIT[0]),
        cost_estimate=pl.CostEstimate(flops=flops, bytes_accessed=0, transcendentals=0),
    )

    def apply(*args):
        *outs, token = run(*args, *behind)
        return outs, token

    return apply


def array(rows, columns, dtype=BF16):
    return jax.ShapeDtypeStruct((rows, columns), dtype)


class Layout:
    def __init__(self, rows, cols, slots, width):
        self.R, self.C = rows, cols
        self.R2, self.chips = rows // 2, cols // 2
        self.U = rows * cols
        self.slots = slots
        self.pair = slots // self.U
        self.slab = 4 * self.pair
        self.upl = CH // self.slab
        self.groups = width // CH // QUARTERS
        self.qw = self.groups * CH
        self.blocks = self.R2 * self.chips
        self.own = 4 * PIECE
        self.chip_cols = 2 * rows * TILE
        self.pay = self.groups * self.slab + 8

    def split_z(self, z):
        return rest(z, 2), over(z, 2)

    def join_z(self, h, l):
        return l * 2 + h


def pack_kernel(lay, me, node, feats, out):
    unit, count = me[0], me[1]
    n = lay.slots
    row = node[...]
    slot = iota((1, n), 1)
    live = slot < count
    p = row // PIECE
    h, l = lay.split_z(p // lay.C)
    c = p % lay.C
    block = l * lay.chips + c // 2
    part = h * 2 + c % 2
    p = jnp.where(live, p, -1)
    across = jnp.broadcast_to(p, (n, n))
    down = jnp.transpose(across)
    before = (across == down) & (iota((n, n), 0) < iota((n, n), 1))
    rank = jnp.sum(jnp.where(before, 1, 0), axis=0, keepdims=True)
    target = jnp.where(live, (block * 4 + part) * lay.pair + rank, -1)
    pick = jnp.where(iota((n, n), 0) == target, 1.0, 0.0).astype(BF16)
    sorted_rows = jnp.dot(pick, feats[...], preferred_element_type=F32).astype(BF16)
    place = jnp.where(live, row % PIECE + 1, 0).astype(F32).astype(BF16)
    place = jnp.broadcast_to(place, (16, n))
    lane = iota((lay.blocks * CH, n), 0)
    inner = lane % CH - (unit % lay.upl) * lay.slab
    wanted = (lane // CH) * lay.slab + inner
    wanted = jnp.where((inner >= 0) & (inner < lay.slab), wanted, -2)
    spread = jnp.where(wanted == target, 1.0, 0.0).astype(BF16)
    places = lax.dot_general(
        place, spread, (((1,), (1,)), ((), ())), preferred_element_type=F32
    ).astype(BF16)
    for z in range(lay.R):
        dh, dl = lay.split_z(z)
        for c in range(lay.C):
            b = dl * lay.chips + c // 2
            q = dh * 2 + c % 2
            d = z * lay.C + c
            for g in range(lay.groups):
                lo = q * lay.qw + g * CH
                out[d, g * lay.slab : (g + 1) * lay.slab, :] = sorted_rows[
                    b * lay.slab : (b + 1) * lay.slab, lo : lo + CH
                ]
            out[d, lay.groups * lay.slab : lay.pay, :] = places[0:8, b * CH : (b + 1) * CH]


def land_kernel(lay, first, many, me, got, out):
    mine = me[2]
    lane = iota((1, CH), 1)
    part = (lane % lay.slab) // lay.pair
    base = (part ^ mine) * PIECE - 1
    rows = iota((lay.own, CH), 0)
    picks = []
    for j in range(lay.U // lay.upl):
        total = jnp.zeros((8, CH), F32)
        for i in range(lay.upl):
            total = total + got[j * lay.upl + i, lay.groups * lay.slab : lay.pay, :].astype(F32)
        place = total[0:1, :].astype(jnp.int32)
        spot = jnp.where(place > 0, base + place, -1)
        picks.append(jnp.where(rows == spot, 1.0, 0.0).astype(BF16))
    pick = jnp.concatenate(picks, axis=1)
    for g in range(many):
        lo = (first + g) * lay.slab
        block = got[:, lo : lo + lay.slab, :].reshape(lay.U * lay.slab, CH)
        out[:, g * CH : (g + 1) * CH] = jnp.dot(
            pick, block, preferred_element_type=F32
        ).astype(BF16)


def dense_kernel(lay, me, i0, i1, i2, i3, v0, v1, v2, v3, a0, at0, a1, at1):
    chip, core = me[3], me[4]
    for ref in (a0, at0, a1, at1):
        ref[...] = jnp.zeros_like(ref)
    spare = 2 * lay.chips
    for ids, values, a, at in ((i0, v0, a0, at0), (i1, v1, a1, at1), (i2, v2, a0, at0), (i3, v3, a1, at1)):

        def body(t, carry, ids=ids, values=values, a=a, at=at):
            rt, ct = ids[0, t], ids[1, t]
            c = rest(rt, lay.C)
            r = (over(c, 2) ^ chip) * 2 + (rest(c, 2) ^ core)
            j = rest(over(ct, lay.R), 2) * lay.R + rest(ct, lay.R)
            r = jnp.where(rt < lay.U, r, spare)
            rr = pl.multiple_of(r * TILE, TILE)
            kk = pl.multiple_of(j * TILE, TILE)
            tile = values[t]
            a[pl.ds(rr, TILE), pl.ds(kk, TILE)] = tile
            at[pl.ds(kk, TILE), pl.ds(rr, TILE)] = jnp.transpose(tile)
            return carry

        lax.fori_loop(0, values.shape[0], body, 0, unroll=4)


def seen_kernel(*refs):
    pass


def back_kernel(chips, lo, width, *refs):
    at0, at1, xs, out = refs[0], refs[1], refs[2 : 2 + chips], refs[2 + chips]
    span = slice(lo, lo + width)
    near = jnp.concatenate([x[0 : 2 * PIECE, span] for x in xs], axis=0)
    depth = near.shape[0]
    far = jnp.concatenate([x[2 * PIECE : 4 * PIECE, span] for x in xs], axis=0)
    for lo in range(0, out.shape[0], BLOCK):
        rows = slice(lo, lo + BLOCK)
        total = jnp.dot(at0[rows, 0:depth], near, preferred_element_type=F32)
        total += jnp.dot(at1[rows, 0:depth], far, preferred_element_type=F32)
        out[rows, :] = total.astype(BF16)


def forward_kernel(first, a0, a1, hidden, *outs):
    for i, out in enumerate(outs):
        rows = slice((first + i) * 2 * PIECE, (first + i + 1) * 2 * PIECE)
        for lo, a in ((0, a0), (2 * PIECE, a1)):
            total = jnp.dot(a[rows, :], hidden[...], preferred_element_type=F32)
            out[lo : lo + 2 * PIECE, :] = total.astype(BF16)


def unit_groups(total):
    power = jnp.mean(total * total, axis=-1, keepdims=True)
    return (total * lax.rsqrt(power + epsilon)).astype(BF16)


def encode_kernel(mix, *refs):
    parts, out = refs[:-1], refs[-1]
    for g in range(out.shape[1] // CH):
        span = slice(g * CH, (g + 1) * CH)
        total = parts[0][:, span].astype(F32)
        for ref in parts[1:]:
            total = total + ref[:, span].astype(F32)
        v = jnp.dot(unit_groups(total), mix[...], preferred_element_type=F32)
        out[:, span] = (0.5 * v * (1.0 + lax.erf(v * (0.5**0.5)))).astype(BF16)


def decode_kernel(parts, takes, lo, done, mix, *refs):
    xs, totals = refs[:takes], refs[takes : takes + parts]
    early, outs = refs[takes + parts : -4], refs[-4:]
    for out, ref in zip(outs, early):
        out[:, 0:done] = ref[...]
    x_at = [(x, at) for x in xs for at in range(0, x.shape[1], CH)][lo // CH :]
    for g in range(totals[0].shape[1] // CH):
        span = slice(g * CH, (g + 1) * CH)
        total = totals[0][:, span].astype(F32)
        for ref in totals[1:]:
            total = total + ref[:, span].astype(F32)
        recon = jnp.dot(unit_groups(total), mix[...], preferred_element_type=F32)
        x, at = x_at[g]
        left = x[:, at : at + CH].astype(F32) - recon
        for i, out in enumerate(outs):
            to = slice(done + g * CH, done + (g + 1) * CH)
            out[:, to] = left[i * PIECE : (i + 1) * PIECE, :].astype(out.dtype)


def join_kernel(lay, me, *refs):
    out = refs[-1]
    for rel in range(4):
        at = pl.multiple_of((me[2] ^ rel) * lay.qw, CH)
        out[:, pl.ds(at, lay.qw)] = refs[rel][...].astype(F32)


GATHER = ((0, 1), (1, 2))
SUMS = ((0, 1), (1, 1), (2, 1))
BLOCK = 256
SEEN_FLOPS = 3_000_000_000
FIRST_FLOPS = 5_000_000_000
DECODE_FLOPS = 3_000_000_000


def inside(parts, first, many):
    for n, (f, m) in enumerate(parts):
        if f <= first and first + many <= f + m:
            return n, (first - f) * CH
    raise ValueError("not nested")


def local(lay, ingest_features, node_map, unit_rows, tile_ids, tile_values, mix_in, mix_out):
    z, c = lax.axis_index("row"), lax.axis_index("col")
    me = jnp.stack(
        [z * lay.C + c, unit_rows[0], rest(z, 2) * 2 + rest(c, 2), over(c, 2), rest(c, 2)]
    ).astype(jnp.int32)

    def exchange(x, dh=0, dl=0, chip=0, core=0):
        pairs = []
        for zz in range(lay.R):
            hh, ll = lay.split_z(zz)
            for cc in range(lay.C):
                to = lay.join_z(hh ^ dh, ll ^ dl) * lay.C + (cc ^ (chip * 2 + core))
                pairs.append((zz * lay.C + cc, to))
        return lax.ppermute(x, ("row", "col"), pairs)

    ids0 = tile_ids.T
    ids1, val1 = exchange(ids0, dh=1), exchange(tile_values, dh=1)
    ids2, val2 = exchange(ids0, core=1), exchange(tile_values, core=1)
    ids3 = exchange(ids1, core=1)

    (outgoing,), _ = call(
        functools.partial(pack_kernel, lay),
        [jax.ShapeDtypeStruct((lay.U, lay.pay, CH), BF16)],
        [SM, VM, VM],
    )(me, node_map.reshape(1, lay.slots), ingest_features)
    got = lax.all_to_all(outgoing, ("row", "col"), split_axis=0, concat_axis=0, tiled=True)

    val3 = exchange(val1, core=1)
    ids, values = (ids0, ids1, ids2, ids3), (tile_values, val1, val2, val3)
    _, token = call(seen_kernel, [], [SM] * 3 + [VM], flops=SEEN_FLOPS)(ids1, ids2, ids3, val3)

    def land(first, many, token):
        (x,), token = call(
            functools.partial(land_kernel, lay, first, many),
            [array(lay.own, many * CH)],
            [SM, VM],
            behind=[token],
        )(me, got)
        return [x] + [exchange(x, chip=s) for s in range(1, lay.chips)], token

    xs, token = land(*GATHER[0], token)
    gathered = [xs]
    depth = 2 * lay.chips * PIECE + TILE
    (a0, at0, a1, at1), token = call(
        functools.partial(dense_kernel, lay),
        [array(depth, lay.chip_cols), array(lay.chip_cols, depth)] * 2,
        [SM] * 5 + [VM] * 4,
        behind=[token],
    )(me, *ids, *values)
    for first, many in GATHER[1:]:
        xs, token = land(first, many, token)
        gathered.append(xs)
    own = [xs[0] for xs in gathered]

    def back(n, token):
        first, many = SUMS[n]
        where, lo = inside(GATHER, first, many)
        (mine,), token = call(
            functools.partial(back_kernel, lay.chips, lo, many * CH),
            [array(lay.chip_cols, many * CH)],
            [VM] * (2 + lay.chips),
            behind=[token],
            flops=0 if n else FIRST_FLOPS,
        )(at0, at1, *gathered[where])
        return [mine] + [exchange(mine, dl=s) for s in range(1, lay.R2)], token

    def forward(sums, token):
        shape = sums[0].shape
        (hidden,), token = call(
            encode_kernel, [array(*shape)], [VM] * (1 + lay.R2), behind=[token]
        )(mix_in, *sums)
        sent, token = call(
            functools.partial(forward_kernel, 1),
            [array(lay.own, shape[1])] * (lay.chips - 1),
            [VM] * 3,
            behind=[token],
        )(a0, a1, hidden)
        kept, token = call(
            functools.partial(forward_kernel, 0),
            [array(lay.own, shape[1])],
            [VM] * 3,
            behind=[token],
        )(a0, a1, hidden)
        return kept + [exchange(f, chip=s + 1) for s, f in enumerate(sent)], token

    def decode(n, parts, left, token, flops=0):
        first, many = SUMS[n]
        done = first * CH
        return call(
            functools.partial(decode_kernel, lay.chips, len(own), done, done),
            [array(PIECE, done + many * CH, F32 if i == 0 else BF16) for i in range(4)],
            [VM] * (1 + len(own) + lay.chips + len(left)),
            behind=[token],
            flops=flops,
        )(mix_out, *own, *parts, *left)

    left, parts = [], []
    sums, token = back(0, token)
    for n in range(len(SUMS)):
        if n == 0:
            later, token = back(1, token)
        part, token = forward(sums, token)
        parts.append(part)
        if n > 0:
            left, token = decode(n - 1, parts[n - 1], left, token, DECODE_FLOPS)
        if n + 2 < len(SUMS):
            sums = later
            later, token = back(n + 2, token)
        else:
            sums = later
    left, token = decode(len(SUMS) - 1, parts[-1], left, token)
    pieces = [
        left[0],
        exchange(left[1], core=1),
        exchange(left[2], dh=1),
        exchange(left[3], dh=1, core=1),
    ]
    (out,), _ = call(
        functools.partial(join_kernel, lay),
        [array(PIECE, QUARTERS * lay.qw, F32)],
        [SM] + [VM] * 4,
    )(me, *pieces)
    return out


def solution(mesh):
    rows, cols = mesh.shape["row"], mesh.shape["col"]

    def run(ingest_features, node_map, *rest):
        VMEM_LIMIT[0] = (16 if rows * cols <= 32 else 56) * 1024 * 1024
        lay = Layout(
            rows, cols, node_map.shape[0] // (rows * cols), ingest_features.shape[1]
        )
        return jax.shard_map(
            functools.partial(local, lay),
            mesh=mesh,
            in_specs=(
                P(("row", "col"), None),
                P(("row", "col")),
                P(("row", "col")),
                P(("row", "col"), None),
                P(("row", "col"), None, None),
                P(),
                P(),
            ),
            out_specs=P(("row", "col"), None),
            check_vma=False,
        )(ingest_features, node_map, *rest)

    return run
```

time: 167 us -> 111 us (0.66)
  waiting for transfers between devices: 91.6 us -> 53.4 us
  Pallas kernels: 44.9 us -> 21.1 us
  starting transfers between devices: 20.7 us -> 33.9 us
  local copies, waits for them, and re-layouts: 8.5 us -> 1.91 us
    ppermute x17 -> x27, waiting for transfers between devices: 91.6 us -> 52.8 us  [exchange(): return lax.ppermute(x, ('row', 'col'), pairs)]
    pallas_call x12 -> x21, Pallas kernels: 44.9 us -> 21.1 us  [apply(): *outs, token = run(*args, *behind)]
    ppermute x17 -> x27, starting transfers between devices: 13.4 us -> 29 us  [exchange(): return lax.ppermute(x, ('row', 'col'), pairs)]
    unnamed x39 -> x12, local copies, waits for them, and re-layouts: 7.84 us -> 1.83 us
    all_to_all x1, starting transfers between devices: 7.3 us -> 4.82 us  [local(): lax.all_to_all(outgoing, ('row', 'col'), split_axis=0, concat_axis=0, til...]
  transfers between devices with their start and end apart: 18 -> 28, of which waited for: 9 -> 12; matrix products, arithmetic and copies ran while one was open for 1% -> 0% of each run, Pallas kernels for 17% -> 17%
where the time goes in v2:
time: 111 us
  waiting for transfers between devices  53.4 us (48%)
  starting transfers between devices  33.9 us (31%)
  Pallas kernels  21.1 us (19%)
  local copies, waits for them, and re-layouts  1.91 us (2%)
    ppermute x27, waiting for transfers between devices, exchange(): return lax.ppermute(x, ('row', 'col'), pairs)  52.8 us
    ppermute x27, starting transfers between devices, exchange(): return lax.ppermute(x, ('row', 'col'), pairs)  29 us
    pallas_call x21, Pallas kernels, apply(): *outs, token = run(*args, *behind)  21.1 us
    all_to_all x1, starting transfers between devices, local(): lax.all_to_all(outgoing, ('row', 'col'), split_axis=0, concat_axis=0, til...  4.82 us
  transfers between devices with their start and end apart: 28, of which 12 were waited for; matrix products, arithmetic and copies ran while one was open for 0% of the time, Pallas kernels for 17%

profile of v2, /device:TPU:0, one launch (start us, length us, event | category | flops | bytes accessed | tf_op | source)
XLA Modules:
  0.0 111.1 jit_solution(15187620909965812350)
XLA Ops:
  0.0 3.0 %collective-permute-start.3 = (bf16[24,128,128]{2,1,0:T(8,128)(2,1)}, bf16[24,128,128]{2,1,0:T(8,128)(2,1)S(1)}, u32[]{:S(2)}, u32[]{:S(2)}) collective-permute-start(bf16[24,128,128]{2,1,0:T(8,128)(2,1)} %refs_5_.1), channel_id=1, source_target_pairs={{0,8},{1,9},{2,10},{3,11},{4,12},{5,13},{6,14},{7,15},{8,0},{9,1},... | collective-permute-start | bytes 2359304 | tf_op jit(solution)/shard_map/ppermute | solution.py:272
  5.6 2.1 %shard_map.73 = (bf16[32,104,128]{2,1,0:T(8,128)(2,1)}, f32[8,128]{1,0:T(8,128)}) custom-call(s32[5]{0:T(128)S(1)} %stack.19.refs_0_, s32[1,256]{1,0:T(1,128)S(1)} %bitcast.6, bf16[256,1536]{1,0:T(8,128)(2,1)S(1)} %copy-done), custom_call_target="tpu_custom_call" | custom-call | tf_op jit(solution)/shard_map/pallas_call | solution.py:55
  7.7 4.8 %all-to-all-start = ((bf16[32,104,128]{2,1,0:T(8,128)(2,1)}), bf16[32,104,128]{2,1,0:T(8,128)(2,1)S(1)}, u32[]{:S(2)}, u32[]{:S(2)}) async-start(bf16[32,104,128]{2,1,0:T(8,128)(2,1)} %get-tuple-element.60), calls=%async_computation | async-start | bytes 1703936 | tf_op jit(solution)/shard_map/all_to_all | solution.py:284
  12.5 14.1 %collective-permute-done.3.refs_6_ = bf16[24,128,128]{2,1,0:T(8,128)(2,1)S(1)} collective-permute-done((bf16[24,128,128]{2,1,0:T(8,128)(2,1)}, bf16[24,128,128]{2,1,0:T(8,128)(2,1)S(1)}, u32[]{:S(2)}, u32[]{:S(2)}) %collective-permute-start.3) | collective-permute-done | bytes 786464 | tf_op jit(solution)/shard_map/ppermute | solution.py:272
  27.2 6.5 %collective-permute-done.refs_0_.refs_2_ = s32[2,24]{1,0:T(2,128)S(1)} collective-permute-done((s32[2,24]{1,0:T(2,128)S(1)}, s32[2,24]{1,0:T(2,128)S(1)}, u32[]{:S(2)}, u32[]{:S(2)}) %collective-permute-start) | collective-permute-done | bytes 224 | tf_op jit(solution)/shard_map/ppermute | solution.py:272
  37.1 1.6 %collective-permute-start.9 = (bf16[512,128]{1,0:T(8,128)(2,1)S(1)}, bf16[512,128]{1,0:T(8,128)(2,1)S(1)}, u32[]{:S(2)}, u32[]{:S(2)}) collective-permute-start(bf16[512,128]{1,0:T(8,128)(2,1)S(1)} %get-tuple-element.61.refs_2_.refs_1_), channel_id=1, source_target_pairs={{0,2},{1,3},{2,0},{3,1},{4,6},{5,7},{6,4},{7,5},{8,10},{9,11},{10,... | collective-permute-start | bytes 393224 | tf_op jit(solution)/shard_map/ppermute | solution.py:272
  40.6 4.3 %shard_map.76 = (bf16[1152,1024]{1,0:T(8,128)(2,1)S(1)}, bf16[1024,1152]{1,0:T(8,128)(2,1)S(1)}, bf16[1152,1024]{1,0:T(8,128)(2,1)S(1)}, bf16[1024,1152]{1,0:T(8,128)(2,1)S(1)}, f32[8,128]{1,0:T(8,128)S(1)}) custom-call(s32[5]{0:T(128)S(1)} %stack.19.refs_0_, s32[2,24]{1,0:T(2,128)S(1)} %bitcast.9, s32[2,24]{1,0:T(2,128)S(1)} %collective-permute-done.refs_0_.refs_2_, ...), custom_call_target="tpu_custom_call" | custom-call | tf_op jit(solution)/shard_map/pallas_call | solution.py:55
  46.2 1.6 %collective-permute-start.6 = (bf16[512,256]{1,0:T(8,128)(2,1)S(1)}, bf16[512,256]{1,0:T(8,128)(2,1)S(1)}, u32[]{:S(2)}, u32[]{:S(2)}) collective-permute-start(bf16[512,256]{1,0:T(8,128)(2,1)S(1)} %get-tuple-element.64.refs_2_), channel_id=1, source_target_pairs={{0,2},{1,3},{2,0},{3,1},{4,6},{5,7},{6,4},{7,5},{8,10},{9,11},{10,... | collective-permute-start | bytes 786440 | tf_op jit(solution)/shard_map/ppermute | solution.py:272
  51.0 3.0 %collective-permute-start.12 = (bf16[1024,128]{1,0:T(8,128)(2,1)S(1)}, bf16[1024,128]{1,0:T(8,128)(2,1)S(1)}, u32[]{:S(2)}, u32[]{:S(2)}) collective-permute-start(bf16[1024,128]{1,0:T(8,128)(2,1)S(1)} %get-tuple-element.70.refs_1_), channel_id=1, source_target_pairs={{0,16},{1,17},{2,18},{3,19},{4,20},{5,21},{6,22},{7,23},{8,24},{9,... | collective-permute-start | bytes 786440 | tf_op jit(solution)/shard_map/ppermute | solution.py:272
  55.3 6.1 %collective-permute-done.7.refs_4_ = bf16[512,256]{1,0:T(8,128)(2,1)S(1)} collective-permute-done((bf16[512,256]{1,0:T(8,128)(2,1)S(1)}, bf16[512,256]{1,0:T(8,128)(2,1)S(1)}, u32[]{:S(2)}, u32[]{:S(2)}) %collective-permute-start.7) | collective-permute-done | bytes 262176 | tf_op jit(solution)/shard_map/ppermute | solution.py:272
  62.6 2.3 %collective-permute-start.17 = (bf16[1024,128]{1,0:T(8,128)(2,1)S(1)}, bf16[1024,128]{1,0:T(8,128)(2,1)S(1)}, u32[]{:S(2)}, u32[]{:S(2)}) collective-permute-start(bf16[1024,128]{1,0:T(8,128)(2,1)S(1)} %get-tuple-element.82.refs_1_), channel_id=1, source_target_pairs={{0,16},{1,17},{2,18},{3,19},{4,20},{5,21},{6,22},{7,23},{8,24},{9,... | collective-permute-start | bytes 786440 | tf_op jit(solution)/shard_map/ppermute | solution.py:272
  64.9 6.4 %collective-permute-done.12.refs_2_ = bf16[1024,128]{1,0:T(8,128)(2,1)S(1)} collective-permute-done((bf16[1024,128]{1,0:T(8,128)(2,1)S(1)}, bf16[1024,128]{1,0:T(8,128)(2,1)S(1)}, u32[]{:S(2)}, u32[]{:S(2)}) %collective-permute-start.12) | collective-permute-done | bytes 262176 | tf_op jit(solution)/shard_map/ppermute | solution.py:272
  72.8 2.2 %collective-permute-start.15 = (bf16[512,128]{1,0:T(8,128)(2,1)S(1)}, bf16[512,128]{1,0:T(8,128)(2,1)S(1)}, u32[]{:S(2)}, u32[]{:S(2)}) collective-permute-start(bf16[512,128]{1,0:T(8,128)(2,1)S(1)} %get-tuple-element.80), channel_id=1, source_target_pairs={{0,4},{1,5},{2,6},{3,7},{4,0},{5,1},{6,2},{7,3},{8,12},{9,13},{10,... | collective-permute-start | bytes 393224 | tf_op jit(solution)/shard_map/ppermute | solution.py:272
  75.0 1.3 %collective-permute-start.16 = (bf16[512,128]{1,0:T(8,128)(2,1)S(1)}, bf16[512,128]{1,0:T(8,128)(2,1)S(1)}, u32[]{:S(2)}, u32[]{:S(2)}) collective-permute-start(bf16[512,128]{1,0:T(8,128)(2,1)S(1)} %get-tuple-element.81), channel_id=1, source_target_pairs={{0,6},{1,7},{2,4},{3,5},{4,2},{5,3},{6,0},{7,1},{8,14},{9,15},{10,... | collective-permute-start | bytes 393224 | tf_op jit(solution)/shard_map/ppermute | solution.py:272
  80.1 2.0 %collective-permute-start.22 = (bf16[512,128]{1,0:T(8,128)(2,1)S(1)}, bf16[512,128]{1,0:T(8,128)(2,1)S(1)}, u32[]{:S(2)}, u32[]{:S(2)}) collective-permute-start(bf16[512,128]{1,0:T(8,128)(2,1)S(1)} %get-tuple-element.98), channel_id=1, source_target_pairs={{0,4},{1,5},{2,6},{3,7},{4,0},{5,1},{6,2},{7,3},{8,12},{9,13},{10,... | collective-permute-start | bytes 393224 | tf_op jit(solution)/shard_map/ppermute | solution.py:272
  82.2 1.6 %collective-permute-start.23 = (bf16[512,128]{1,0:T(8,128)(2,1)S(1)}, bf16[512,128]{1,0:T(8,128)(2,1)S(1)}, u32[]{:S(2)}, u32[]{:S(2)}) collective-permute-start(bf16[512,128]{1,0:T(8,128)(2,1)S(1)} %get-tuple-element.99), channel_id=1, source_target_pairs={{0,6},{1,7},{2,4},{3,5},{4,2},{5,3},{6,0},{7,1},{8,14},{9,15},{10,... | collective-permute-start | bytes 393224 | tf_op jit(solution)/shard_map/ppermute | solution.py:272
  84.1 7.6 %collective-permute-done.13.refs_2_ = bf16[1024,128]{1,0:T(8,128)(2,1)S(1)} collective-permute-done((bf16[1024,128]{1,0:T(8,128)(2,1)S(1)}, bf16[1024,128]{1,0:T(8,128)(2,1)S(1)}, u32[]{:S(2)}, u32[]{:S(2)}) %collective-permute-start.13) | collective-permute-done | bytes 262176 | tf_op jit(solution)/shard_map/ppermute | solution.py:272
  94.6 2.5 %collective-permute-start.20 = (bf16[512,128]{1,0:T(8,128)(2,1)S(1)}, bf16[512,128]{1,0:T(8,128)(2,1)S(1)}, u32[]{:S(2)}, u32[]{:S(2)}) collective-permute-start(bf16[512,128]{1,0:T(8,128)(2,1)S(1)} %get-tuple-element.95), channel_id=1, source_target_pairs={{0,6},{1,7},{2,4},{3,5},{4,2},{5,3},{6,0},{7,1},{8,14},{9,15},{10,... | collective-permute-start | bytes 393224 | tf_op jit(solution)/shard_map/ppermute | solution.py:272
  97.4 2.6 %collective-permute-done.18.refs_4_ = bf16[512,128]{1,0:T(8,128)(2,1)S(1)} collective-permute-done((bf16[512,128]{1,0:T(8,128)(2,1)S(1)}, bf16[512,128]{1,0:T(8,128)(2,1)S(1)}, u32[]{:S(2)}, u32[]{:S(2)}) %collective-permute-start.18) | collective-permute-done | bytes 131104 | tf_op jit(solution)/shard_map/ppermute | solution.py:272
  99.9 1.9 %collective-permute-done.19.refs_5_ = bf16[512,128]{1,0:T(8,128)(2,1)S(1)} collective-permute-done((bf16[512,128]{1,0:T(8,128)(2,1)S(1)}, bf16[512,128]{1,0:T(8,128)(2,1)S(1)}, u32[]{:S(2)}, u32[]{:S(2)}) %collective-permute-start.19) | collective-permute-done | bytes 131104 | tf_op jit(solution)/shard_map/ppermute | solution.py:272
  102.7 1.9 %collective-permute-start.26 = (bf16[128,384]{1,0:T(8,128)(2,1)S(1)}, bf16[128,384]{1,0:T(8,128)(2,1)S(1)}, u32[]{:S(2)}, u32[]{:S(2)}) collective-permute-start(bf16[128,384]{1,0:T(8,128)(2,1)S(1)} %get-tuple-element.113), channel_id=1, source_target_pairs={{0,9},{1,8},{2,11},{3,10},{4,13},{5,12},{6,15},{7,14},{8,1},{9,0},... | collective-permute-start | bytes 294920 | tf_op jit(solution)/shard_map/ppermute | solution.py:272
  104.5 3.7 %collective-permute-done.25.refs_3_ = bf16[128,384]{1,0:T(8,128)(2,1)S(1)} collective-permute-done((bf16[128,384]{1,0:T(8,128)(2,1)S(1)}, bf16[128,384]{1,0:T(8,128)(2,1)S(1)}, u32[]{:S(2)}, u32[]{:S(2)}) %collective-permute-start.25) | collective-permute-done | bytes 98336 | tf_op jit(solution)/shard_map/ppermute | solution.py:272
  108.3 1.3 %collective-permute-done.26.refs_4_ = bf16[128,384]{1,0:T(8,128)(2,1)S(1)} collective-permute-done((bf16[128,384]{1,0:T(8,128)(2,1)S(1)}, bf16[128,384]{1,0:T(8,128)(2,1)S(1)}, u32[]{:S(2)}, u32[]{:S(2)}) %collective-permute-start.26) | collective-permute-done | bytes 98336 | tf_op jit(solution)/shard_map/ppermute | solution.py:272
  109.6 1.5 %shard_map.93 = (f32[128,1536]{1,0:T(8,128)}, f32[8,128]{1,0:T(8,128)}) custom-call(s32[5]{0:T(128)S(1)} %stack.19.refs_0_, f32[128,384]{1,0:T(8,128)S(1)} %get-tuple-element.110.refs_1_, bf16[128,384]{1,0:T(8,128)(2,1)S(1)} %collective-permute-done.24.refs_2_, bf16[128,384]{1,0:T(8,128)(2,1)S(1)} %collective-permute-done.25.refs_3_, ...), custom_call_target="tpu_custom_call" | custom-call | tf_op jit(solution)/shard_map/pallas_call | solution.py:55
  (66 shorter events, 24.3 us)
Async XLA Ops:
  0.0 26.6 %collective-permute-start.3 = (bf16[24,128,128]{2,1,0:T(8,128)(2,1)}, bf16[24,128,128]{2,1,0:T(8,128)(2,1)S(1)}, u32[]{:S(2)}, u32[]{:S(2)}) collective-permute-start(bf16[24,128,128]{2,1,0:T(8,128)(2,1)} %refs_5_.1), channel_id=1, source_target_pairs={{0,8},{1,9},{2,10},{3,11},{4,12},{5,13},{6,14},{7,15},{8,0},{9,1},... | collective-permute-start | bytes 2359304 | tf_op jit(solution)/shard_map/ppermute | solution.py:272
  7.7 28.4 %all-to-all-start = ((bf16[32,104,128]{2,1,0:T(8,128)(2,1)}), bf16[32,104,128]{2,1,0:T(8,128)(2,1)S(1)}, u32[]{:S(2)}, u32[]{:S(2)}) async-start(bf16[32,104,128]{2,1,0:T(8,128)(2,1)} %get-tuple-element.60), calls=%async_computation | async-start | bytes 1703936 | tf_op jit(solution)/shard_map/all_to_all | solution.py:284
  26.6 8.4 %collective-permute-start.4 = (bf16[24,128,128]{2,1,0:T(8,128)(2,1)S(1)}, bf16[24,128,128]{2,1,0:T(8,128)(2,1)S(1)}, u32[]{:S(2)}, u32[]{:S(2)}) collective-permute-start(bf16[24,128,128]{2,1,0:T(8,128)(2,1)S(1)} %collective-permute-done.3.refs_6_), channel_id=1, source_target_pairs={{0,1},{1,0},{2,3},{3,2},{4,5},{5,4},{6,7},{7,6},{8,9},{9,8},{10,11... | collective-permute-start | bytes 2359304 | tf_op jit(solution)/shard_map/ppermute | solution.py:272
  26.6 14.1 %collective-permute-start.5 = (bf16[24,128,128]{2,1,0:T(8,128)(2,1)S(1)}, bf16[24,128,128]{2,1,0:T(8,128)(2,1)}, u32[]{:S(2)}, u32[]{:S(2)}) collective-permute-start(bf16[24,128,128]{2,1,0:T(8,128)(2,1)S(1)} %copy-done.1), channel_id=1, source_target_pairs={{0,1},{1,0},{2,3},{3,2},{4,5},{5,4},{6,7},{7,6},{8,9},{9,8},{10,11... | collective-permute-start | bytes 2359304 | tf_op jit(solution)/shard_map/ppermute | solution.py:272
  27.1 6.7 %collective-permute-start = (s32[2,24]{1,0:T(2,128)S(1)}, s32[2,24]{1,0:T(2,128)S(1)}, u32[]{:S(2)}, u32[]{:S(2)}) collective-permute-start(s32[2,24]{1,0:T(2,128)S(1)} %bitcast.7), channel_id=1, source_target_pairs={{0,8},{1,9},{2,10},{3,11},{4,12},{5,13},{6,14},{7,15},{8,0},{9,1},... | collective-permute-start | bytes 584 | tf_op jit(solution)/shard_map/ppermute | solution.py:272
  27.1 6.7 %collective-permute-start.1 = (s32[2,24]{1,0:T(2,128)S(1)}, s32[2,24]{1,0:T(2,128)S(1)}, u32[]{:S(2)}, u32[]{:S(2)}) collective-permute-start(s32[2,24]{1,0:T(2,128)S(1)} %bitcast.8), channel_id=1, source_target_pairs={{0,1},{1,0},{2,3},{3,2},{4,5},{5,4},{6,7},{7,6},{8,9},{9,8},{10,11... | collective-permute-start | bytes 584 | tf_op jit(solution)/shard_map/ppermute | solution.py:272
  37.1 12.0 %collective-permute-start.9 = (bf16[512,128]{1,0:T(8,128)(2,1)S(1)}, bf16[512,128]{1,0:T(8,128)(2,1)S(1)}, u32[]{:S(2)}, u32[]{:S(2)}) collective-permute-start(bf16[512,128]{1,0:T(8,128)(2,1)S(1)} %get-tuple-element.61.refs_2_.refs_1_), channel_id=1, source_target_pairs={{0,2},{1,3},{2,0},{3,1},{4,6},{5,7},{6,4},{7,5},{8,10},{9,11},{10,... | collective-permute-start | bytes 393224 | tf_op jit(solution)/shard_map/ppermute | solution.py:272
  38.6 11.1 %collective-permute-start.10 = (bf16[512,128]{1,0:T(8,128)(2,1)S(1)}, bf16[512,128]{1,0:T(8,128)(2,1)S(1)}, u32[]{:S(2)}, u32[]{:S(2)}) collective-permute-start(bf16[512,128]{1,0:T(8,128)(2,1)S(1)} %get-tuple-element.61.refs_2_.refs_1_), channel_id=1, source_target_pairs={{0,4},{1,5},{2,6},{3,7},{4,0},{5,1},{6,2},{7,3},{8,12},{9,13},{10,... | collective-permute-start | bytes 393224 | tf_op jit(solution)/shard_map/ppermute | solution.py:272
  39.9 9.9 %collective-permute-start.11 = (bf16[512,128]{1,0:T(8,128)(2,1)S(1)}, bf16[512,128]{1,0:T(8,128)(2,1)S(1)}, u32[]{:S(2)}, u32[]{:S(2)}) collective-permute-start(bf16[512,128]{1,0:T(8,128)(2,1)S(1)} %get-tuple-element.61.refs_2_.refs_1_), channel_id=1, source_target_pairs={{0,6},{1,7},{2,4},{3,5},{4,2},{5,3},{6,0},{7,1},{8,14},{9,15},{10,... | collective-permute-start | bytes 393224 | tf_op jit(solution)/shard_map/ppermute | solution.py:272
  46.2 9.1 %collective-permute-start.6 = (bf16[512,256]{1,0:T(8,128)(2,1)S(1)}, bf16[512,256]{1,0:T(8,128)(2,1)S(1)}, u32[]{:S(2)}, u32[]{:S(2)}) collective-permute-start(bf16[512,256]{1,0:T(8,128)(2,1)S(1)} %get-tuple-element.64.refs_2_), channel_id=1, source_target_pairs={{0,2},{1,3},{2,0},{3,1},{4,6},{5,7},{6,4},{7,5},{8,10},{9,11},{10,... | collective-permute-start | bytes 786440 | tf_op jit(solution)/shard_map/ppermute | solution.py:272
  47.8 13.6 %collective-permute-start.7 = (bf16[512,256]{1,0:T(8,128)(2,1)S(1)}, bf16[512,256]{1,0:T(8,128)(2,1)S(1)}, u32[]{:S(2)}, u32[]{:S(2)}) collective-permute-start(bf16[512,256]{1,0:T(8,128)(2,1)S(1)} %get-tuple-element.64.refs_2_), channel_id=1, source_target_pairs={{0,4},{1,5},{2,6},{3,7},{4,0},{5,1},{6,2},{7,3},{8,12},{9,13},{10,... | collective-permute-start | bytes 786440 | tf_op jit(solution)/shard_map/ppermute | solution.py:272
  49.0 12.3 %collective-permute-start.8 = (bf16[512,256]{1,0:T(8,128)(2,1)S(1)}, bf16[512,256]{1,0:T(8,128)(2,1)S(1)}, u32[]{:S(2)}, u32[]{:S(2)}) collective-permute-start(bf16[512,256]{1,0:T(8,128)(2,1)S(1)} %get-tuple-element.64.refs_2_), channel_id=1, source_target_pairs={{0,6},{1,7},{2,4},{3,5},{4,2},{5,3},{6,0},{7,1},{8,14},{9,15},{10,... | collective-permute-start | bytes 786440 | tf_op jit(solution)/shard_map/ppermute | solution.py:272
  51.0 20.3 %collective-permute-start.12 = (bf16[1024,128]{1,0:T(8,128)(2,1)S(1)}, bf16[1024,128]{1,0:T(8,128)(2,1)S(1)}, u32[]{:S(2)}, u32[]{:S(2)}) collective-permute-start(bf16[1024,128]{1,0:T(8,128)(2,1)S(1)} %get-tuple-element.70.refs_1_), channel_id=1, source_target_pairs={{0,16},{1,17},{2,18},{3,19},{4,20},{5,21},{6,22},{7,23},{8,24},{9,... | collective-permute-start | bytes 786440 | tf_op jit(solution)/shard_map/ppermute | solution.py:272
  62.6 15.5 %collective-permute-start.17 = (bf16[1024,128]{1,0:T(8,128)(2,1)S(1)}, bf16[1024,128]{1,0:T(8,128)(2,1)S(1)}, u32[]{:S(2)}, u32[]{:S(2)}) collective-permute-start(bf16[1024,128]{1,0:T(8,128)(2,1)S(1)} %get-tuple-element.82.refs_1_), channel_id=1, source_target_pairs={{0,16},{1,17},{2,18},{3,19},{4,20},{5,21},{6,22},{7,23},{8,24},{9,... | collective-permute-start | bytes 786440 | tf_op jit(solution)/shard_map/ppermute | solution.py:272
  72.7 7.4 %collective-permute-start.14 = (bf16[512,128]{1,0:T(8,128)(2,1)S(1)}, bf16[512,128]{1,0:T(8,128)(2,1)S(1)}, u32[]{:S(2)}, u32[]{:S(2)}) collective-permute-start(bf16[512,128]{1,0:T(8,128)(2,1)S(1)} %get-tuple-element.79), channel_id=1, source_target_pairs={{0,2},{1,3},{2,0},{3,1},{4,6},{5,7},{6,4},{7,5},{8,10},{9,11},{10,... | collective-permute-start | bytes 393224 | tf_op jit(solution)/shard_map/ppermute | solution.py:272
  72.8 9.3 %collective-permute-start.15 = (bf16[512,128]{1,0:T(8,128)(2,1)S(1)}, bf16[512,128]{1,0:T(8,128)(2,1)S(1)}, u32[]{:S(2)}, u32[]{:S(2)}) collective-permute-start(bf16[512,128]{1,0:T(8,128)(2,1)S(1)} %get-tuple-element.80), channel_id=1, source_target_pairs={{0,4},{1,5},{2,6},{3,7},{4,0},{5,1},{6,2},{7,3},{8,12},{9,13},{10,... | collective-permute-start | bytes 393224 | tf_op jit(solution)/shard_map/ppermute | solution.py:272
  75.0 8.8 %collective-permute-start.16 = (bf16[512,128]{1,0:T(8,128)(2,1)S(1)}, bf16[512,128]{1,0:T(8,128)(2,1)S(1)}, u32[]{:S(2)}, u32[]{:S(2)}) collective-permute-start(bf16[512,128]{1,0:T(8,128)(2,1)S(1)} %get-tuple-element.81), channel_id=1, source_target_pairs={{0,6},{1,7},{2,4},{3,5},{4,2},{5,3},{6,0},{7,1},{8,14},{9,15},{10,... | collective-permute-start | bytes 393224 | tf_op jit(solution)/shard_map/ppermute | solution.py:272
  78.0 13.8 %collective-permute-start.13 = (bf16[1024,128]{1,0:T(8,128)(2,1)S(1)}, bf16[1024,128]{1,0:T(8,128)(2,1)S(1)}, u32[]{:S(2)}, u32[]{:S(2)}) collective-permute-start(bf16[1024,128]{1,0:T(8,128)(2,1)S(1)} %get-tuple-element.77.refs_1_), channel_id=1, source_target_pairs={{0,16},{1,17},{2,18},{3,19},{4,20},{5,21},{6,22},{7,23},{8,24},{9,... | collective-permute-start | bytes 786440 | tf_op jit(solution)/shard_map/ppermute | solution.py:272
  79.9 14.8 %collective-permute-start.21 = (bf16[512,128]{1,0:T(8,128)(2,1)S(1)}, bf16[512,128]{1,0:T(8,128)(2,1)S(1)}, u32[]{:S(2)}, u32[]{:S(2)}) collective-permute-start(bf16[512,128]{1,0:T(8,128)(2,1)S(1)} %get-tuple-element.97), channel_id=1, source_target_pairs={{0,2},{1,3},{2,0},{3,1},{4,6},{5,7},{6,4},{7,5},{8,10},{9,11},{10,... | collective-permute-start | bytes 393224 | tf_op jit(solution)/shard_map/ppermute | solution.py:272
  80.1 16.9 %collective-permute-start.22 = (bf16[512,128]{1,0:T(8,128)(2,1)S(1)}, bf16[512,128]{1,0:T(8,128)(2,1)S(1)}, u32[]{:S(2)}, u32[]{:S(2)}) collective-permute-start(bf16[512,128]{1,0:T(8,128)(2,1)S(1)} %get-tuple-element.98), channel_id=1, source_target_pairs={{0,4},{1,5},{2,6},{3,7},{4,0},{5,1},{6,2},{7,3},{8,12},{9,13},{10,... | collective-permute-start | bytes 393224 | tf_op jit(solution)/shard_map/ppermute | solution.py:272
  82.2 14.9 %collective-permute-start.23 = (bf16[512,128]{1,0:T(8,128)(2,1)S(1)}, bf16[512,128]{1,0:T(8,128)(2,1)S(1)}, u32[]{:S(2)}, u32[]{:S(2)}) collective-permute-start(bf16[512,128]{1,0:T(8,128)(2,1)S(1)} %get-tuple-element.99), channel_id=1, source_target_pairs={{0,6},{1,7},{2,4},{3,5},{4,2},{5,3},{6,0},{7,1},{8,14},{9,15},{10,... | collective-permute-start | bytes 393224 | tf_op jit(solution)/shard_map/ppermute | solution.py:272
  94.1 7.8 %collective-permute-start.19 = (bf16[512,128]{1,0:T(8,128)(2,1)S(1)}, bf16[512,128]{1,0:T(8,128)(2,1)S(1)}, u32[]{:S(2)}, u32[]{:S(2)}) collective-permute-start(bf16[512,128]{1,0:T(8,128)(2,1)S(1)} %get-tuple-element.94), channel_id=1, source_target_pairs={{0,4},{1,5},{2,6},{3,7},{4,0},{5,1},{6,2},{7,3},{8,12},{9,13},{10,... | collective-permute-start | bytes 393224 | tf_op jit(solution)/shard_map/ppermute | solution.py:272
  94.6 7.3 %collective-permute-start.20 = (bf16[512,128]{1,0:T(8,128)(2,1)S(1)}, bf16[512,128]{1,0:T(8,128)(2,1)S(1)}, u32[]{:S(2)}, u32[]{:S(2)}) collective-permute-start(bf16[512,128]{1,0:T(8,128)(2,1)S(1)} %get-tuple-element.95), channel_id=1, source_target_pairs={{0,6},{1,7},{2,4},{3,5},{4,2},{5,3},{6,0},{7,1},{8,14},{9,15},{10,... | collective-permute-start | bytes 393224 | tf_op jit(solution)/shard_map/ppermute | solution.py:272
  102.7 6.9 %collective-permute-start.26 = (bf16[128,384]{1,0:T(8,128)(2,1)S(1)}, bf16[128,384]{1,0:T(8,128)(2,1)S(1)}, u32[]{:S(2)}, u32[]{:S(2)}) collective-permute-start(bf16[128,384]{1,0:T(8,128)(2,1)S(1)} %get-tuple-element.113), channel_id=1, source_target_pairs={{0,9},{1,8},{2,11},{3,10},{4,13},{5,12},{6,15},{7,14},{8,1},{9,0},... | collective-permute-start | bytes 294920 | tf_op jit(solution)/shard_map/ppermute | solution.py:272
  (10 other events, 79.3 us)

commit v3 on v2

--- a/solution.py
+++ b/solution.py
@@ -19,6 +19,7 @@
 F32 = jnp.float32
 VM = pl.BlockSpec(memory_space=pltpu.VMEM)
 SM = pl.BlockSpec(memory_space=pltpu.SMEM)
+HB = pl.BlockSpec(memory_space=pltpu.HBM)
 
 
 def over(x, n):
@@ -35,19 +36,21 @@
     return lax.broadcasted_iota(jnp.int32, shape, axis)
 
 
-def call(kernel, out_shape, in_specs, behind=(), flops=0):
+def call(kernel, out_shape, in_specs, behind=(), flops=0, scratch=(), vmem=None):
     count, many = len(in_specs), len(out_shape)
+    last = count + len(behind) + many
 
     def body(*refs):
-        kernel(*refs[:count], *refs[count + len(behind) : -1])
-        refs[-1][...] = jnp.zeros_like(refs[-1])
+        kernel(*refs[:count], *refs[count + len(behind) : last], *refs[last + 1 :])
+        refs[last][...] = jnp.zeros_like(refs[last])
 
     run = pl.pallas_call(
         body,
         out_shape=list(out_shape) + [jax.ShapeDtypeStruct((8, CH), F32)],
         in_specs=list(in_specs) + [VM] * len(behind),
         out_specs=[VM] * (many + 1),
-        compiler_params=pltpu.CompilerParams(vmem_limit_bytes=VMEM_LIMIT[0]),
+        scratch_shapes=list(scratch),
+        compiler_params=pltpu.CompilerParams(vmem_limit_bytes=vmem or VMEM_LIMIT[0]),
         cost_estimate=pl.CostEstimate(flops=flops, bytes_accessed=0, transcendentals=0),
     )
 
@@ -85,9 +88,13 @@
         return l * 2 + h
 
 
-def pack_kernel(lay, me, node, feats, out):
+def pack_kernel(lay, me, node, tiles, feats_far, out, feats, ids, arrived):
     unit, count = me[0], me[1]
     n = lay.slots
+    bring = pltpu.make_async_copy(feats_far, feats, arrived)
+    bring.start()
+    ids[...] = jnp.zeros_like(ids)
+    ids[1:3, 0 : tiles.shape[1]] = tiles[...]
     row = node[...]
     slot = iota((1, n), 1)
     live = slot < count
@@ -103,7 +110,6 @@
     rank = jnp.sum(jnp.where(before, 1, 0), axis=0, keepdims=True)
     target = jnp.where(live, (block * 4 + part) * lay.pair + rank, -1)
     pick = jnp.where(iota((n, n), 0) == target, 1.0, 0.0).astype(BF16)
-    sorted_rows = jnp.dot(pick, feats[...], preferred_element_type=F32).astype(BF16)
     place = jnp.where(live, row % PIECE + 1, 0).astype(F32).astype(BF16)
     place = jnp.broadcast_to(place, (16, n))
     lane = iota((lay.blocks * CH, n), 0)
@@ -113,7 +119,15 @@
     spread = jnp.where(wanted == target, 1.0, 0.0).astype(BF16)
     places = lax.dot_general(
         place, spread, (((1,), (1,)), ((), ())), preferred_element_type=F32
-    ).astype(BF16)
+    )[0:8]
+    top = iota((8, CH), 0) == 0
+    lower = ids[...].astype(F32)
+    bring.wait()
+    sorted_rows = jnp.dot(pick, feats[...], preferred_element_type=F32).astype(BF16)
+    below = [
+        jnp.where(top, places[:, b * CH : (b + 1) * CH], lower).astype(BF16)
+        for b in range(lay.blocks)
+    ]
     for z in range(lay.R):
         dh, dl = lay.split_z(z)
         for c in range(lay.C):
@@ -125,10 +139,10 @@
                 out[d, g * lay.slab : (g + 1) * lay.slab, :] = sorted_rows[
                     b * lay.slab : (b + 1) * lay.slab, lo : lo + CH
                 ]
-            out[d, lay.groups * lay.slab : lay.pay, :] = places[0:8, b * CH : (b + 1) * CH]
-
-
-def land_kernel(lay, first, many, me, got, out):
+            out[d, lay.groups * lay.slab : lay.pay, :] = below[b]
+
+
+def land_kernel(lay, first, many, me, got, out, ids=None):
     mine = me[2]
     lane = iota((1, CH), 1)
     part = (lane % lay.slab) // lay.pair
@@ -149,26 +163,31 @@
         out[:, g * CH : (g + 1) * CH] = jnp.dot(
             pick, block, preferred_element_type=F32
         ).astype(BF16)
-
-
-def dense_kernel(lay, me, i0, i1, i2, i3, v0, v1, v2, v3, a0, at0, a1, at1):
+    if ids is not None:
+        for i in range(4):
+            found = got[me[5 + i], lay.groups * lay.slab : lay.pay, :].astype(F32)
+            ids[2 * i : 2 * i + 2, :] = found[1:3, :].astype(jnp.int32)
+
+
+def dense_kernel(lay, turned, me, ids, v0, v1, v2, v3, near, far):
     chip, core = me[3], me[4]
-    for ref in (a0, at0, a1, at1):
-        ref[...] = jnp.zeros_like(ref)
+    near[...] = jnp.zeros_like(near)
+    far[...] = jnp.zeros_like(far)
     spare = 2 * lay.chips
-    for ids, values, a, at in ((i0, v0, a0, at0), (i1, v1, a1, at1), (i2, v2, a0, at0), (i3, v3, a1, at1)):
-
-        def body(t, carry, ids=ids, values=values, a=a, at=at):
-            rt, ct = ids[0, t], ids[1, t]
+    for i, (values, to) in enumerate(((v0, near), (v1, far), (v2, near), (v3, far))):
+
+        def body(t, carry, i=i, values=values, to=to):
+            rt, ct = ids[2 * i, t], ids[2 * i + 1, t]
             c = rest(rt, lay.C)
             r = (over(c, 2) ^ chip) * 2 + (rest(c, 2) ^ core)
-            j = rest(over(ct, lay.R), 2) * lay.R + rest(ct, lay.R)
+            k = rest(over(ct, lay.R), 2) * lay.R + rest(ct, lay.R)
             r = jnp.where(rt < lay.U, r, spare)
-            rr = pl.multiple_of(r * TILE, TILE)
-            kk = pl.multiple_of(j * TILE, TILE)
-            tile = values[t]
-            a[pl.ds(rr, TILE), pl.ds(kk, TILE)] = tile
-            at[pl.ds(kk, TILE), pl.ds(rr, TILE)] = jnp.transpose(tile)
+            rr = pl.ds(pl.multiple_of(r * TILE, TILE), TILE)
+            kk = pl.ds(pl.multiple_of(k * TILE, TILE), TILE)
+            if turned:
+                to[kk, rr] = jnp.transpose(values[t])
+            else:
+                to[rr, kk] = values[t]
             return carry
 
         lax.fori_loop(0, values.shape[0], body, 0, unroll=4)
@@ -204,15 +223,16 @@
     return (total * lax.rsqrt(power + epsilon)).astype(BF16)
 
 
-def encode_kernel(mix, *refs):
-    parts, out = refs[:-1], refs[-1]
-    for g in range(out.shape[1] // CH):
+def encode_kernel(parts, mix, *refs):
+    sums, a0, a1, hidden, outs = refs[:parts], refs[parts], refs[parts + 1], refs[parts + 2], refs[parts + 3 :]
+    for g in range(hidden.shape[1] // CH):
         span = slice(g * CH, (g + 1) * CH)
-        total = parts[0][:, span].astype(F32)
-        for ref in parts[1:]:
+        total = sums[0][:, span].astype(F32)
+        for ref in sums[1:]:
             total = total + ref[:, span].astype(F32)
         v = jnp.dot(unit_groups(total), mix[...], preferred_element_type=F32)
-        out[:, span] = (0.5 * v * (1.0 + lax.erf(v * (0.5**0.5)))).astype(BF16)
+        hidden[:, span] = (0.5 * v * (1.0 + lax.erf(v * (0.5**0.5)))).astype(BF16)
+    forward_kernel(1, a0, a1, hidden, *outs)
 
 
 def decode_kernel(parts, takes, lo, done, mix, *refs):
@@ -235,15 +255,19 @@
 
 
 def join_kernel(lay, me, *refs):
-    out = refs[-1]
+    early, late, out = refs[0:4], refs[4:8], refs[8]
     for rel in range(4):
-        at = pl.multiple_of((me[2] ^ rel) * lay.qw, CH)
-        out[:, pl.ds(at, lay.qw)] = refs[rel][...].astype(F32)
+        at = (me[2] ^ rel) * lay.qw
+        for ref in (early[rel], late[rel]):
+            width = ref.shape[1]
+            out[:, pl.ds(pl.multiple_of(at, CH), width)] = ref[...].astype(F32)
+            at += width
 
 
 GATHER = ((0, 1), (1, 2))
 SUMS = ((0, 1), (1, 1), (2, 1))
 BLOCK = 256
+PACK_VMEM = 58 * 1024 * 1024
 SEEN_FLOPS = 3_000_000_000
 FIRST_FLOPS = 5_000_000_000
 DECODE_FLOPS = 3_000_000_000
@@ -258,8 +282,10 @@
 
 def local(lay, ingest_features, node_map, unit_rows, tile_ids, tile_values, mix_in, mix_out):
     z, c = lax.axis_index("row"), lax.axis_index("col")
+    h, l = lay.split_z(z)
+    near = [lay.join_z(h ^ dh, l) * lay.C + (c ^ dc) for dc in (0, 1) for dh in (0, 1)]
     me = jnp.stack(
-        [z * lay.C + c, unit_rows[0], rest(z, 2) * 2 + rest(c, 2), over(c, 2), rest(c, 2)]
+        [z * lay.C + c, unit_rows[0], h * 2 + rest(c, 2), over(c, 2), rest(c, 2), *near]
     ).astype(jnp.int32)
 
     def exchange(x, dh=0, dl=0, chip=0, core=0):
@@ -271,42 +297,49 @@
                 pairs.append((zz * lay.C + cc, to))
         return lax.ppermute(x, ("row", "col"), pairs)
 
-    ids0 = tile_ids.T
-    ids1, val1 = exchange(ids0, dh=1), exchange(tile_values, dh=1)
-    ids2, val2 = exchange(ids0, core=1), exchange(tile_values, core=1)
-    ids3 = exchange(ids1, core=1)
+    val1, val2 = exchange(tile_values, dh=1), exchange(tile_values, core=1)
+    val3 = exchange(val1, core=1)
+    values = (tile_values, val1, val2, val3)
 
     (outgoing,), _ = call(
         functools.partial(pack_kernel, lay),
         [jax.ShapeDtypeStruct((lay.U, lay.pay, CH), BF16)],
-        [SM, VM, VM],
-    )(me, node_map.reshape(1, lay.slots), ingest_features)
+        [SM, VM, VM, HB],
+        scratch=[
+            pltpu.VMEM(ingest_features.shape, BF16),
+            pltpu.VMEM((8, CH), jnp.int32),
+            pltpu.SemaphoreType.DMA(()),
+        ],
+        vmem=PACK_VMEM,
+    )(me, node_map.reshape(1, lay.slots), tile_ids.T, ingest_features)
     got = lax.all_to_all(outgoing, ("row", "col"), split_axis=0, concat_axis=0, tiled=True)
 
-    val3 = exchange(val1, core=1)
-    ids, values = (ids0, ids1, ids2, ids3), (tile_values, val1, val2, val3)
-    _, token = call(seen_kernel, [], [SM] * 3 + [VM], flops=SEEN_FLOPS)(ids1, ids2, ids3, val3)
-
-    def land(first, many, token):
-        (x,), token = call(
+    _, token = call(seen_kernel, [], [VM], flops=SEEN_FLOPS)(val3)
+
+    def land(first, many, token, extra=()):
+        (x, *more), token = call(
             functools.partial(land_kernel, lay, first, many),
-            [array(lay.own, many * CH)],
+            [array(lay.own, many * CH), *extra],
             [SM, VM],
             behind=[token],
         )(me, got)
-        return [x] + [exchange(x, chip=s) for s in range(1, lay.chips)], token
-
-    xs, token = land(*GATHER[0], token)
+        return [x] + [exchange(x, chip=s) for s in range(1, lay.chips)], more, token
+
+    def dense(turned, token):
+        depth = 2 * lay.chips * PIECE + TILE
+        shape = (lay.chip_cols, depth) if turned else (depth, lay.chip_cols)
+        return call(
+            functools.partial(dense_kernel, lay, turned),
+            [array(*shape)] * 2,
+            [SM] * 2 + [VM] * 4,
+            behind=[token],
+        )(me, ids, *values)
+
+    xs, (ids,), token = land(*GATHER[0], token, [array(8, CH, jnp.int32)])
     gathered = [xs]
-    depth = 2 * lay.chips * PIECE + TILE
-    (a0, at0, a1, at1), token = call(
-        functools.partial(dense_kernel, lay),
-        [array(depth, lay.chip_cols), array(lay.chip_cols, depth)] * 2,
-        [SM] * 5 + [VM] * 4,
-        behind=[token],
-    )(me, *ids, *values)
+    (at0, at1), token = dense(True, token)
     for first, many in GATHER[1:]:
-        xs, token = land(first, many, token)
+        xs, _, token = land(first, many, token)
         gathered.append(xs)
     own = [xs[0] for xs in gathered]
 
@@ -324,16 +357,13 @@
 
     def forward(sums, token):
         shape = sums[0].shape
-        (hidden,), token = call(
-            encode_kernel, [array(*shape)], [VM] * (1 + lay.R2), behind=[token]
-        )(mix_in, *sums)
-        sent, token = call(
-            functools.partial(forward_kernel, 1),
-            [array(lay.own, shape[1])] * (lay.chips - 1),
-            [VM] * 3,
-            behind=[token],
-        )(a0, a1, hidden)
-        kept, token = call(
+        (hidden, *sent), token = call(
+            functools.partial(encode_kernel, lay.R2),
+            [array(*shape)] + [array(lay.own, shape[1])] * (lay.chips - 1),
+            [VM] * (3 + lay.R2),
+            behind=[token],
+        )(mix_in, *sums, a0, a1)
+        kept, _ = call(
             functools.partial(forward_kernel, 0),
             [array(lay.own, shape[1])],
             [VM] * 3,
@@ -343,40 +373,45 @@
 
     def decode(n, parts, left, token, flops=0):
         first, many = SUMS[n]
-        done = first * CH
+        done = left[0].shape[1] if left else 0
         return call(
-            functools.partial(decode_kernel, lay.chips, len(own), done, done),
+            functools.partial(decode_kernel, lay.chips, len(own), first * CH, done),
             [array(PIECE, done + many * CH, F32 if i == 0 else BF16) for i in range(4)],
             [VM] * (1 + len(own) + lay.chips + len(left)),
             behind=[token],
             flops=flops,
         )(mix_out, *own, *parts, *left)
+
+    def deliver(left):
+        return [
+            left[0],
+            exchange(left[1], core=1),
+            exchange(left[2], dh=1),
+            exchange(left[3], dh=1, core=1),
+        ]
 
     left, parts = [], []
     sums, token = back(0, token)
     for n in range(len(SUMS)):
         if n == 0:
             later, token = back(1, token)
+            (a0, a1), token = dense(False, token)
         part, token = forward(sums, token)
         parts.append(part)
         if n > 0:
             left, token = decode(n - 1, parts[n - 1], left, token, DECODE_FLOPS)
+        sums = later
         if n + 2 < len(SUMS):
-            sums = later
             later, token = back(n + 2, token)
-        else:
-            sums = later
-    left, token = decode(len(SUMS) - 1, parts[-1], left, token)
-    pieces = [
-        left[0],
-        exchange(left[1], core=1),
-        exchange(left[2], dh=1),
-        exchange(left[3], dh=1, core=1),
-    ]
+    early = deliver(left)
+    left, token = decode(len(SUMS) - 1, parts[-1], [], token)
+    _, token = call(seen_kernel, [], [VM] * 3, behind=[token], flops=SEEN_FLOPS)(*early[1:])
+    pieces = early + deliver(left)
     (out,), _ = call(
         functools.partial(join_kernel, lay),
         [array(PIECE, QUARTERS * lay.qw, F32)],
-        [SM] + [VM] * 4,
+        [SM] + [VM] * 8,
+        behind=[token],
     )(me, *pieces)
     return out
 

time: 111 us -> 107 us (0.964)
  starting transfers between devices: 33.9 us -> 30.2 us
  Pallas kernels: 21.1 us -> 24.7 us
  waiting for transfers between devices: 53.4 us -> 50.7 us
  local copies, waits for them, and re-layouts: 1.91 us -> 0.63 us
    ppermute x27, waiting for transfers between devices: 52.8 us -> 44.8 us  [exchange(): return lax.ppermute(x, ('row', 'col'), pairs)]
    all_to_all x1, waiting for transfers between devices: 0.6 us -> 5.84 us  [local(): lax.all_to_all(outgoing, ('row', 'col'), split_axis=0, concat_axis=0, til...]
    ppermute x27, starting transfers between devices: 29 us -> 25.4 us  [exchange(): return lax.ppermute(x, ('row', 'col'), pairs)]
    pallas_call x21 -> x20, Pallas kernels: 21.1 us -> 24.7 us  [apply(): *outs, token = run(*args, *behind)]
    unnamed x12 -> x8, local copies, waits for them, and re-layouts: 1.83 us -> 0.02 us
  transfers between devices with their start and end apart: 28 -> 28, of which waited for: 12 -> 11; matrix products, arithmetic and copies ran while one was open for 0% -> 1% of each run, Pallas kernels for 17% -> 22%
where the time goes in v3:
time: 107 us
  waiting for transfers between devices  50.7 us (47%)
  starting transfers between devices  30.2 us (28%)
  Pallas kernels  24.7 us (23%)
    ppermute x27, waiting for transfers between devices, exchange(): return lax.ppermute(x, ('row', 'col'), pairs)  44.8 us
    ppermute x27, starting transfers between devices, exchange(): return lax.ppermute(x, ('row', 'col'), pairs)  25.4 us
    pallas_call x20, Pallas kernels, apply(): *outs, token = run(*args, *behind)  24.7 us
    all_to_all x1, waiting for transfers between devices, local(): lax.all_to_all(outgoing, ('row', 'col'), split_axis=0, concat_axis=0, til...  5.84 us
    all_to_all x1, starting transfers between devices, local(): lax.all_to_all(outgoing, ('row', 'col'), split_axis=0, concat_axis=0, til...  4.84 us
  transfers between devices with their start and end apart: 28, of which 11 were waited for; matrix products, arithmetic and copies ran while one was open for 1% of the time, Pallas kernels for 22%

profile of v3, /device:TPU:0, one launch (start us, length us, event | category | flops | bytes accessed | tf_op | source)
XLA Modules:
  0.0 107.0 jit_solution(4273331980484383901)
XLA Ops:
  0.0 3.0 %collective-permute-start = (bf16[24,128,128]{2,1,0:T(8,128)(2,1)}, bf16[24,128,128]{2,1,0:T(8,128)(2,1)S(1)}, u32[]{:S(2)}, u32[]{:S(2)}) collective-permute-start(bf16[24,128,128]{2,1,0:T(8,128)(2,1)} %refs_2_.3), channel_id=1, source_target_pairs={{0,8},{1,9},{2,10},{3,11},{4,12},{5,13},{6,14},{7,15},{8,0},{9,1},... | collective-permute-start | bytes 2359304 | tf_op jit(solution)/shard_map/ppermute | solution.py:298
  4.3 3.1 %shard_map.73 = (bf16[32,104,128]{2,1,0:T(8,128)(2,1)}, f32[8,128]{1,0:T(8,128)}) custom-call(s32[9]{0:T(128)} %stack.35.refs_0_, s32[1,256]{1,0:T(1,128)} %bitcast.10, s32[2,24]{1,0:T(2,128)} %bitcast.11, bf16[256,1536]{1,0:T(8,128)(2,1)} %refs_3_.1), custom_call_target="tpu_custom_call" | custom-call | tf_op jit(solution)/shard_map/pallas_call | solution.py:58
  7.4 4.8 %all-to-all-start = ((bf16[32,104,128]{2,1,0:T(8,128)(2,1)}), bf16[32,104,128]{2,1,0:T(8,128)(2,1)S(1)}, u32[]{:S(2)}, u32[]{:S(2)}) async-start(bf16[32,104,128]{2,1,0:T(8,128)(2,1)} %get-tuple-element.57), calls=%async_computation | async-start | bytes 1703936 | tf_op jit(solution)/shard_map/all_to_all | solution.py:315
  12.3 14.6 %collective-permute-done.refs_3_ = bf16[24,128,128]{2,1,0:T(8,128)(2,1)S(1)} collective-permute-done((bf16[24,128,128]{2,1,0:T(8,128)(2,1)}, bf16[24,128,128]{2,1,0:T(8,128)(2,1)S(1)}, u32[]{:S(2)}, u32[]{:S(2)}) %collective-permute-start) | collective-permute-done | bytes 786464 | tf_op jit(solution)/shard_map/ppermute | solution.py:298
  27.4 2.8 %collective-permute-done.1.refs_0_.refs_5_ = bf16[24,128,128]{2,1,0:T(8,128)(2,1)S(1)} collective-permute-done((bf16[24,128,128]{2,1,0:T(8,128)(2,1)S(1)}, bf16[24,128,128]{2,1,0:T(8,128)(2,1)S(1)}, u32[]{:S(2)}, u32[]{:S(2)}) %collective-permute-start.1) | collective-permute-done | bytes 786464 | tf_op jit(solution)/shard_map/ppermute | solution.py:298
  30.2 5.8 %all-to-all-done.refs_1_ = bf16[32,104,128]{2,1,0:T(8,128)(2,1)S(1)} async-done(((bf16[32,104,128]{2,1,0:T(8,128)(2,1)}), bf16[32,104,128]{2,1,0:T(8,128)(2,1)S(1)}, u32[]{:S(2)}, u32[]{:S(2)}) %all-to-all-start) | async-done | bytes 852000 | tf_op jit(solution)/shard_map/all_to_all | solution.py:315
  37.1 1.6 %collective-permute-start.6 = (bf16[512,128]{1,0:T(8,128)(2,1)S(1)}, bf16[512,128]{1,0:T(8,128)(2,1)S(1)}, u32[]{:S(2)}, u32[]{:S(2)}) collective-permute-start(bf16[512,128]{1,0:T(8,128)(2,1)S(1)} %get-tuple-element.58.refs_2_.refs_1_), channel_id=1, source_target_pairs={{0,2},{1,3},{2,0},{3,1},{4,6},{5,7},{6,4},{7,5},{8,10},{9,11},{10,... | collective-permute-start | bytes 393224 | tf_op jit(solution)/shard_map/ppermute | solution.py:298
  40.6 3.7 %shard_map.76 = (bf16[1024,1152]{1,0:T(8,128)(2,1)S(1)}, bf16[1024,1152]{1,0:T(8,128)(2,1)S(1)}, f32[8,128]{1,0:T(8,128)S(1)}) custom-call(s32[9]{0:T(128)S(1)} %copy-done.3, s32[8,128]{1,0:T(8,128)S(1)} %get-tuple-element.59.refs_1_, bf16[24,128,128]{2,1,0:T(8,128)(2,1)S(1)} %copy-done, bf16[24,128,128]{2,1,0:T(8,128)(2,1)S(1)} %collective-permute-done.refs_3_, ...), custom_call_target="tpu_custom_call" | custom-call | tf_op jit(solution)/shard_map/pallas_call | solution.py:58
  45.6 1.6 %collective-permute-start.3 = (bf16[512,256]{1,0:T(8,128)(2,1)S(1)}, bf16[512,256]{1,0:T(8,128)(2,1)S(1)}, u32[]{:S(2)}, u32[]{:S(2)}) collective-permute-start(bf16[512,256]{1,0:T(8,128)(2,1)S(1)} %get-tuple-element.62.refs_2_), channel_id=1, source_target_pairs={{0,2},{1,3},{2,0},{3,1},{4,6},{5,7},{6,4},{7,5},{8,10},{9,11},{10,... | collective-permute-start | bytes 786440 | tf_op jit(solution)/shard_map/ppermute | solution.py:298
  50.4 1.4 %collective-permute-start.10 = (bf16[1024,128]{1,0:T(8,128)(2,1)S(1)}, bf16[1024,128]{1,0:T(8,128)(2,1)S(1)}, u32[]{:S(2)}, u32[]{:S(2)}) collective-permute-start(bf16[1024,128]{1,0:T(8,128)(2,1)S(1)} %get-tuple-element.71.refs_1_), channel_id=1, source_target_pairs={{0,16},{1,17},{2,18},{3,19},{4,20},{5,21},{6,22},{7,23},{8,24},{9,... | collective-permute-start | bytes 786440 | tf_op jit(solution)/shard_map/ppermute | solution.py:298
  51.8 2.8 %collective-permute-done.3.refs_3_ = bf16[512,256]{1,0:T(8,128)(2,1)S(1)} collective-permute-done((bf16[512,256]{1,0:T(8,128)(2,1)S(1)}, bf16[512,256]{1,0:T(8,128)(2,1)S(1)}, u32[]{:S(2)}, u32[]{:S(2)}) %collective-permute-start.3) | collective-permute-done | bytes 262176 | tf_op jit(solution)/shard_map/ppermute | solution.py:298
  54.6 6.1 %collective-permute-done.4.refs_4_ = bf16[512,256]{1,0:T(8,128)(2,1)S(1)} collective-permute-done((bf16[512,256]{1,0:T(8,128)(2,1)S(1)}, bf16[512,256]{1,0:T(8,128)(2,1)S(1)}, u32[]{:S(2)}, u32[]{:S(2)}) %collective-permute-start.4) | collective-permute-done | bytes 262176 | tf_op jit(solution)/shard_map/ppermute | solution.py:298
  62.5 2.7 %shard_map.80 = (bf16[1152,1024]{1,0:T(8,128)(2,1)S(1)}, bf16[1152,1024]{1,0:T(8,128)(2,1)S(1)}, f32[8,128]{1,0:T(8,128)S(1)}) custom-call(s32[9]{0:T(128)S(1)} %copy-done.3, s32[8,128]{1,0:T(8,128)S(1)} %get-tuple-element.59.refs_1_, bf16[24,128,128]{2,1,0:T(8,128)(2,1)S(1)} %copy-done, bf16[24,128,128]{2,1,0:T(8,128)(2,1)S(1)} %collective-permute-done.refs_3_, ...), custom_call_target="tpu_custom_call" | custom-call | tf_op jit(solution)/shard_map/pallas_call | solution.py:58
  65.3 5.1 %collective-permute-done.10.refs_2_ = bf16[1024,128]{1,0:T(8,128)(2,1)S(1)} collective-permute-done((bf16[1024,128]{1,0:T(8,128)(2,1)S(1)}, bf16[1024,128]{1,0:T(8,128)(2,1)S(1)}, u32[]{:S(2)}, u32[]{:S(2)}) %collective-permute-start.10) | collective-permute-done | bytes 262176 | tf_op jit(solution)/shard_map/ppermute | solution.py:298
  72.3 1.4 %collective-permute-start.15 = (bf16[512,128]{1,0:T(8,128)(2,1)S(1)}, bf16[512,128]{1,0:T(8,128)(2,1)S(1)}, u32[]{:S(2)}, u32[]{:S(2)}) collective-permute-start(bf16[512,128]{1,0:T(8,128)(2,1)S(1)} %get-tuple-element.84), channel_id=1, source_target_pairs={{0,4},{1,5},{2,6},{3,7},{4,0},{5,1},{6,2},{7,3},{8,12},{9,13},{10,... | collective-permute-start | bytes 393224 | tf_op jit(solution)/shard_map/ppermute | solution.py:298
  73.7 1.6 %collective-permute-start.16 = (bf16[512,128]{1,0:T(8,128)(2,1)S(1)}, bf16[512,128]{1,0:T(8,128)(2,1)S(1)}, u32[]{:S(2)}, u32[]{:S(2)}) collective-permute-start(bf16[512,128]{1,0:T(8,128)(2,1)S(1)} %get-tuple-element.85), channel_id=1, source_target_pairs={{0,6},{1,7},{2,4},{3,5},{4,2},{5,3},{6,0},{7,1},{8,14},{9,15},{10,... | collective-permute-start | bytes 393224 | tf_op jit(solution)/shard_map/ppermute | solution.py:298
  77.6 1.3 %shard_map.83 = (bf16[1024,128]{1,0:T(8,128)(2,1)S(1)}, bf16[512,128]{1,0:T(8,128)(2,1)S(1)}, bf16[512,128]{1,0:T(8,128)(2,1)S(1)}, bf16[512,128]{1,0:T(8,128)(2,1)S(1)}, f32[8,128]{1,0:T(8,128)S(1)}) custom-call(bf16[128,128]{1,0:T(8,128)(2,1)S(1)} %copy-done.1, bf16[1024,128]{1,0:T(8,128)(2,1)S(1)} %get-tuple-element.70.refs_1_, ...), custom_call_target="tpu_custom_call" | custom-call | tf_op jit(solution)/shard_map/pallas_call | solution.py:58
  80.4 1.4 %collective-permute-start.12 = (bf16[512,128]{1,0:T(8,128)(2,1)S(1)}, bf16[512,128]{1,0:T(8,128)(2,1)S(1)}, u32[]{:S(2)}, u32[]{:S(2)}) collective-permute-start(bf16[512,128]{1,0:T(8,128)(2,1)S(1)} %get-tuple-element.79), channel_id=1, source_target_pairs={{0,4},{1,5},{2,6},{3,7},{4,0},{5,1},{6,2},{7,3},{8,12},{9,13},{10,... | collective-permute-start | bytes 393224 | tf_op jit(solution)/shard_map/ppermute | solution.py:298
  81.8 1.6 %collective-permute-start.13 = (bf16[512,128]{1,0:T(8,128)(2,1)S(1)}, bf16[512,128]{1,0:T(8,128)(2,1)S(1)}, u32[]{:S(2)}, u32[]{:S(2)}) collective-permute-start(bf16[512,128]{1,0:T(8,128)(2,1)S(1)} %get-tuple-element.80), channel_id=1, source_target_pairs={{0,6},{1,7},{2,4},{3,5},{4,2},{5,3},{6,0},{7,1},{8,14},{9,15},{10,... | collective-permute-start | bytes 393224 | tf_op jit(solution)/shard_map/ppermute | solution.py:298
  83.7 7.0 %collective-permute-done.17.refs_2_ = bf16[1024,128]{1,0:T(8,128)(2,1)S(1)} collective-permute-done((bf16[1024,128]{1,0:T(8,128)(2,1)S(1)}, bf16[1024,128]{1,0:T(8,128)(2,1)S(1)}, u32[]{:S(2)}, u32[]{:S(2)}) %collective-permute-start.17) | collective-permute-done | bytes 262176 | tf_op jit(solution)/shard_map/ppermute | solution.py:298
  92.9 2.6 %collective-permute-start.23 = (bf16[512,128]{1,0:T(8,128)(2,1)S(1)}, bf16[512,128]{1,0:T(8,128)(2,1)S(1)}, u32[]{:S(2)}, u32[]{:S(2)}) collective-permute-start(bf16[512,128]{1,0:T(8,128)(2,1)S(1)} %get-tuple-element.101), channel_id=1, source_target_pairs={{0,6},{1,7},{2,4},{3,5},{4,2},{5,3},{6,0},{7,1},{8,14},{9,15},{10,... | collective-permute-start | bytes 393224 | tf_op jit(solution)/shard_map/ppermute | solution.py:298
  96.0 2.4 %collective-permute-done.21.refs_4_ = bf16[512,128]{1,0:T(8,128)(2,1)S(1)} collective-permute-done((bf16[512,128]{1,0:T(8,128)(2,1)S(1)}, bf16[512,128]{1,0:T(8,128)(2,1)S(1)}, u32[]{:S(2)}, u32[]{:S(2)}) %collective-permute-start.21) | collective-permute-done | bytes 131104 | tf_op jit(solution)/shard_map/ppermute | solution.py:298
  102.7 2.1 %collective-permute-done.25.refs_7_ = bf16[128,128]{1,0:T(8,128)(2,1)S(1)} collective-permute-done((bf16[128,128]{1,0:T(8,128)(2,1)S(1)}, bf16[128,128]{1,0:T(8,128)(2,1)S(1)}, u32[]{:S(2)}, u32[]{:S(2)}) %collective-permute-start.25) | collective-permute-done | bytes 32800 | tf_op jit(solution)/shard_map/ppermute | solution.py:298
  105.6 1.5 %shard_map.92 = (f32[128,1536]{1,0:T(8,128)}, f32[8,128]{1,0:T(8,128)}) custom-call(s32[9]{0:T(128)S(1)} %copy-done.3, f32[128,256]{1,0:T(8,128)S(1)} %get-tuple-element.93.refs_1_, bf16[128,256]{1,0:T(8,128)(2,1)S(1)} %collective-permute-done.18.refs_0_.refs_2_, bf16[128,256]{1,0:T(8,128)(2,1)S(1)} %collective-permute-done.19.refs_1_.refs_3_, ...), custom_call_target="tpu_custom_call" | custom-call | tf_op jit(solution)/shard_map/pallas_call | solution.py:58
  (61 shorter events, 24.1 us)
Async XLA Ops:
  0.0 26.9 %collective-permute-start = (bf16[24,128,128]{2,1,0:T(8,128)(2,1)}, bf16[24,128,128]{2,1,0:T(8,128)(2,1)S(1)}, u32[]{:S(2)}, u32[]{:S(2)}) collective-permute-start(bf16[24,128,128]{2,1,0:T(8,128)(2,1)} %refs_2_.3), channel_id=1, source_target_pairs={{0,8},{1,9},{2,10},{3,11},{4,12},{5,13},{6,14},{7,15},{8,0},{9,1},... | collective-permute-start | bytes 2359304 | tf_op jit(solution)/shard_map/ppermute | solution.py:298
  7.4 28.7 %all-to-all-start = ((bf16[32,104,128]{2,1,0:T(8,128)(2,1)}), bf16[32,104,128]{2,1,0:T(8,128)(2,1)S(1)}, u32[]{:S(2)}, u32[]{:S(2)}) async-start(bf16[32,104,128]{2,1,0:T(8,128)(2,1)} %get-tuple-element.57), calls=%async_computation | async-start | bytes 1703936 | tf_op jit(solution)/shard_map/all_to_all | solution.py:315
  26.9 13.7 %collective-permute-start.2 = (bf16[24,128,128]{2,1,0:T(8,128)(2,1)S(1)}, bf16[24,128,128]{2,1,0:T(8,128)(2,1)}, u32[]{:S(2)}, u32[]{:S(2)}) collective-permute-start(bf16[24,128,128]{2,1,0:T(8,128)(2,1)S(1)} %copy-done), channel_id=1, source_target_pairs={{0,1},{1,0},{2,3},{3,2},{4,5},{5,4},{6,7},{7,6},{8,9},{9,8},{10,11... | collective-permute-start | bytes 2359304 | tf_op jit(solution)/shard_map/ppermute | solution.py:298
  37.1 11.3 %collective-permute-start.6 = (bf16[512,128]{1,0:T(8,128)(2,1)S(1)}, bf16[512,128]{1,0:T(8,128)(2,1)S(1)}, u32[]{:S(2)}, u32[]{:S(2)}) collective-permute-start(bf16[512,128]{1,0:T(8,128)(2,1)S(1)} %get-tuple-element.58.refs_2_.refs_1_), channel_id=1, source_target_pairs={{0,2},{1,3},{2,0},{3,1},{4,6},{5,7},{6,4},{7,5},{8,10},{9,11},{10,... | collective-permute-start | bytes 393224 | tf_op jit(solution)/shard_map/ppermute | solution.py:298
  38.6 10.5 %collective-permute-start.7 = (bf16[512,128]{1,0:T(8,128)(2,1)S(1)}, bf16[512,128]{1,0:T(8,128)(2,1)S(1)}, u32[]{:S(2)}, u32[]{:S(2)}) collective-permute-start(bf16[512,128]{1,0:T(8,128)(2,1)S(1)} %get-tuple-element.58.refs_2_.refs_1_), channel_id=1, source_target_pairs={{0,4},{1,5},{2,6},{3,7},{4,0},{5,1},{6,2},{7,3},{8,12},{9,13},{10,... | collective-permute-start | bytes 393224 | tf_op jit(solution)/shard_map/ppermute | solution.py:298
  39.9 9.3 %collective-permute-start.8 = (bf16[512,128]{1,0:T(8,128)(2,1)S(1)}, bf16[512,128]{1,0:T(8,128)(2,1)S(1)}, u32[]{:S(2)}, u32[]{:S(2)}) collective-permute-start(bf16[512,128]{1,0:T(8,128)(2,1)S(1)} %get-tuple-element.58.refs_2_.refs_1_), channel_id=1, source_target_pairs={{0,6},{1,7},{2,4},{3,5},{4,2},{5,3},{6,0},{7,1},{8,14},{9,15},{10,... | collective-permute-start | bytes 393224 | tf_op jit(solution)/shard_map/ppermute | solution.py:298
  45.6 9.1 %collective-permute-start.3 = (bf16[512,256]{1,0:T(8,128)(2,1)S(1)}, bf16[512,256]{1,0:T(8,128)(2,1)S(1)}, u32[]{:S(2)}, u32[]{:S(2)}) collective-permute-start(bf16[512,256]{1,0:T(8,128)(2,1)S(1)} %get-tuple-element.62.refs_2_), channel_id=1, source_target_pairs={{0,2},{1,3},{2,0},{3,1},{4,6},{5,7},{6,4},{7,5},{8,10},{9,11},{10,... | collective-permute-start | bytes 786440 | tf_op jit(solution)/shard_map/ppermute | solution.py:298
  47.1 13.6 %collective-permute-start.4 = (bf16[512,256]{1,0:T(8,128)(2,1)S(1)}, bf16[512,256]{1,0:T(8,128)(2,1)S(1)}, u32[]{:S(2)}, u32[]{:S(2)}) collective-permute-start(bf16[512,256]{1,0:T(8,128)(2,1)S(1)} %get-tuple-element.62.refs_2_), channel_id=1, source_target_pairs={{0,4},{1,5},{2,6},{3,7},{4,0},{5,1},{6,2},{7,3},{8,12},{9,13},{10,... | collective-permute-start | bytes 786440 | tf_op jit(solution)/shard_map/ppermute | solution.py:298
  48.4 12.3 %collective-permute-start.5 = (bf16[512,256]{1,0:T(8,128)(2,1)S(1)}, bf16[512,256]{1,0:T(8,128)(2,1)S(1)}, u32[]{:S(2)}, u32[]{:S(2)}) collective-permute-start(bf16[512,256]{1,0:T(8,128)(2,1)S(1)} %get-tuple-element.62.refs_2_), channel_id=1, source_target_pairs={{0,6},{1,7},{2,4},{3,5},{4,2},{5,3},{6,0},{7,1},{8,14},{9,15},{10,... | collective-permute-start | bytes 786440 | tf_op jit(solution)/shard_map/ppermute | solution.py:298
  50.4 20.0 %collective-permute-start.10 = (bf16[1024,128]{1,0:T(8,128)(2,1)S(1)}, bf16[1024,128]{1,0:T(8,128)(2,1)S(1)}, u32[]{:S(2)}, u32[]{:S(2)}) collective-permute-start(bf16[1024,128]{1,0:T(8,128)(2,1)S(1)} %get-tuple-element.71.refs_1_), channel_id=1, source_target_pairs={{0,16},{1,17},{2,18},{3,19},{4,20},{5,21},{6,22},{7,23},{8,24},{9,... | collective-permute-start | bytes 786440 | tf_op jit(solution)/shard_map/ppermute | solution.py:298
  62.0 15.6 %collective-permute-start.9 = (bf16[1024,128]{1,0:T(8,128)(2,1)S(1)}, bf16[1024,128]{1,0:T(8,128)(2,1)S(1)}, u32[]{:S(2)}, u32[]{:S(2)}) collective-permute-start(bf16[1024,128]{1,0:T(8,128)(2,1)S(1)} %get-tuple-element.70.refs_1_), channel_id=1, source_target_pairs={{0,16},{1,17},{2,18},{3,19},{4,20},{5,21},{6,22},{7,23},{8,24},{9,... | collective-permute-start | bytes 786440 | tf_op jit(solution)/shard_map/ppermute | solution.py:298
  71.7 8.7 %collective-permute-start.14 = (bf16[512,128]{1,0:T(8,128)(2,1)S(1)}, bf16[512,128]{1,0:T(8,128)(2,1)S(1)}, u32[]{:S(2)}, u32[]{:S(2)}) collective-permute-start(bf16[512,128]{1,0:T(8,128)(2,1)S(1)} %get-tuple-element.83), channel_id=1, source_target_pairs={{0,2},{1,3},{2,0},{3,1},{4,6},{5,7},{6,4},{7,5},{8,10},{9,11},{10,... | collective-permute-start | bytes 393224 | tf_op jit(solution)/shard_map/ppermute | solution.py:298
  72.3 9.5 %collective-permute-start.15 = (bf16[512,128]{1,0:T(8,128)(2,1)S(1)}, bf16[512,128]{1,0:T(8,128)(2,1)S(1)}, u32[]{:S(2)}, u32[]{:S(2)}) collective-permute-start(bf16[512,128]{1,0:T(8,128)(2,1)S(1)} %get-tuple-element.84), channel_id=1, source_target_pairs={{0,4},{1,5},{2,6},{3,7},{4,0},{5,1},{6,2},{7,3},{8,12},{9,13},{10,... | collective-permute-start | bytes 393224 | tf_op jit(solution)/shard_map/ppermute | solution.py:298
  73.7 9.8 %collective-permute-start.16 = (bf16[512,128]{1,0:T(8,128)(2,1)S(1)}, bf16[512,128]{1,0:T(8,128)(2,1)S(1)}, u32[]{:S(2)}, u32[]{:S(2)}) collective-permute-start(bf16[512,128]{1,0:T(8,128)(2,1)S(1)} %get-tuple-element.85), channel_id=1, source_target_pairs={{0,6},{1,7},{2,4},{3,5},{4,2},{5,3},{6,0},{7,1},{8,14},{9,15},{10,... | collective-permute-start | bytes 393224 | tf_op jit(solution)/shard_map/ppermute | solution.py:298
  77.5 13.2 %collective-permute-start.17 = (bf16[1024,128]{1,0:T(8,128)(2,1)S(1)}, bf16[1024,128]{1,0:T(8,128)(2,1)S(1)}, u32[]{:S(2)}, u32[]{:S(2)}) collective-permute-start(bf16[1024,128]{1,0:T(8,128)(2,1)S(1)} %get-tuple-element.90.refs_1_), channel_id=1, source_target_pairs={{0,16},{1,17},{2,18},{3,19},{4,20},{5,21},{6,22},{7,23},{8,24},{9,... | collective-permute-start | bytes 786440 | tf_op jit(solution)/shard_map/ppermute | solution.py:298
  78.9 14.0 %collective-permute-start.11 = (bf16[512,128]{1,0:T(8,128)(2,1)S(1)}, bf16[512,128]{1,0:T(8,128)(2,1)S(1)}, u32[]{:S(2)}, u32[]{:S(2)}) collective-permute-start(bf16[512,128]{1,0:T(8,128)(2,1)S(1)} %get-tuple-element.78), channel_id=1, source_target_pairs={{0,2},{1,3},{2,0},{3,1},{4,6},{5,7},{6,4},{7,5},{8,10},{9,11},{10,... | collective-permute-start | bytes 393224 | tf_op jit(solution)/shard_map/ppermute | solution.py:298
  80.4 15.1 %collective-permute-start.12 = (bf16[512,128]{1,0:T(8,128)(2,1)S(1)}, bf16[512,128]{1,0:T(8,128)(2,1)S(1)}, u32[]{:S(2)}, u32[]{:S(2)}) collective-permute-start(bf16[512,128]{1,0:T(8,128)(2,1)S(1)} %get-tuple-element.79), channel_id=1, source_target_pairs={{0,4},{1,5},{2,6},{3,7},{4,0},{5,1},{6,2},{7,3},{8,12},{9,13},{10,... | collective-permute-start | bytes 393224 | tf_op jit(solution)/shard_map/ppermute | solution.py:298
  81.8 13.8 %collective-permute-start.13 = (bf16[512,128]{1,0:T(8,128)(2,1)S(1)}, bf16[512,128]{1,0:T(8,128)(2,1)S(1)}, u32[]{:S(2)}, u32[]{:S(2)}) collective-permute-start(bf16[512,128]{1,0:T(8,128)(2,1)S(1)} %get-tuple-element.80), channel_id=1, source_target_pairs={{0,6},{1,7},{2,4},{3,5},{4,2},{5,3},{6,0},{7,1},{8,14},{9,15},{10,... | collective-permute-start | bytes 393224 | tf_op jit(solution)/shard_map/ppermute | solution.py:298
  92.0 6.4 %collective-permute-start.21 = (bf16[512,128]{1,0:T(8,128)(2,1)S(1)}, bf16[512,128]{1,0:T(8,128)(2,1)S(1)}, u32[]{:S(2)}, u32[]{:S(2)}) collective-permute-start(bf16[512,128]{1,0:T(8,128)(2,1)S(1)} %get-tuple-element.99), channel_id=1, source_target_pairs={{0,2},{1,3},{2,0},{3,1},{4,6},{5,7},{6,4},{7,5},{8,10},{9,11},{10,... | collective-permute-start | bytes 393224 | tf_op jit(solution)/shard_map/ppermute | solution.py:298
  92.5 7.9 %collective-permute-start.22 = (bf16[512,128]{1,0:T(8,128)(2,1)S(1)}, bf16[512,128]{1,0:T(8,128)(2,1)S(1)}, u32[]{:S(2)}, u32[]{:S(2)}) collective-permute-start(bf16[512,128]{1,0:T(8,128)(2,1)S(1)} %get-tuple-element.100), channel_id=1, source_target_pairs={{0,4},{1,5},{2,6},{3,7},{4,0},{5,1},{6,2},{7,3},{8,12},{9,13},{10,... | collective-permute-start | bytes 393224 | tf_op jit(solution)/shard_map/ppermute | solution.py:298
  92.9 7.5 %collective-permute-start.23 = (bf16[512,128]{1,0:T(8,128)(2,1)S(1)}, bf16[512,128]{1,0:T(8,128)(2,1)S(1)}, u32[]{:S(2)}, u32[]{:S(2)}) collective-permute-start(bf16[512,128]{1,0:T(8,128)(2,1)S(1)} %get-tuple-element.101), channel_id=1, source_target_pairs={{0,6},{1,7},{2,4},{3,5},{4,2},{5,3},{6,0},{7,1},{8,14},{9,15},{10,... | collective-permute-start | bytes 393224 | tf_op jit(solution)/shard_map/ppermute | solution.py:298
  95.9 6.0 %collective-permute-start.18 = (bf16[128,256]{1,0:T(8,128)(2,1)S(1)}, bf16[128,256]{1,0:T(8,128)(2,1)S(1)}, u32[]{:S(2)}, u32[]{:S(2)}) collective-permute-start(bf16[128,256]{1,0:T(8,128)(2,1)S(1)} %get-tuple-element.94), channel_id=1, source_target_pairs={{0,1},{1,0},{2,3},{3,2},{4,5},{5,4},{6,7},{7,6},{8,9},{9,8},{10,11... | collective-permute-start | bytes 196616 | tf_op jit(solution)/shard_map/ppermute | solution.py:298
  96.0 6.7 %collective-permute-start.19 = (bf16[128,256]{1,0:T(8,128)(2,1)S(1)}, bf16[128,256]{1,0:T(8,128)(2,1)S(1)}, u32[]{:S(2)}, u32[]{:S(2)}) collective-permute-start(bf16[128,256]{1,0:T(8,128)(2,1)S(1)} %get-tuple-element.95), channel_id=1, source_target_pairs={{0,8},{1,9},{2,10},{3,11},{4,12},{5,13},{6,14},{7,15},{8,0},{9,1},... | collective-permute-start | bytes 196616 | tf_op jit(solution)/shard_map/ppermute | solution.py:298
  98.4 4.2 %collective-permute-start.20 = (bf16[128,256]{1,0:T(8,128)(2,1)S(1)}, bf16[128,256]{1,0:T(8,128)(2,1)S(1)}, u32[]{:S(2)}, u32[]{:S(2)}) collective-permute-start(bf16[128,256]{1,0:T(8,128)(2,1)S(1)} %get-tuple-element.96), channel_id=1, source_target_pairs={{0,9},{1,8},{2,11},{3,10},{4,13},{5,12},{6,15},{7,14},{8,1},{9,0},... | collective-permute-start | bytes 196616 | tf_op jit(solution)/shard_map/ppermute | solution.py:298
  (8 other events, 76.0 us)

commit v4 on v3

--- a/solution.py
+++ b/solution.py
@@ -22,6 +22,15 @@
 HB = pl.BlockSpec(memory_space=pltpu.HBM)
 
 
+class Here:
+    def __init__(self, lay):
+        z, c = lax.axis_index("row"), lax.axis_index("col")
+        self.col, self.unit = c, z * lay.C + c
+        self.h, self.l = lay.split_z(z)
+        self.chip, self.core = over(c, 2), rest(c, 2)
+        self.quarter = self.h * 2 + self.core
+
+
 def over(x, n):
     assert n & (n - 1) == 0
     return x >> (n.bit_length() - 1)
@@ -36,7 +45,7 @@
     return lax.broadcasted_iota(jnp.int32, shape, axis)
 
 
-def call(kernel, out_shape, in_specs, behind=(), flops=0, scratch=(), vmem=None):
+def call(kernel, out_shape, in_specs, behind=(), flops=0, scratch=(), vmem=None, out_specs=None, aliases=None):
     count, many = len(in_specs), len(out_shape)
     last = count + len(behind) + many
 
@@ -48,7 +57,8 @@
         body,
         out_shape=list(out_shape) + [jax.ShapeDtypeStruct((8, CH), F32)],
         in_specs=list(in_specs) + [VM] * len(behind),
-        out_specs=[VM] * (many + 1),
+        out_specs=list(out_specs or [VM] * many) + [VM],
+        input_output_aliases=aliases or {},
         scratch_shapes=list(scratch),
         compiler_params=pltpu.CompilerParams(vmem_limit_bytes=vmem or VMEM_LIMIT[0]),
         cost_estimate=pl.CostEstimate(flops=flops, bytes_accessed=0, transcendentals=0),
@@ -88,8 +98,8 @@
         return l * 2 + h
 
 
-def pack_kernel(lay, me, node, tiles, feats_far, out, feats, ids, arrived):
-    unit, count = me[0], me[1]
+def pack_kernel(lay, held, node, tiles, feats_far, out_far, out, feats, ids, arrived, gone):
+    unit, count = Here(lay).unit, held[0]
     n = lay.slots
     bring = pltpu.make_async_copy(feats_far, feats, arrived)
     bring.start()
@@ -98,11 +108,11 @@
     row = node[...]
     slot = iota((1, n), 1)
     live = slot < count
-    p = row // PIECE
-    h, l = lay.split_z(p // lay.C)
-    c = p % lay.C
-    block = l * lay.chips + c // 2
-    part = h * 2 + c % 2
+    p = over(row, PIECE)
+    h, l = lay.split_z(over(p, lay.C))
+    c = rest(p, lay.C)
+    block = l * lay.chips + over(c, 2)
+    part = h * 2 + rest(c, 2)
     p = jnp.where(live, p, -1)
     across = jnp.broadcast_to(p, (n, n))
     down = jnp.transpose(across)
@@ -110,43 +120,49 @@
     rank = jnp.sum(jnp.where(before, 1, 0), axis=0, keepdims=True)
     target = jnp.where(live, (block * 4 + part) * lay.pair + rank, -1)
     pick = jnp.where(iota((n, n), 0) == target, 1.0, 0.0).astype(BF16)
-    place = jnp.where(live, row % PIECE + 1, 0).astype(F32).astype(BF16)
+    place = jnp.where(live, rest(row, PIECE) + 1, 0).astype(F32).astype(BF16)
     place = jnp.broadcast_to(place, (16, n))
-    lane = iota((lay.blocks * CH, n), 0)
-    inner = lane % CH - (unit % lay.upl) * lay.slab
-    wanted = (lane // CH) * lay.slab + inner
-    wanted = jnp.where((inner >= 0) & (inner < lay.slab), wanted, -2)
-    spread = jnp.where(wanted == target, 1.0, 0.0).astype(BF16)
     places = lax.dot_general(
-        place, spread, (((1,), (1,)), ((), ())), preferred_element_type=F32
-    )[0:8]
+        place, pick, (((1,), (1,)), ((), ())), preferred_element_type=F32
+    )
+    block = over(iota((lay.blocks, n), 1), lay.slab) == iota((lay.blocks, n), 0)
+    place = jnp.where(block, places[0:1, :], 0.0).astype(BF16)
+    fro, to = iota((n, CH), 0), iota((n, CH), 1)
+    move = (rest(fro, lay.slab) == rest(to, lay.slab)) & (
+        over(to, lay.slab) == rest(unit, lay.upl)
+    )
+    move = jnp.where(move, 1.0, 0.0).astype(BF16)
+    places = jnp.dot(place, move, preferred_element_type=F32)
     top = iota((8, CH), 0) == 0
     lower = ids[...].astype(F32)
     bring.wait()
-    sorted_rows = jnp.dot(pick, feats[...], preferred_element_type=F32).astype(BF16)
     below = [
-        jnp.where(top, places[:, b * CH : (b + 1) * CH], lower).astype(BF16)
+        jnp.where(top, places[b : b + 1, :], lower).astype(BF16)
         for b in range(lay.blocks)
     ]
-    for z in range(lay.R):
-        dh, dl = lay.split_z(z)
-        for c in range(lay.C):
-            b = dl * lay.chips + c // 2
-            q = dh * 2 + c % 2
-            d = z * lay.C + c
-            for g in range(lay.groups):
-                lo = q * lay.qw + g * CH
-                out[d, g * lay.slab : (g + 1) * lay.slab, :] = sorted_rows[
-                    b * lay.slab : (b + 1) * lay.slab, lo : lo + CH
-                ]
-            out[d, lay.groups * lay.slab : lay.pay, :] = below[b]
-
-
-def land_kernel(lay, first, many, me, got, out, ids=None):
-    mine = me[2]
+    for q in range(QUARTERS):
+        ordered = jnp.dot(
+            pick, feats[:, q * lay.qw : (q + 1) * lay.qw], preferred_element_type=F32
+        ).astype(BF16)
+        for l in range(lay.R2):
+            for chip in range(lay.chips):
+                b = l * lay.chips + chip
+                d = lay.join_z(q // 2, l) * lay.C + chip * 2 + q % 2
+                for g in range(lay.groups):
+                    out[d, g * lay.slab : (g + 1) * lay.slab, :] = ordered[
+                        b * lay.slab : (b + 1) * lay.slab, g * CH : (g + 1) * CH
+                    ]
+                out[d, lay.groups * lay.slab : lay.pay, :] = below[b]
+                pltpu.make_async_copy(out.at[d], out_far.at[d], gone.at[d]).start()
+    for d in range(lay.U):
+        pltpu.make_async_copy(out.at[d], out_far.at[d], gone.at[d]).wait()
+
+
+def land_kernel(lay, first, many, got, out, ids=None):
+    here = Here(lay)
     lane = iota((1, CH), 1)
     part = (lane % lay.slab) // lay.pair
-    base = (part ^ mine) * PIECE - 1
+    base = (part ^ here.quarter) * PIECE - 1
     rows = iota((lay.own, CH), 0)
     picks = []
     for j in range(lay.U // lay.upl):
@@ -165,12 +181,13 @@
         ).astype(BF16)
     if ids is not None:
         for i in range(4):
-            found = got[me[5 + i], lay.groups * lay.slab : lay.pay, :].astype(F32)
+            z = lay.join_z(here.h ^ (i % 2), here.l)
+            found = got[z * lay.C + (here.col ^ (i // 2)), lay.groups * lay.slab : lay.pay, :].astype(F32)
             ids[2 * i : 2 * i + 2, :] = found[1:3, :].astype(jnp.int32)
 
 
-def dense_kernel(lay, turned, me, ids, v0, v1, v2, v3, near, far):
-    chip, core = me[3], me[4]
+def dense_kernel(lay, turned, ids, v0, v1, v2, v3, near, far):
+    here = Here(lay)
     near[...] = jnp.zeros_like(near)
     far[...] = jnp.zeros_like(far)
     spare = 2 * lay.chips
@@ -179,7 +196,7 @@
         def body(t, carry, i=i, values=values, to=to):
             rt, ct = ids[2 * i, t], ids[2 * i + 1, t]
             c = rest(rt, lay.C)
-            r = (over(c, 2) ^ chip) * 2 + (rest(c, 2) ^ core)
+            r = (over(c, 2) ^ here.chip) * 2 + (rest(c, 2) ^ here.core)
             k = rest(over(ct, lay.R), 2) * lay.R + rest(ct, lay.R)
             r = jnp.where(rt < lay.U, r, spare)
             rr = pl.ds(pl.multiple_of(r * TILE, TILE), TILE)
@@ -254,14 +271,24 @@
             out[:, to] = left[i * PIECE : (i + 1) * PIECE, :].astype(out.dtype)
 
 
-def join_kernel(lay, me, *refs):
-    early, late, out = refs[0:4], refs[4:8], refs[8]
-    for rel in range(4):
-        at = (me[2] ^ rel) * lay.qw
-        for ref in (early[rel], late[rel]):
-            width = ref.shape[1]
-            out[:, pl.ds(pl.multiple_of(at, CH), width)] = ref[...].astype(F32)
-            at += width
+def join_kernel(lay, done, kept, *refs):
+    pieces = refs[:4]
+    far, wide, gone = refs[-3:]
+    mine, width = Here(lay).quarter, pieces[0].shape[1]
+    copies = []
+    for rel, ref in enumerate(pieces):
+        wide[rel] = ref[...].astype(F32)
+        at = pl.multiple_of((mine ^ rel) * lay.qw + done, CH)
+        copies.append(
+            pltpu.make_async_copy(wide.at[rel], far.at[:, pl.ds(at, width)], gone.at[rel])
+        )
+        copies[-1].start()
+    for copy in copies:
+        copy.wait()
+
+
+def first_join_kernel(lay, done, *refs):
+    join_kernel(lay, done, None, *refs)
 
 
 GATHER = ((0, 1), (1, 2))
@@ -281,13 +308,6 @@
 
 
 def local(lay, ingest_features, node_map, unit_rows, tile_ids, tile_values, mix_in, mix_out):
-    z, c = lax.axis_index("row"), lax.axis_index("col")
-    h, l = lay.split_z(z)
-    near = [lay.join_z(h ^ dh, l) * lay.C + (c ^ dc) for dc in (0, 1) for dh in (0, 1)]
-    me = jnp.stack(
-        [z * lay.C + c, unit_rows[0], h * 2 + rest(c, 2), over(c, 2), rest(c, 2), *near]
-    ).astype(jnp.int32)
-
     def exchange(x, dh=0, dl=0, chip=0, core=0):
         pairs = []
         for zz in range(lay.R):
@@ -305,13 +325,16 @@
         functools.partial(pack_kernel, lay),
         [jax.ShapeDtypeStruct((lay.U, lay.pay, CH), BF16)],
         [SM, VM, VM, HB],
+        out_specs=[HB],
         scratch=[
+            pltpu.VMEM((lay.U, lay.pay, CH), BF16),
             pltpu.VMEM(ingest_features.shape, BF16),
             pltpu.VMEM((8, CH), jnp.int32),
             pltpu.SemaphoreType.DMA(()),
+            pltpu.SemaphoreType.DMA((lay.U,)),
         ],
         vmem=PACK_VMEM,
-    )(me, node_map.reshape(1, lay.slots), tile_ids.T, ingest_features)
+    )(unit_rows, node_map.reshape(1, lay.slots), tile_ids.T, ingest_features)
     got = lax.all_to_all(outgoing, ("row", "col"), split_axis=0, concat_axis=0, tiled=True)
 
     _, token = call(seen_kernel, [], [VM], flops=SEEN_FLOPS)(val3)
@@ -320,9 +343,9 @@
         (x, *more), token = call(
             functools.partial(land_kernel, lay, first, many),
             [array(lay.own, many * CH), *extra],
-            [SM, VM],
-            behind=[token],
-        )(me, got)
+            [VM],
+            behind=[token],
+        )(got)
         return [x] + [exchange(x, chip=s) for s in range(1, lay.chips)], more, token
 
     def dense(turned, token):
@@ -331,9 +354,9 @@
         return call(
             functools.partial(dense_kernel, lay, turned),
             [array(*shape)] * 2,
-            [SM] * 2 + [VM] * 4,
-            behind=[token],
-        )(me, ids, *values)
+            [SM] + [VM] * 4,
+            behind=[token],
+        )(ids, *values)
 
     xs, (ids,), token = land(*GATHER[0], token, [array(8, CH, jnp.int32)])
     gathered = [xs]
@@ -343,14 +366,14 @@
         gathered.append(xs)
     own = [xs[0] for xs in gathered]
 
-    def back(n, token):
+    def back(n, token, wait=()):
         first, many = SUMS[n]
         where, lo = inside(GATHER, first, many)
         (mine,), token = call(
             functools.partial(back_kernel, lay.chips, lo, many * CH),
             [array(lay.chip_cols, many * CH)],
             [VM] * (2 + lay.chips),
-            behind=[token],
+            behind=[token, *wait],
             flops=0 if n else FIRST_FLOPS,
         )(at0, at1, *gathered[where])
         return [mine] + [exchange(mine, dl=s) for s in range(1, lay.R2)], token
@@ -391,28 +414,34 @@
         ]
 
     left, parts = [], []
-    sums, token = back(0, token)
+    ready, token = back(0, token)
+    coming, token = back(1, token)
+    (a0, a1), token = dense(False, token)
     for n in range(len(SUMS)):
-        if n == 0:
-            later, token = back(1, token)
-            (a0, a1), token = dense(False, token)
-        part, token = forward(sums, token)
+        following = None
+        if n + 2 < len(SUMS):
+            following, token = back(n + 2, token, ready[1:])
+        part, token = forward(ready, token)
         parts.append(part)
         if n > 0:
             left, token = decode(n - 1, parts[n - 1], left, token, DECODE_FLOPS)
-        sums = later
-        if n + 2 < len(SUMS):
-            later, token = back(n + 2, token)
+        ready, coming = coming, following
     early = deliver(left)
     left, token = decode(len(SUMS) - 1, parts[-1], [], token)
-    _, token = call(seen_kernel, [], [VM] * 3, behind=[token], flops=SEEN_FLOPS)(*early[1:])
-    pieces = early + deliver(left)
-    (out,), _ = call(
-        functools.partial(join_kernel, lay),
-        [array(PIECE, QUARTERS * lay.qw, F32)],
-        [SM] + [VM] * 8,
-        behind=[token],
-    )(me, *pieces)
+    late = deliver(left)
+    out = None
+    for done, pieces in ((0, early), (early[0].shape[1], late)):
+        width = pieces[0].shape[1]
+        (out,), token = call(
+            functools.partial(join_kernel if done else first_join_kernel, lay, done),
+            [array(PIECE, QUARTERS * lay.qw, F32)],
+            [HB] * (1 if done else 0) + [VM] * 4,
+            behind=[token],
+            flops=0 if done else SEEN_FLOPS,
+            out_specs=[HB],
+            scratch=[pltpu.VMEM((4, PIECE, width), F32), pltpu.SemaphoreType.DMA((4,))],
+            aliases={0: 0} if done else None,
+        )(*([out] if done else []), *pieces)
     return out
 
 

time: 107 us -> 105 us (0.981)
  waiting for transfers between devices: 50.7 us -> 48.9 us
    ppermute x27, waiting for transfers between devices: 44.8 us -> 43 us  [exchange(): return lax.ppermute(x, ('row', 'col'), pairs)]
  transfers between devices with their start and end apart: 28 -> 28, of which waited for: 11 -> 11; matrix products, arithmetic and copies ran while one was open for 1% -> 0% of each run, Pallas kernels for 22% -> 22%
where the time goes in v4:
time: 105 us
  waiting for transfers between devices  48.9 us (47%)
  starting transfers between devices  30.1 us (29%)
  Pallas kernels  24.8 us (24%)
    ppermute x27, waiting for transfers between devices, exchange(): return lax.ppermute(x, ('row', 'col'), pairs)  43 us
    ppermute x27, starting transfers between devices, exchange(): return lax.ppermute(x, ('row', 'col'), pairs)  25.3 us
    pallas_call x20, Pallas kernels, apply(): *outs, token = run(*args, *behind)  24.8 us
    all_to_all x1, waiting for transfers between devices, local(): lax.all_to_all(outgoing, ('row', 'col'), split_axis=0, concat_axis=0, til...  5.9 us
    all_to_all x1, starting transfers between devices, local(): lax.all_to_all(outgoing, ('row', 'col'), split_axis=0, concat_axis=0, til...  4.84 us
  transfers between devices with their start and end apart: 28, of which 11 were waited for; matrix products, arithmetic and copies ran while one was open for 0% of the time, Pallas kernels for 22%

profile of v4, /device:TPU:0, one launch (start us, length us, event | category | flops | bytes accessed | tf_op | source)
XLA Modules:
  0.0 104.9 jit_solution(3669035146524617267)
XLA Ops:
  0.0 3.0 %collective-permute-start = (bf16[24,128,128]{2,1,0:T(8,128)(2,1)}, bf16[24,128,128]{2,1,0:T(8,128)(2,1)S(1)}, u32[]{:S(2)}, u32[]{:S(2)}) collective-permute-start(bf16[24,128,128]{2,1,0:T(8,128)(2,1)} %refs_1_.3), channel_id=1, source_target_pairs={{0,8},{1,9},{2,10},{3,11},{4,12},{5,13},{6,14},{7,15},{8,0},{9,1},... | collective-permute-start | bytes 2359304 | tf_op jit(solution)/shard_map/ppermute | solution.py:318
  3.7 3.8 %shard_map.73 = (bf16[32,104,128]{2,1,0:T(8,128)(2,1)}, f32[8,128]{1,0:T(8,128)}) custom-call(s32[1]{0:T(128)S(6)} %copy.10.refs_0_, s32[1,256]{1,0:T(1,128)} %bitcast.2, s32[2,24]{1,0:T(2,128)} %bitcast.3, bf16[256,1536]{1,0:T(8,128)(2,1)} %refs_3_.1), custom_call_target="tpu_custom_call" | custom-call | tf_op jit(solution)/shard_map/pallas_call | solution.py:68
  7.5 4.8 %all-to-all-start = ((bf16[32,104,128]{2,1,0:T(8,128)(2,1)}), bf16[32,104,128]{2,1,0:T(8,128)(2,1)S(1)}, u32[]{:S(2)}, u32[]{:S(2)}) async-start(bf16[32,104,128]{2,1,0:T(8,128)(2,1)} %get-tuple-element.59), calls=%async_computation | async-start | bytes 1703936 | tf_op jit(solution)/shard_map/all_to_all | solution.py:338
  12.3 14.5 %collective-permute-done.refs_2_ = bf16[24,128,128]{2,1,0:T(8,128)(2,1)S(1)} collective-permute-done((bf16[24,128,128]{2,1,0:T(8,128)(2,1)}, bf16[24,128,128]{2,1,0:T(8,128)(2,1)S(1)}, u32[]{:S(2)}, u32[]{:S(2)}) %collective-permute-start) | collective-permute-done | bytes 786464 | tf_op jit(solution)/shard_map/ppermute | solution.py:318
  27.4 2.8 %collective-permute-done.1.refs_0_.refs_4_ = bf16[24,128,128]{2,1,0:T(8,128)(2,1)S(1)} collective-permute-done((bf16[24,128,128]{2,1,0:T(8,128)(2,1)S(1)}, bf16[24,128,128]{2,1,0:T(8,128)(2,1)S(1)}, u32[]{:S(2)}, u32[]{:S(2)}) %collective-permute-start.1) | collective-permute-done | bytes 786464 | tf_op jit(solution)/shard_map/ppermute | solution.py:318
  30.2 5.9 %all-to-all-done.refs_0_ = bf16[32,104,128]{2,1,0:T(8,128)(2,1)S(1)} async-done(((bf16[32,104,128]{2,1,0:T(8,128)(2,1)}), bf16[32,104,128]{2,1,0:T(8,128)(2,1)S(1)}, u32[]{:S(2)}, u32[]{:S(2)}) %all-to-all-start) | async-done | bytes 852000 | tf_op jit(solution)/shard_map/all_to_all | solution.py:338
  36.5 1.6 %collective-permute-start.6 = (bf16[512,128]{1,0:T(8,128)(2,1)S(1)}, bf16[512,128]{1,0:T(8,128)(2,1)S(1)}, u32[]{:S(2)}, u32[]{:S(2)}) collective-permute-start(bf16[512,128]{1,0:T(8,128)(2,1)S(1)} %get-tuple-element.60.refs_2_.refs_1_), channel_id=1, source_target_pairs={{0,2},{1,3},{2,0},{3,1},{4,6},{5,7},{6,4},{7,5},{8,10},{9,11},{10,... | collective-permute-start | bytes 393224 | tf_op jit(solution)/shard_map/ppermute | solution.py:318
  40.1 3.7 %shard_map.76 = (bf16[1024,1152]{1,0:T(8,128)(2,1)S(1)}, bf16[1024,1152]{1,0:T(8,128)(2,1)S(1)}, f32[8,128]{1,0:T(8,128)S(1)}) custom-call(s32[8,128]{1,0:T(8,128)S(1)} %get-tuple-element.61.refs_0_, bf16[24,128,128]{2,1,0:T(8,128)(2,1)S(1)} %copy-done, bf16[24,128,128]{2,1,0:T(8,128)(2,1)S(1)} %collective-permute-done.refs_2_, ...), custom_call_target="tpu_custom_call" | custom-call | tf_op jit(solution)/shard_map/pallas_call | solution.py:68
  44.5 1.6 %collective-permute-start.3 = (bf16[512,256]{1,0:T(8,128)(2,1)S(1)}, bf16[512,256]{1,0:T(8,128)(2,1)S(1)}, u32[]{:S(2)}, u32[]{:S(2)}) collective-permute-start(bf16[512,256]{1,0:T(8,128)(2,1)S(1)} %get-tuple-element.64.refs_2_), channel_id=1, source_target_pairs={{0,2},{1,3},{2,0},{3,1},{4,6},{5,7},{6,4},{7,5},{8,10},{9,11},{10,... | collective-permute-start | bytes 786440 | tf_op jit(solution)/shard_map/ppermute | solution.py:318
  49.3 1.4 %collective-permute-start.10 = (bf16[1024,128]{1,0:T(8,128)(2,1)S(1)}, bf16[1024,128]{1,0:T(8,128)(2,1)S(1)}, u32[]{:S(2)}, u32[]{:S(2)}) collective-permute-start(bf16[1024,128]{1,0:T(8,128)(2,1)S(1)} %get-tuple-element.73.refs_1_), channel_id=1, source_target_pairs={{0,16},{1,17},{2,18},{3,19},{4,20},{5,21},{6,22},{7,23},{8,24},{9,... | collective-permute-start | bytes 786440 | tf_op jit(solution)/shard_map/ppermute | solution.py:318
  50.7 2.9 %collective-permute-done.3.refs_3_ = bf16[512,256]{1,0:T(8,128)(2,1)S(1)} collective-permute-done((bf16[512,256]{1,0:T(8,128)(2,1)S(1)}, bf16[512,256]{1,0:T(8,128)(2,1)S(1)}, u32[]{:S(2)}, u32[]{:S(2)}) %collective-permute-start.3) | collective-permute-done | bytes 262176 | tf_op jit(solution)/shard_map/ppermute | solution.py:318
  53.5 6.1 %collective-permute-done.4.refs_4_ = bf16[512,256]{1,0:T(8,128)(2,1)S(1)} collective-permute-done((bf16[512,256]{1,0:T(8,128)(2,1)S(1)}, bf16[512,256]{1,0:T(8,128)(2,1)S(1)}, u32[]{:S(2)}, u32[]{:S(2)}) %collective-permute-start.4) | collective-permute-done | bytes 262176 | tf_op jit(solution)/shard_map/ppermute | solution.py:318
  61.4 2.7 %shard_map.80 = (bf16[1152,1024]{1,0:T(8,128)(2,1)S(1)}, bf16[1152,1024]{1,0:T(8,128)(2,1)S(1)}, f32[8,128]{1,0:T(8,128)S(1)}) custom-call(s32[8,128]{1,0:T(8,128)S(1)} %get-tuple-element.61.refs_0_, bf16[24,128,128]{2,1,0:T(8,128)(2,1)S(1)} %copy-done, bf16[24,128,128]{2,1,0:T(8,128)(2,1)S(1)} %collective-permute-done.refs_2_, ...), custom_call_target="tpu_custom_call" | custom-call | tf_op jit(solution)/shard_map/pallas_call | solution.py:68
  64.2 5.1 %collective-permute-done.10.refs_7_.refs_2_ = bf16[1024,128]{1,0:T(8,128)(2,1)S(1)} collective-permute-done((bf16[1024,128]{1,0:T(8,128)(2,1)S(1)}, bf16[1024,128]{1,0:T(8,128)(2,1)S(1)}, u32[]{:S(2)}, u32[]{:S(2)}) %collective-permute-start.10) | collective-permute-done | bytes 262176 | tf_op jit(solution)/shard_map/ppermute | solution.py:318
  70.6 1.3 %shard_map.82 = (bf16[1024,128]{1,0:T(8,128)(2,1)S(1)}, bf16[512,128]{1,0:T(8,128)(2,1)S(1)}, bf16[512,128]{1,0:T(8,128)(2,1)S(1)}, bf16[512,128]{1,0:T(8,128)(2,1)S(1)}, f32[8,128]{1,0:T(8,128)S(1)}) custom-call(bf16[128,128]{1,0:T(8,128)(2,1)S(1)} %copy-done.1, bf16[1024,128]{1,0:T(8,128)(2,1)S(1)} %get-tuple-element.73.refs_1_, ...), custom_call_target="tpu_custom_call" | custom-call | tf_op jit(solution)/shard_map/pallas_call | solution.py:68
  72.4 1.4 %collective-permute-start.15 = (bf16[512,128]{1,0:T(8,128)(2,1)S(1)}, bf16[512,128]{1,0:T(8,128)(2,1)S(1)}, u32[]{:S(2)}, u32[]{:S(2)}) collective-permute-start(bf16[512,128]{1,0:T(8,128)(2,1)S(1)} %get-tuple-element.86), channel_id=1, source_target_pairs={{0,4},{1,5},{2,6},{3,7},{4,0},{5,1},{6,2},{7,3},{8,12},{9,13},{10,... | collective-permute-start | bytes 393224 | tf_op jit(solution)/shard_map/ppermute | solution.py:318
  73.8 1.6 %collective-permute-start.16 = (bf16[512,128]{1,0:T(8,128)(2,1)S(1)}, bf16[512,128]{1,0:T(8,128)(2,1)S(1)}, u32[]{:S(2)}, u32[]{:S(2)}) collective-permute-start(bf16[512,128]{1,0:T(8,128)(2,1)S(1)} %get-tuple-element.87), channel_id=1, source_target_pairs={{0,6},{1,7},{2,4},{3,5},{4,2},{5,3},{6,0},{7,1},{8,14},{9,15},{10,... | collective-permute-start | bytes 393224 | tf_op jit(solution)/shard_map/ppermute | solution.py:318
  76.4 1.3 %shard_map.83 = (bf16[1024,128]{1,0:T(8,128)(2,1)S(1)}, bf16[512,128]{1,0:T(8,128)(2,1)S(1)}, bf16[512,128]{1,0:T(8,128)(2,1)S(1)}, bf16[512,128]{1,0:T(8,128)(2,1)S(1)}, f32[8,128]{1,0:T(8,128)S(1)}) custom-call(bf16[128,128]{1,0:T(8,128)(2,1)S(1)} %copy-done.1, bf16[1024,128]{1,0:T(8,128)(2,1)S(1)} %get-tuple-element.72.refs_1_, ...), custom_call_target="tpu_custom_call" | custom-call | tf_op jit(solution)/shard_map/pallas_call | solution.py:68
  79.2 1.4 %collective-permute-start.12 = (bf16[512,128]{1,0:T(8,128)(2,1)S(1)}, bf16[512,128]{1,0:T(8,128)(2,1)S(1)}, u32[]{:S(2)}, u32[]{:S(2)}) collective-permute-start(bf16[512,128]{1,0:T(8,128)(2,1)S(1)} %get-tuple-element.81), channel_id=1, source_target_pairs={{0,4},{1,5},{2,6},{3,7},{4,0},{5,1},{6,2},{7,3},{8,12},{9,13},{10,... | collective-permute-start | bytes 393224 | tf_op jit(solution)/shard_map/ppermute | solution.py:318
  80.6 1.6 %collective-permute-start.13 = (bf16[512,128]{1,0:T(8,128)(2,1)S(1)}, bf16[512,128]{1,0:T(8,128)(2,1)S(1)}, u32[]{:S(2)}, u32[]{:S(2)}) collective-permute-start(bf16[512,128]{1,0:T(8,128)(2,1)S(1)} %get-tuple-element.82), channel_id=1, source_target_pairs={{0,6},{1,7},{2,4},{3,5},{4,2},{5,3},{6,0},{7,1},{8,14},{9,15},{10,... | collective-permute-start | bytes 393224 | tf_op jit(solution)/shard_map/ppermute | solution.py:318
  82.4 6.1 %collective-permute-done.17.refs_2_ = bf16[1024,128]{1,0:T(8,128)(2,1)S(1)} collective-permute-done((bf16[1024,128]{1,0:T(8,128)(2,1)S(1)}, bf16[1024,128]{1,0:T(8,128)(2,1)S(1)}, u32[]{:S(2)}, u32[]{:S(2)}) %collective-permute-start.17) | collective-permute-done | bytes 262176 | tf_op jit(solution)/shard_map/ppermute | solution.py:318
  90.8 2.6 %collective-permute-start.23 = (bf16[512,128]{1,0:T(8,128)(2,1)S(1)}, bf16[512,128]{1,0:T(8,128)(2,1)S(1)}, u32[]{:S(2)}, u32[]{:S(2)}) collective-permute-start(bf16[512,128]{1,0:T(8,128)(2,1)S(1)} %get-tuple-element.103), channel_id=1, source_target_pairs={{0,6},{1,7},{2,4},{3,5},{4,2},{5,3},{6,0},{7,1},{8,14},{9,15},{10,... | collective-permute-start | bytes 393224 | tf_op jit(solution)/shard_map/ppermute | solution.py:318
  93.9 2.4 %collective-permute-done.21.refs_4_ = bf16[512,128]{1,0:T(8,128)(2,1)S(1)} collective-permute-done((bf16[512,128]{1,0:T(8,128)(2,1)S(1)}, bf16[512,128]{1,0:T(8,128)(2,1)S(1)}, u32[]{:S(2)}, u32[]{:S(2)}) %collective-permute-start.21) | collective-permute-done | bytes 131104 | tf_op jit(solution)/shard_map/ppermute | solution.py:318
  103.4 1.3 %shard_map.92 = (f32[128,1536]{1,0:T(8,128)}, f32[8,128]{1,0:T(8,128)}) custom-call(f32[128,1536]{1,0:T(8,128)} %get-tuple-element.106.refs_0_, f32[128,128]{1,0:T(8,128)S(1)} %get-tuple-element.107.refs_1_, bf16[128,128]{1,0:T(8,128)(2,1)S(1)} %collective-permute-done.24.refs_2_, ...), custom_call_target="tpu_custom_call", output_to_operand_aliasing={{0}: (0, {})} | custom-call | tf_op jit(solution)/shard_map/pallas_call | solution.py:68
  (58 shorter events, 23.0 us)
Async XLA Ops:
  0.0 26.8 %collective-permute-start = (bf16[24,128,128]{2,1,0:T(8,128)(2,1)}, bf16[24,128,128]{2,1,0:T(8,128)(2,1)S(1)}, u32[]{:S(2)}, u32[]{:S(2)}) collective-permute-start(bf16[24,128,128]{2,1,0:T(8,128)(2,1)} %refs_1_.3), channel_id=1, source_target_pairs={{0,8},{1,9},{2,10},{3,11},{4,12},{5,13},{6,14},{7,15},{8,0},{9,1},... | collective-permute-start | bytes 2359304 | tf_op jit(solution)/shard_map/ppermute | solution.py:318
  7.5 28.6 %all-to-all-start = ((bf16[32,104,128]{2,1,0:T(8,128)(2,1)}), bf16[32,104,128]{2,1,0:T(8,128)(2,1)S(1)}, u32[]{:S(2)}, u32[]{:S(2)}) async-start(bf16[32,104,128]{2,1,0:T(8,128)(2,1)} %get-tuple-element.59), calls=%async_computation | async-start | bytes 1703936 | tf_op jit(solution)/shard_map/all_to_all | solution.py:338
  26.8 13.2 %collective-permute-start.2 = (bf16[24,128,128]{2,1,0:T(8,128)(2,1)S(1)}, bf16[24,128,128]{2,1,0:T(8,128)(2,1)}, u32[]{:S(2)}, u32[]{:S(2)}) collective-permute-start(bf16[24,128,128]{2,1,0:T(8,128)(2,1)S(1)} %copy-done), channel_id=1, source_target_pairs={{0,1},{1,0},{2,3},{3,2},{4,5},{5,4},{6,7},{7,6},{8,9},{9,8},{10,11... | collective-permute-start | bytes 2359304 | tf_op jit(solution)/shard_map/ppermute | solution.py:318
  36.5 10.7 %collective-permute-start.6 = (bf16[512,128]{1,0:T(8,128)(2,1)S(1)}, bf16[512,128]{1,0:T(8,128)(2,1)S(1)}, u32[]{:S(2)}, u32[]{:S(2)}) collective-permute-start(bf16[512,128]{1,0:T(8,128)(2,1)S(1)} %get-tuple-element.60.refs_2_.refs_1_), channel_id=1, source_target_pairs={{0,2},{1,3},{2,0},{3,1},{4,6},{5,7},{6,4},{7,5},{8,10},{9,11},{10,... | collective-permute-start | bytes 393224 | tf_op jit(solution)/shard_map/ppermute | solution.py:318
  38.1 10.0 %collective-permute-start.7 = (bf16[512,128]{1,0:T(8,128)(2,1)S(1)}, bf16[512,128]{1,0:T(8,128)(2,1)S(1)}, u32[]{:S(2)}, u32[]{:S(2)}) collective-permute-start(bf16[512,128]{1,0:T(8,128)(2,1)S(1)} %get-tuple-element.60.refs_2_.refs_1_), channel_id=1, source_target_pairs={{0,4},{1,5},{2,6},{3,7},{4,0},{5,1},{6,2},{7,3},{8,12},{9,13},{10,... | collective-permute-start | bytes 393224 | tf_op jit(solution)/shard_map/ppermute | solution.py:318
  39.3 8.7 %collective-permute-start.8 = (bf16[512,128]{1,0:T(8,128)(2,1)S(1)}, bf16[512,128]{1,0:T(8,128)(2,1)S(1)}, u32[]{:S(2)}, u32[]{:S(2)}) collective-permute-start(bf16[512,128]{1,0:T(8,128)(2,1)S(1)} %get-tuple-element.60.refs_2_.refs_1_), channel_id=1, source_target_pairs={{0,6},{1,7},{2,4},{3,5},{4,2},{5,3},{6,0},{7,1},{8,14},{9,15},{10,... | collective-permute-start | bytes 393224 | tf_op jit(solution)/shard_map/ppermute | solution.py:318
  44.5 9.1 %collective-permute-start.3 = (bf16[512,256]{1,0:T(8,128)(2,1)S(1)}, bf16[512,256]{1,0:T(8,128)(2,1)S(1)}, u32[]{:S(2)}, u32[]{:S(2)}) collective-permute-start(bf16[512,256]{1,0:T(8,128)(2,1)S(1)} %get-tuple-element.64.refs_2_), channel_id=1, source_target_pairs={{0,2},{1,3},{2,0},{3,1},{4,6},{5,7},{6,4},{7,5},{8,10},{9,11},{10,... | collective-permute-start | bytes 786440 | tf_op jit(solution)/shard_map/ppermute | solution.py:318
  46.0 13.6 %collective-permute-start.4 = (bf16[512,256]{1,0:T(8,128)(2,1)S(1)}, bf16[512,256]{1,0:T(8,128)(2,1)S(1)}, u32[]{:S(2)}, u32[]{:S(2)}) collective-permute-start(bf16[512,256]{1,0:T(8,128)(2,1)S(1)} %get-tuple-element.64.refs_2_), channel_id=1, source_target_pairs={{0,4},{1,5},{2,6},{3,7},{4,0},{5,1},{6,2},{7,3},{8,12},{9,13},{10,... | collective-permute-start | bytes 786440 | tf_op jit(solution)/shard_map/ppermute | solution.py:318
  47.3 12.3 %collective-permute-start.5 = (bf16[512,256]{1,0:T(8,128)(2,1)S(1)}, bf16[512,256]{1,0:T(8,128)(2,1)S(1)}, u32[]{:S(2)}, u32[]{:S(2)}) collective-permute-start(bf16[512,256]{1,0:T(8,128)(2,1)S(1)} %get-tuple-element.64.refs_2_), channel_id=1, source_target_pairs={{0,6},{1,7},{2,4},{3,5},{4,2},{5,3},{6,0},{7,1},{8,14},{9,15},{10,... | collective-permute-start | bytes 786440 | tf_op jit(solution)/shard_map/ppermute | solution.py:318
  49.3 20.0 %collective-permute-start.10 = (bf16[1024,128]{1,0:T(8,128)(2,1)S(1)}, bf16[1024,128]{1,0:T(8,128)(2,1)S(1)}, u32[]{:S(2)}, u32[]{:S(2)}) collective-permute-start(bf16[1024,128]{1,0:T(8,128)(2,1)S(1)} %get-tuple-element.73.refs_1_), channel_id=1, source_target_pairs={{0,16},{1,17},{2,18},{3,19},{4,20},{5,21},{6,22},{7,23},{8,24},{9,... | collective-permute-start | bytes 786440 | tf_op jit(solution)/shard_map/ppermute | solution.py:318
  60.9 15.5 %collective-permute-start.9 = (bf16[1024,128]{1,0:T(8,128)(2,1)S(1)}, bf16[1024,128]{1,0:T(8,128)(2,1)S(1)}, u32[]{:S(2)}, u32[]{:S(2)}) collective-permute-start(bf16[1024,128]{1,0:T(8,128)(2,1)S(1)} %get-tuple-element.72.refs_1_), channel_id=1, source_target_pairs={{0,16},{1,17},{2,18},{3,19},{4,20},{5,21},{6,22},{7,23},{8,24},{9,... | collective-permute-start | bytes 786440 | tf_op jit(solution)/shard_map/ppermute | solution.py:318
  71.9 7.3 %collective-permute-start.14 = (bf16[512,128]{1,0:T(8,128)(2,1)S(1)}, bf16[512,128]{1,0:T(8,128)(2,1)S(1)}, u32[]{:S(2)}, u32[]{:S(2)}) collective-permute-start(bf16[512,128]{1,0:T(8,128)(2,1)S(1)} %get-tuple-element.85), channel_id=1, source_target_pairs={{0,2},{1,3},{2,0},{3,1},{4,6},{5,7},{6,4},{7,5},{8,10},{9,11},{10,... | collective-permute-start | bytes 393224 | tf_op jit(solution)/shard_map/ppermute | solution.py:318
  72.4 8.1 %collective-permute-start.15 = (bf16[512,128]{1,0:T(8,128)(2,1)S(1)}, bf16[512,128]{1,0:T(8,128)(2,1)S(1)}, u32[]{:S(2)}, u32[]{:S(2)}) collective-permute-start(bf16[512,128]{1,0:T(8,128)(2,1)S(1)} %get-tuple-element.86), channel_id=1, source_target_pairs={{0,4},{1,5},{2,6},{3,7},{4,0},{5,1},{6,2},{7,3},{8,12},{9,13},{10,... | collective-permute-start | bytes 393224 | tf_op jit(solution)/shard_map/ppermute | solution.py:318
  73.8 8.3 %collective-permute-start.16 = (bf16[512,128]{1,0:T(8,128)(2,1)S(1)}, bf16[512,128]{1,0:T(8,128)(2,1)S(1)}, u32[]{:S(2)}, u32[]{:S(2)}) collective-permute-start(bf16[512,128]{1,0:T(8,128)(2,1)S(1)} %get-tuple-element.87), channel_id=1, source_target_pairs={{0,6},{1,7},{2,4},{3,5},{4,2},{5,3},{6,0},{7,1},{8,14},{9,15},{10,... | collective-permute-start | bytes 393224 | tf_op jit(solution)/shard_map/ppermute | solution.py:318
  75.4 13.2 %collective-permute-start.17 = (bf16[1024,128]{1,0:T(8,128)(2,1)S(1)}, bf16[1024,128]{1,0:T(8,128)(2,1)S(1)}, u32[]{:S(2)}, u32[]{:S(2)}) collective-permute-start(bf16[1024,128]{1,0:T(8,128)(2,1)S(1)} %get-tuple-element.92.refs_1_), channel_id=1, source_target_pairs={{0,16},{1,17},{2,18},{3,19},{4,20},{5,21},{6,22},{7,23},{8,24},{9,... | collective-permute-start | bytes 786440 | tf_op jit(solution)/shard_map/ppermute | solution.py:318
  77.7 13.1 %collective-permute-start.11 = (bf16[512,128]{1,0:T(8,128)(2,1)S(1)}, bf16[512,128]{1,0:T(8,128)(2,1)S(1)}, u32[]{:S(2)}, u32[]{:S(2)}) collective-permute-start(bf16[512,128]{1,0:T(8,128)(2,1)S(1)} %get-tuple-element.80), channel_id=1, source_target_pairs={{0,2},{1,3},{2,0},{3,1},{4,6},{5,7},{6,4},{7,5},{8,10},{9,11},{10,... | collective-permute-start | bytes 393224 | tf_op jit(solution)/shard_map/ppermute | solution.py:318
  79.2 14.2 %collective-permute-start.12 = (bf16[512,128]{1,0:T(8,128)(2,1)S(1)}, bf16[512,128]{1,0:T(8,128)(2,1)S(1)}, u32[]{:S(2)}, u32[]{:S(2)}) collective-permute-start(bf16[512,128]{1,0:T(8,128)(2,1)S(1)} %get-tuple-element.81), channel_id=1, source_target_pairs={{0,4},{1,5},{2,6},{3,7},{4,0},{5,1},{6,2},{7,3},{8,12},{9,13},{10,... | collective-permute-start | bytes 393224 | tf_op jit(solution)/shard_map/ppermute | solution.py:318
  80.6 12.9 %collective-permute-start.13 = (bf16[512,128]{1,0:T(8,128)(2,1)S(1)}, bf16[512,128]{1,0:T(8,128)(2,1)S(1)}, u32[]{:S(2)}, u32[]{:S(2)}) collective-permute-start(bf16[512,128]{1,0:T(8,128)(2,1)S(1)} %get-tuple-element.82), channel_id=1, source_target_pairs={{0,6},{1,7},{2,4},{3,5},{4,2},{5,3},{6,0},{7,1},{8,14},{9,15},{10,... | collective-permute-start | bytes 393224 | tf_op jit(solution)/shard_map/ppermute | solution.py:318
  89.9 6.4 %collective-permute-start.21 = (bf16[512,128]{1,0:T(8,128)(2,1)S(1)}, bf16[512,128]{1,0:T(8,128)(2,1)S(1)}, u32[]{:S(2)}, u32[]{:S(2)}) collective-permute-start(bf16[512,128]{1,0:T(8,128)(2,1)S(1)} %get-tuple-element.101), channel_id=1, source_target_pairs={{0,2},{1,3},{2,0},{3,1},{4,6},{5,7},{6,4},{7,5},{8,10},{9,11},{10,... | collective-permute-start | bytes 393224 | tf_op jit(solution)/shard_map/ppermute | solution.py:318
  90.3 7.9 %collective-permute-start.22 = (bf16[512,128]{1,0:T(8,128)(2,1)S(1)}, bf16[512,128]{1,0:T(8,128)(2,1)S(1)}, u32[]{:S(2)}, u32[]{:S(2)}) collective-permute-start(bf16[512,128]{1,0:T(8,128)(2,1)S(1)} %get-tuple-element.102), channel_id=1, source_target_pairs={{0,4},{1,5},{2,6},{3,7},{4,0},{5,1},{6,2},{7,3},{8,12},{9,13},{10,... | collective-permute-start | bytes 393224 | tf_op jit(solution)/shard_map/ppermute | solution.py:318
  90.8 7.5 %collective-permute-start.23 = (bf16[512,128]{1,0:T(8,128)(2,1)S(1)}, bf16[512,128]{1,0:T(8,128)(2,1)S(1)}, u32[]{:S(2)}, u32[]{:S(2)}) collective-permute-start(bf16[512,128]{1,0:T(8,128)(2,1)S(1)} %get-tuple-element.103), channel_id=1, source_target_pairs={{0,6},{1,7},{2,4},{3,5},{4,2},{5,3},{6,0},{7,1},{8,14},{9,15},{10,... | collective-permute-start | bytes 393224 | tf_op jit(solution)/shard_map/ppermute | solution.py:318
  93.7 6.0 %collective-permute-start.18 = (bf16[128,256]{1,0:T(8,128)(2,1)S(1)}, bf16[128,256]{1,0:T(8,128)(2,1)S(1)}, u32[]{:S(2)}, u32[]{:S(2)}) collective-permute-start(bf16[128,256]{1,0:T(8,128)(2,1)S(1)} %get-tuple-element.96), channel_id=1, source_target_pairs={{0,1},{1,0},{2,3},{3,2},{4,5},{5,4},{6,7},{7,6},{8,9},{9,8},{10,11... | collective-permute-start | bytes 196616 | tf_op jit(solution)/shard_map/ppermute | solution.py:318
  93.8 6.7 %collective-permute-start.19 = (bf16[128,256]{1,0:T(8,128)(2,1)S(1)}, bf16[128,256]{1,0:T(8,128)(2,1)S(1)}, u32[]{:S(2)}, u32[]{:S(2)}) collective-permute-start(bf16[128,256]{1,0:T(8,128)(2,1)S(1)} %get-tuple-element.97), channel_id=1, source_target_pairs={{0,8},{1,9},{2,10},{3,11},{4,12},{5,13},{6,14},{7,15},{8,0},{9,1},... | collective-permute-start | bytes 196616 | tf_op jit(solution)/shard_map/ppermute | solution.py:318
  96.3 4.2 %collective-permute-start.20 = (bf16[128,256]{1,0:T(8,128)(2,1)S(1)}, bf16[128,256]{1,0:T(8,128)(2,1)S(1)}, u32[]{:S(2)}, u32[]{:S(2)}) collective-permute-start(bf16[128,256]{1,0:T(8,128)(2,1)S(1)} %get-tuple-element.98), channel_id=1, source_target_pairs={{0,9},{1,8},{2,11},{3,10},{4,13},{5,12},{6,15},{7,14},{8,1},{9,0},... | collective-permute-start | bytes 196616 | tf_op jit(solution)/shard_map/ppermute | solution.py:318
  (7 other events, 45.8 us)

commit v5 on v4

--- a/solution.py
+++ b/solution.py
@@ -98,11 +98,17 @@
         return l * 2 + h
 
 
-def pack_kernel(lay, held, node, tiles, feats_far, out_far, out, feats, ids, arrived, gone):
-    unit, count = Here(lay).unit, held[0]
+def pack_kernel(lay, held_far, node_far, tiles_far, feats_far, out_far, out, feats, ids, held, node, tiles, arrived, gone):
+    unit = Here(lay).unit
     n = lay.slots
-    bring = pltpu.make_async_copy(feats_far, feats, arrived)
-    bring.start()
+    pairs = ((held_far, held), (node_far, node), (tiles_far, tiles), (feats_far, feats))
+    first = [pltpu.make_async_copy(a, b, arrived.at[i]) for i, (a, b) in enumerate(pairs)]
+    for copy in first:
+        copy.start()
+    bring = first.pop()
+    for copy in first:
+        copy.wait()
+    count = held[0]
     ids[...] = jnp.zeros_like(ids)
     ids[1:3, 0 : tiles.shape[1]] = tiles[...]
     row = node[...]
@@ -186,15 +192,24 @@
             ids[2 * i : 2 * i + 2, :] = found[1:3, :].astype(jnp.int32)
 
 
-def dense_kernel(lay, turned, ids, v0, v1, v2, v3, near, far):
+def dense_kernel(lay, turned, ids, far0, far2, v1, w1, v3, w3, near, far, v0, v2, arrived):
     here = Here(lay)
+    fetch = [
+        pltpu.make_async_copy(a, b, arrived.at[i]) for i, (a, b) in enumerate(((far0, v0), (far2, v2)))
+    ]
+    for copy in fetch:
+        copy.start()
     near[...] = jnp.zeros_like(near)
     far[...] = jnp.zeros_like(far)
     spare = 2 * lay.chips
-    for i, (values, to) in enumerate(((v0, near), (v1, far), (v2, near), (v3, far))):
-
-        def body(t, carry, i=i, values=values, to=to):
-            rt, ct = ids[2 * i, t], ids[2 * i + 1, t]
+    cut = v1.shape[0]
+    sets = ((1, 0, v1, far), (3, 0, v3, far), (0, 0, v0, near), (2, 0, v2, near), (1, cut, w1, far), (3, cut, w3, far))
+    for i, skip, values, to in sets:
+        if i % 2 == 0:
+            fetch[i // 2].wait()
+
+        def body(t, carry, i=i, skip=skip, values=values, to=to):
+            rt, ct = ids[2 * i, skip + t], ids[2 * i + 1, skip + t]
             c = rest(rt, lay.C)
             r = (over(c, 2) ^ here.chip) * 2 + (rest(c, 2) ^ here.core)
             k = rest(over(ct, lay.R), 2) * lay.R + rest(ct, lay.R)
@@ -207,7 +222,7 @@
                 to[rr, kk] = values[t]
             return carry
 
-        lax.fori_loop(0, values.shape[0], body, 0, unroll=4)
+        lax.fori_loop(0, values.shape[0], body, 0, unroll=min(4, values.shape[0]))
 
 
 def seen_kernel(*refs):
@@ -294,8 +309,9 @@
 GATHER = ((0, 1), (1, 2))
 SUMS = ((0, 1), (1, 1), (2, 1))
 BLOCK = 256
+AHEAD = 5
 PACK_VMEM = 58 * 1024 * 1024
-SEEN_FLOPS = 3_000_000_000
+SEEN_FLOPS = 7_500_000_000
 FIRST_FLOPS = 5_000_000_000
 DECODE_FLOPS = 3_000_000_000
 
@@ -317,27 +333,32 @@
                 pairs.append((zz * lay.C + cc, to))
         return lax.ppermute(x, ("row", "col"), pairs)
 
-    val1, val2 = exchange(tile_values, dh=1), exchange(tile_values, core=1)
-    val3 = exchange(val1, core=1)
-    values = (tile_values, val1, val2, val3)
+    cut = tile_values.shape[0] * AHEAD // 8
+    val1 = [exchange(x, dh=1) for x in (tile_values[:cut], tile_values[cut:])]
+    val2 = exchange(tile_values, core=1)
+    val3 = [exchange(x, core=1) for x in val1]
+    values = (tile_values, val2, *val1, *val3)
 
     (outgoing,), _ = call(
         functools.partial(pack_kernel, lay),
         [jax.ShapeDtypeStruct((lay.U, lay.pay, CH), BF16)],
-        [SM, VM, VM, HB],
+        [HB] * 4,
         out_specs=[HB],
         scratch=[
             pltpu.VMEM((lay.U, lay.pay, CH), BF16),
             pltpu.VMEM(ingest_features.shape, BF16),
             pltpu.VMEM((8, CH), jnp.int32),
-            pltpu.SemaphoreType.DMA(()),
+            pltpu.SMEM((1,), jnp.int32),
+            pltpu.VMEM((1, lay.slots), jnp.int32),
+            pltpu.VMEM(tile_ids.shape[::-1], jnp.int32),
+            pltpu.SemaphoreType.DMA((4,)),
             pltpu.SemaphoreType.DMA((lay.U,)),
         ],
         vmem=PACK_VMEM,
     )(unit_rows, node_map.reshape(1, lay.slots), tile_ids.T, ingest_features)
     got = lax.all_to_all(outgoing, ("row", "col"), split_axis=0, concat_axis=0, tiled=True)
 
-    _, token = call(seen_kernel, [], [VM], flops=SEEN_FLOPS)(val3)
+    _, token = call(seen_kernel, [], [VM], flops=SEEN_FLOPS)(val3[0])
 
     def land(first, many, token, extra=()):
         (x, *more), token = call(
@@ -354,8 +375,9 @@
         return call(
             functools.partial(dense_kernel, lay, turned),
             [array(*shape)] * 2,
-            [SM] + [VM] * 4,
-            behind=[token],
+            [SM, HB, HB, VM, VM, VM, VM],
+            behind=[token],
+            scratch=[pltpu.VMEM(tile_values.shape, BF16)] * 2 + [pltpu.SemaphoreType.DMA((2,))],
         )(ids, *values)
 
     xs, (ids,), token = land(*GATHER[0], token, [array(8, CH, jnp.int32)])

time: 105 us -> 103 us (0.981)
  waiting for transfers between devices: 48.9 us -> 36.4 us
  starting transfers between devices: 30.1 us -> 39.6 us
  local copies, waits for them, and re-layouts: 0.01 us -> 1.17 us
    ppermute x27 -> x29, starting transfers between devices: 25.3 us -> 34.8 us  [exchange(): return lax.ppermute(x, ('row', 'col'), pairs)]
    ppermute x27 -> x29, waiting for transfers between devices: 43 us -> 36.4 us  [exchange(): return lax.ppermute(x, ('row', 'col'), pairs)]
    all_to_all x1, waiting for transfers between devices: 5.9 us -> 0.01 us  [local(): lax.all_to_all(outgoing, ('row', 'col'), split_axis=0, concat_axis=0, til...]
    slice x0 -> x2, local copies, waits for them, and re-layouts: none -> 1.16 us  [local(): val1 = [exchange(x, dh=1) for x in (tile_values[:cut], tile_values[cut:])]]
  transfers between devices with their start and end apart: 28 -> 30, of which waited for: 11 -> 8; matrix products, arithmetic and copies ran while one was open for 0% -> 0% of each run, Pallas kernels for 22% -> 23%
where the time goes in v5:
time: 103 us
  starting transfers between devices  39.6 us (38%)
  waiting for transfers between devices  36.4 us (35%)
  Pallas kernels  24.6 us (24%)
  local copies, waits for them, and re-layouts  1.17 us (1%)
    ppermute x29, waiting for transfers between devices, exchange(): return lax.ppermute(x, ('row', 'col'), pairs)  36.4 us
    ppermute x29, starting transfers between devices, exchange(): return lax.ppermute(x, ('row', 'col'), pairs)  34.8 us
    pallas_call x20, Pallas kernels, apply(): *outs, token = run(*args, *behind)  24.6 us
    all_to_all x1, starting transfers between devices, local(): lax.all_to_all(outgoing, ('row', 'col'), split_axis=0, concat_axis=0, til...  4.84 us
  transfers between devices with their start and end apart: 30, of which 8 were waited for; matrix products, arithmetic and copies ran while one was open for 0% of the time, Pallas kernels for 23%

profile of v5, /device:TPU:0, one launch (start us, length us, event | category | flops | bytes accessed | tf_op | source)
XLA Modules:
  0.0 102.9 jit_solution(3568078384712750399)
XLA Ops:
  1.1 3.1 %collective-permute-start = (bf16[15,128,128]{2,1,0:T(8,128)(2,1)S(1)}, bf16[15,128,128]{2,1,0:T(8,128)(2,1)S(1)}, u32[]{:S(2)}, u32[]{:S(2)}) collective-permute-start(bf16[15,128,128]{2,1,0:T(8,128)(2,1)S(1)} %slice.6), channel_id=1, source_target_pairs={{0,8},{1,9},{2,10},{3,11},{4,12},{5,13},{6,14},{7,15},{8,0},{9,1},... | collective-permute-start | bytes 1474568 | tf_op jit(solution)/shard_map/ppermute | solution.py:334
  4.9 3.2 %shard_map.73 = (bf16[32,104,128]{2,1,0:T(8,128)(2,1)}, f32[8,128]{1,0:T(8,128)}) custom-call(s32[1]{0:T(128)S(6)} %copy.10.refs_0_, s32[1,256]{1,0:T(1,128)} %bitcast.2, s32[2,24]{1,0:T(2,128)} %bitcast.3, bf16[256,1536]{1,0:T(8,128)(2,1)} %refs_3_.1), custom_call_target="tpu_custom_call" | custom-call | tf_op jit(solution)/shard_map/pallas_call | solution.py:68
  8.1 4.8 %all-to-all-start = ((bf16[32,104,128]{2,1,0:T(8,128)(2,1)}), bf16[32,104,128]{2,1,0:T(8,128)(2,1)S(1)}, u32[]{:S(2)}, u32[]{:S(2)}) async-start(bf16[32,104,128]{2,1,0:T(8,128)(2,1)} %get-tuple-element.59), calls=%async_computation | async-start | bytes 1703936 | tf_op jit(solution)/shard_map/all_to_all | solution.py:359
  12.9 2.8 %collective-permute-done.refs_3_ = bf16[15,128,128]{2,1,0:T(8,128)(2,1)S(1)} collective-permute-done((bf16[15,128,128]{2,1,0:T(8,128)(2,1)S(1)}, bf16[15,128,128]{2,1,0:T(8,128)(2,1)S(1)}, u32[]{:S(2)}, u32[]{:S(2)}) %collective-permute-start) | collective-permute-done | bytes 491552 | tf_op jit(solution)/shard_map/ppermute | solution.py:334
  15.7 2.5 %collective-permute-start.3 = (bf16[9,128,128]{2,1,0:T(8,128)(2,1)S(1)}, bf16[9,128,128]{2,1,0:T(8,128)(2,1)}, u32[]{:S(2)}, u32[]{:S(2)}) collective-permute-start(bf16[9,128,128]{2,1,0:T(8,128)(2,1)S(1)} %slice.7), channel_id=1, source_target_pairs={{0,8},{1,9},{2,10},{3,11},{4,12},{5,13},{6,14},{7,15},{8,0},{9,1},... | collective-permute-start | bytes 884744 | tf_op jit(solution)/shard_map/ppermute | solution.py:334
  18.5 17.4 %collective-permute-done.3.refs_4_ = bf16[9,128,128]{2,1,0:T(8,128)(2,1)} collective-permute-done((bf16[9,128,128]{2,1,0:T(8,128)(2,1)S(1)}, bf16[9,128,128]{2,1,0:T(8,128)(2,1)}, u32[]{:S(2)}, u32[]{:S(2)}) %collective-permute-start.3) | collective-permute-done | bytes 294944 | tf_op jit(solution)/shard_map/ppermute | solution.py:334
  36.4 2.5 %collective-permute-start.10 = (bf16[512,128]{1,0:T(8,128)(2,1)S(1)}, bf16[512,128]{1,0:T(8,128)(2,1)S(1)}, u32[]{:S(2)}, u32[]{:S(2)}) collective-permute-start(bf16[512,128]{1,0:T(8,128)(2,1)S(1)} %get-tuple-element.60.refs_2_.refs_1_), channel_id=1, source_target_pairs={{0,6},{1,7},{2,4},{3,5},{4,2},{5,3},{6,0},{7,1},{8,14},{9,15},{10,... | collective-permute-start | bytes 393224 | tf_op jit(solution)/shard_map/ppermute | solution.py:334
  39.9 4.1 %shard_map.76 = (bf16[1024,1152]{1,0:T(8,128)(2,1)S(1)}, bf16[1024,1152]{1,0:T(8,128)(2,1)S(1)}, f32[8,128]{1,0:T(8,128)S(1)}) custom-call(s32[8,128]{1,0:T(8,128)S(1)} %get-tuple-element.61.refs_0_, bf16[24,128,128]{2,1,0:T(8,128)(2,1)S(1)} %copy-done, bf16[24,128,128]{2,1,0:T(8,128)(2,1)S(1)} %collective-permute-done.2.refs_2_, ...), custom_call_target="tpu_custom_call" | custom-call | tf_op jit(solution)/shard_map/pallas_call | solution.py:68
  44.7 1.5 %collective-permute-start.5 = (bf16[512,256]{1,0:T(8,128)(2,1)S(1)}, bf16[512,256]{1,0:T(8,128)(2,1)S(1)}, u32[]{:S(2)}, u32[]{:S(2)}) collective-permute-start(bf16[512,256]{1,0:T(8,128)(2,1)S(1)} %get-tuple-element.64.refs_2_), channel_id=1, source_target_pairs={{0,2},{1,3},{2,0},{3,1},{4,6},{5,7},{6,4},{7,5},{8,10},{9,11},{10,... | collective-permute-start | bytes 786440 | tf_op jit(solution)/shard_map/ppermute | solution.py:334
  46.2 1.5 %collective-permute-start.6 = (bf16[512,256]{1,0:T(8,128)(2,1)S(1)}, bf16[512,256]{1,0:T(8,128)(2,1)S(1)}, u32[]{:S(2)}, u32[]{:S(2)}) collective-permute-start(bf16[512,256]{1,0:T(8,128)(2,1)S(1)} %get-tuple-element.64.refs_2_), channel_id=1, source_target_pairs={{0,4},{1,5},{2,6},{3,7},{4,0},{5,1},{6,2},{7,3},{8,12},{9,13},{10,... | collective-permute-start | bytes 786440 | tf_op jit(solution)/shard_map/ppermute | solution.py:334
  49.5 2.5 %collective-permute-start.12 = (bf16[1024,128]{1,0:T(8,128)(2,1)S(1)}, bf16[1024,128]{1,0:T(8,128)(2,1)S(1)}, u32[]{:S(2)}, u32[]{:S(2)}) collective-permute-start(bf16[1024,128]{1,0:T(8,128)(2,1)S(1)} %get-tuple-element.73.refs_1_), channel_id=1, source_target_pairs={{0,16},{1,17},{2,18},{3,19},{4,20},{5,21},{6,22},{7,23},{8,24},{9,... | collective-permute-start | bytes 786440 | tf_op jit(solution)/shard_map/ppermute | solution.py:334
  52.0 2.0 %collective-permute-done.5.refs_3_ = bf16[512,256]{1,0:T(8,128)(2,1)S(1)} collective-permute-done((bf16[512,256]{1,0:T(8,128)(2,1)S(1)}, bf16[512,256]{1,0:T(8,128)(2,1)S(1)}, u32[]{:S(2)}, u32[]{:S(2)}) %collective-permute-start.5) | collective-permute-done | bytes 262176 | tf_op jit(solution)/shard_map/ppermute | solution.py:334
  54.0 5.5 %collective-permute-done.6.refs_4_ = bf16[512,256]{1,0:T(8,128)(2,1)S(1)} collective-permute-done((bf16[512,256]{1,0:T(8,128)(2,1)S(1)}, bf16[512,256]{1,0:T(8,128)(2,1)S(1)}, u32[]{:S(2)}, u32[]{:S(2)}) %collective-permute-start.6) | collective-permute-done | bytes 262176 | tf_op jit(solution)/shard_map/ppermute | solution.py:334
  60.7 2.5 %collective-permute-start.11 = (bf16[1024,128]{1,0:T(8,128)(2,1)S(1)}, bf16[1024,128]{1,0:T(8,128)(2,1)S(1)}, u32[]{:S(2)}, u32[]{:S(2)}) collective-permute-start(bf16[1024,128]{1,0:T(8,128)(2,1)S(1)} %get-tuple-element.72.refs_1_), channel_id=1, source_target_pairs={{0,16},{1,17},{2,18},{3,19},{4,20},{5,21},{6,22},{7,23},{8,24},{9,... | collective-permute-start | bytes 786440 | tf_op jit(solution)/shard_map/ppermute | solution.py:334
  63.2 2.8 %shard_map.80 = (bf16[1152,1024]{1,0:T(8,128)(2,1)S(1)}, bf16[1152,1024]{1,0:T(8,128)(2,1)S(1)}, f32[8,128]{1,0:T(8,128)S(1)}) custom-call(s32[8,128]{1,0:T(8,128)S(1)} %get-tuple-element.61.refs_0_, bf16[24,128,128]{2,1,0:T(8,128)(2,1)S(1)} %copy-done, bf16[24,128,128]{2,1,0:T(8,128)(2,1)S(1)} %collective-permute-done.2.refs_2_, ...), custom_call_target="tpu_custom_call" | custom-call | tf_op jit(solution)/shard_map/pallas_call | solution.py:68
  69.9 5.5 %collective-permute-start.17 = (bf16[512,128]{1,0:T(8,128)(2,1)S(1)}, bf16[512,128]{1,0:T(8,128)(2,1)S(1)}, u32[]{:S(2)}, u32[]{:S(2)}) collective-permute-start(bf16[512,128]{1,0:T(8,128)(2,1)S(1)} %get-tuple-element.86), channel_id=1, source_target_pairs={{0,4},{1,5},{2,6},{3,7},{4,0},{5,1},{6,2},{7,3},{8,12},{9,13},{10,... | collective-permute-start | bytes 393224 | tf_op jit(solution)/shard_map/ppermute | solution.py:334
  77.7 1.5 %collective-permute-start.13 = (bf16[512,128]{1,0:T(8,128)(2,1)S(1)}, bf16[512,128]{1,0:T(8,128)(2,1)S(1)}, u32[]{:S(2)}, u32[]{:S(2)}) collective-permute-start(bf16[512,128]{1,0:T(8,128)(2,1)S(1)} %get-tuple-element.80), channel_id=1, source_target_pairs={{0,2},{1,3},{2,0},{3,1},{4,6},{5,7},{6,4},{7,5},{8,10},{9,11},{10,... | collective-permute-start | bytes 393224 | tf_op jit(solution)/shard_map/ppermute | solution.py:334
  80.1 2.0 %collective-permute-start.14 = (bf16[512,128]{1,0:T(8,128)(2,1)S(1)}, bf16[512,128]{1,0:T(8,128)(2,1)S(1)}, u32[]{:S(2)}, u32[]{:S(2)}) collective-permute-start(bf16[512,128]{1,0:T(8,128)(2,1)S(1)} %get-tuple-element.81), channel_id=1, source_target_pairs={{0,4},{1,5},{2,6},{3,7},{4,0},{5,1},{6,2},{7,3},{8,12},{9,13},{10,... | collective-permute-start | bytes 393224 | tf_op jit(solution)/shard_map/ppermute | solution.py:334
  82.5 4.1 %collective-permute-done.19.refs_2_ = bf16[1024,128]{1,0:T(8,128)(2,1)S(1)} collective-permute-done((bf16[1024,128]{1,0:T(8,128)(2,1)S(1)}, bf16[1024,128]{1,0:T(8,128)(2,1)S(1)}, u32[]{:S(2)}, u32[]{:S(2)}) %collective-permute-start.19) | collective-permute-done | bytes 262176 | tf_op jit(solution)/shard_map/ppermute | solution.py:334
  87.9 1.6 %collective-permute-start.23 = (bf16[512,128]{1,0:T(8,128)(2,1)S(1)}, bf16[512,128]{1,0:T(8,128)(2,1)S(1)}, u32[]{:S(2)}, u32[]{:S(2)}) collective-permute-start(bf16[512,128]{1,0:T(8,128)(2,1)S(1)} %get-tuple-element.101), channel_id=1, source_target_pairs={{0,2},{1,3},{2,0},{3,1},{4,6},{5,7},{6,4},{7,5},{8,10},{9,11},{10,... | collective-permute-start | bytes 393224 | tf_op jit(solution)/shard_map/ppermute | solution.py:334
  89.5 1.5 %collective-permute-start.24 = (bf16[512,128]{1,0:T(8,128)(2,1)S(1)}, bf16[512,128]{1,0:T(8,128)(2,1)S(1)}, u32[]{:S(2)}, u32[]{:S(2)}) collective-permute-start(bf16[512,128]{1,0:T(8,128)(2,1)S(1)} %get-tuple-element.102), channel_id=1, source_target_pairs={{0,4},{1,5},{2,6},{3,7},{4,0},{5,1},{6,2},{7,3},{8,12},{9,13},{10,... | collective-permute-start | bytes 393224 | tf_op jit(solution)/shard_map/ppermute | solution.py:334
  94.7 2.2 %collective-permute-done.25.refs_6_ = bf16[512,128]{1,0:T(8,128)(2,1)S(1)} collective-permute-done((bf16[512,128]{1,0:T(8,128)(2,1)S(1)}, bf16[512,128]{1,0:T(8,128)(2,1)S(1)}, u32[]{:S(2)}, u32[]{:S(2)}) %collective-permute-start.25) | collective-permute-done | bytes 131104 | tf_op jit(solution)/shard_map/ppermute | solution.py:334
  97.6 1.5 %collective-permute-start.28 = (bf16[128,128]{1,0:T(8,128)(2,1)S(1)}, bf16[128,128]{1,0:T(8,128)(2,1)S(1)}, u32[]{:S(2)}, u32[]{:S(2)}) collective-permute-start(bf16[128,128]{1,0:T(8,128)(2,1)S(1)} %get-tuple-element.110), channel_id=1, source_target_pairs={{0,9},{1,8},{2,11},{3,10},{4,13},{5,12},{6,15},{7,14},{8,1},{9,0},... | collective-permute-start | bytes 98312 | tf_op jit(solution)/shard_map/ppermute | solution.py:334
  100.0 1.4 %collective-permute-done.27.refs_3_ = bf16[128,128]{1,0:T(8,128)(2,1)S(1)} collective-permute-done((bf16[128,128]{1,0:T(8,128)(2,1)S(1)}, bf16[128,128]{1,0:T(8,128)(2,1)S(1)}, u32[]{:S(2)}, u32[]{:S(2)}) %collective-permute-start.27) | collective-permute-done | bytes 32800 | tf_op jit(solution)/shard_map/ppermute | solution.py:334
  (64 shorter events, 21.8 us)
Async XLA Ops:
  1.1 14.6 %collective-permute-start = (bf16[15,128,128]{2,1,0:T(8,128)(2,1)S(1)}, bf16[15,128,128]{2,1,0:T(8,128)(2,1)S(1)}, u32[]{:S(2)}, u32[]{:S(2)}) collective-permute-start(bf16[15,128,128]{2,1,0:T(8,128)(2,1)S(1)} %slice.6), channel_id=1, source_target_pairs={{0,8},{1,9},{2,10},{3,11},{4,12},{5,13},{6,14},{7,15},{8,0},{9,1},... | collective-permute-start | bytes 1474568 | tf_op jit(solution)/shard_map/ppermute | solution.py:334
  8.1 27.8 %all-to-all-start = ((bf16[32,104,128]{2,1,0:T(8,128)(2,1)}), bf16[32,104,128]{2,1,0:T(8,128)(2,1)S(1)}, u32[]{:S(2)}, u32[]{:S(2)}) async-start(bf16[32,104,128]{2,1,0:T(8,128)(2,1)} %get-tuple-element.59), calls=%async_computation | async-start | bytes 1703936 | tf_op jit(solution)/shard_map/all_to_all | solution.py:359
  15.7 20.2 %collective-permute-start.1 = (bf16[15,128,128]{2,1,0:T(8,128)(2,1)S(1)}, bf16[15,128,128]{2,1,0:T(8,128)(2,1)S(1)}, u32[]{:S(2)}, u32[]{:S(2)}) collective-permute-start(bf16[15,128,128]{2,1,0:T(8,128)(2,1)S(1)} %collective-permute-done.refs_3_), channel_id=1, source_target_pairs={{0,1},{1,0},{2,3},{3,2},{4,5},{5,4},{6,7},{7,6},{8,9},{9,8},{10,11... | collective-permute-start | bytes 1474568 | tf_op jit(solution)/shard_map/ppermute | solution.py:334
  15.7 20.2 %collective-permute-start.3 = (bf16[9,128,128]{2,1,0:T(8,128)(2,1)S(1)}, bf16[9,128,128]{2,1,0:T(8,128)(2,1)}, u32[]{:S(2)}, u32[]{:S(2)}) collective-permute-start(bf16[9,128,128]{2,1,0:T(8,128)(2,1)S(1)} %slice.7), channel_id=1, source_target_pairs={{0,8},{1,9},{2,10},{3,11},{4,12},{5,13},{6,14},{7,15},{8,0},{9,1},... | collective-permute-start | bytes 884744 | tf_op jit(solution)/shard_map/ppermute | solution.py:334
  18.3 21.6 %collective-permute-start.2 = (bf16[24,128,128]{2,1,0:T(8,128)(2,1)S(1)}, bf16[24,128,128]{2,1,0:T(8,128)(2,1)S(1)}, u32[]{:S(2)}, u32[]{:S(2)}) collective-permute-start(bf16[24,128,128]{2,1,0:T(8,128)(2,1)S(1)} %copy-done), channel_id=1, source_target_pairs={{0,1},{1,0},{2,3},{3,2},{4,5},{5,4},{6,7},{7,6},{8,9},{9,8},{10,11... | collective-permute-start | bytes 2359304 | tf_op jit(solution)/shard_map/ppermute | solution.py:334
  36.4 11.4 %collective-permute-start.10 = (bf16[512,128]{1,0:T(8,128)(2,1)S(1)}, bf16[512,128]{1,0:T(8,128)(2,1)S(1)}, u32[]{:S(2)}, u32[]{:S(2)}) collective-permute-start(bf16[512,128]{1,0:T(8,128)(2,1)S(1)} %get-tuple-element.60.refs_2_.refs_1_), channel_id=1, source_target_pairs={{0,6},{1,7},{2,4},{3,5},{4,2},{5,3},{6,0},{7,1},{8,14},{9,15},{10,... | collective-permute-start | bytes 393224 | tf_op jit(solution)/shard_map/ppermute | solution.py:334
  38.8 9.4 %collective-permute-start.8 = (bf16[512,128]{1,0:T(8,128)(2,1)S(1)}, bf16[512,128]{1,0:T(8,128)(2,1)S(1)}, u32[]{:S(2)}, u32[]{:S(2)}) collective-permute-start(bf16[512,128]{1,0:T(8,128)(2,1)S(1)} %get-tuple-element.60.refs_2_.refs_1_), channel_id=1, source_target_pairs={{0,2},{1,3},{2,0},{3,1},{4,6},{5,7},{6,4},{7,5},{8,10},{9,11},{10,... | collective-permute-start | bytes 393224 | tf_op jit(solution)/shard_map/ppermute | solution.py:334
  39.4 8.9 %collective-permute-start.9 = (bf16[512,128]{1,0:T(8,128)(2,1)S(1)}, bf16[512,128]{1,0:T(8,128)(2,1)S(1)}, u32[]{:S(2)}, u32[]{:S(2)}) collective-permute-start(bf16[512,128]{1,0:T(8,128)(2,1)S(1)} %get-tuple-element.60.refs_2_.refs_1_), channel_id=1, source_target_pairs={{0,4},{1,5},{2,6},{3,7},{4,0},{5,1},{6,2},{7,3},{8,12},{9,13},{10,... | collective-permute-start | bytes 393224 | tf_op jit(solution)/shard_map/ppermute | solution.py:334
  44.7 9.3 %collective-permute-start.5 = (bf16[512,256]{1,0:T(8,128)(2,1)S(1)}, bf16[512,256]{1,0:T(8,128)(2,1)S(1)}, u32[]{:S(2)}, u32[]{:S(2)}) collective-permute-start(bf16[512,256]{1,0:T(8,128)(2,1)S(1)} %get-tuple-element.64.refs_2_), channel_id=1, source_target_pairs={{0,2},{1,3},{2,0},{3,1},{4,6},{5,7},{6,4},{7,5},{8,10},{9,11},{10,... | collective-permute-start | bytes 786440 | tf_op jit(solution)/shard_map/ppermute | solution.py:334
  46.2 13.2 %collective-permute-start.6 = (bf16[512,256]{1,0:T(8,128)(2,1)S(1)}, bf16[512,256]{1,0:T(8,128)(2,1)S(1)}, u32[]{:S(2)}, u32[]{:S(2)}) collective-permute-start(bf16[512,256]{1,0:T(8,128)(2,1)S(1)} %get-tuple-element.64.refs_2_), channel_id=1, source_target_pairs={{0,4},{1,5},{2,6},{3,7},{4,0},{5,1},{6,2},{7,3},{8,12},{9,13},{10,... | collective-permute-start | bytes 786440 | tf_op jit(solution)/shard_map/ppermute | solution.py:334
  47.8 11.7 %collective-permute-start.7 = (bf16[512,256]{1,0:T(8,128)(2,1)S(1)}, bf16[512,256]{1,0:T(8,128)(2,1)S(1)}, u32[]{:S(2)}, u32[]{:S(2)}) collective-permute-start(bf16[512,256]{1,0:T(8,128)(2,1)S(1)} %get-tuple-element.64.refs_2_), channel_id=1, source_target_pairs={{0,6},{1,7},{2,4},{3,5},{4,2},{5,3},{6,0},{7,1},{8,14},{9,15},{10,... | collective-permute-start | bytes 786440 | tf_op jit(solution)/shard_map/ppermute | solution.py:334
  49.5 16.5 %collective-permute-start.12 = (bf16[1024,128]{1,0:T(8,128)(2,1)S(1)}, bf16[1024,128]{1,0:T(8,128)(2,1)S(1)}, u32[]{:S(2)}, u32[]{:S(2)}) collective-permute-start(bf16[1024,128]{1,0:T(8,128)(2,1)S(1)} %get-tuple-element.73.refs_1_), channel_id=1, source_target_pairs={{0,16},{1,17},{2,18},{3,19},{4,20},{5,21},{6,22},{7,23},{8,24},{9,... | collective-permute-start | bytes 786440 | tf_op jit(solution)/shard_map/ppermute | solution.py:334
  60.7 15.7 %collective-permute-start.11 = (bf16[1024,128]{1,0:T(8,128)(2,1)S(1)}, bf16[1024,128]{1,0:T(8,128)(2,1)S(1)}, u32[]{:S(2)}, u32[]{:S(2)}) collective-permute-start(bf16[1024,128]{1,0:T(8,128)(2,1)S(1)} %get-tuple-element.72.refs_1_), channel_id=1, source_target_pairs={{0,16},{1,17},{2,18},{3,19},{4,20},{5,21},{6,22},{7,23},{8,24},{9,... | collective-permute-start | bytes 786440 | tf_op jit(solution)/shard_map/ppermute | solution.py:334
  68.6 11.5 %collective-permute-start.16 = (bf16[512,128]{1,0:T(8,128)(2,1)S(1)}, bf16[512,128]{1,0:T(8,128)(2,1)S(1)}, u32[]{:S(2)}, u32[]{:S(2)}) collective-permute-start(bf16[512,128]{1,0:T(8,128)(2,1)S(1)} %get-tuple-element.85), channel_id=1, source_target_pairs={{0,2},{1,3},{2,0},{3,1},{4,6},{5,7},{6,4},{7,5},{8,10},{9,11},{10,... | collective-permute-start | bytes 393224 | tf_op jit(solution)/shard_map/ppermute | solution.py:334
  69.9 12.2 %collective-permute-start.17 = (bf16[512,128]{1,0:T(8,128)(2,1)S(1)}, bf16[512,128]{1,0:T(8,128)(2,1)S(1)}, u32[]{:S(2)}, u32[]{:S(2)}) collective-permute-start(bf16[512,128]{1,0:T(8,128)(2,1)S(1)} %get-tuple-element.86), channel_id=1, source_target_pairs={{0,4},{1,5},{2,6},{3,7},{4,0},{5,1},{6,2},{7,3},{8,12},{9,13},{10,... | collective-permute-start | bytes 393224 | tf_op jit(solution)/shard_map/ppermute | solution.py:334
  75.4 6.8 %collective-permute-start.18 = (bf16[512,128]{1,0:T(8,128)(2,1)S(1)}, bf16[512,128]{1,0:T(8,128)(2,1)S(1)}, u32[]{:S(2)}, u32[]{:S(2)}) collective-permute-start(bf16[512,128]{1,0:T(8,128)(2,1)S(1)} %get-tuple-element.87), channel_id=1, source_target_pairs={{0,6},{1,7},{2,4},{3,5},{4,2},{5,3},{6,0},{7,1},{8,14},{9,15},{10,... | collective-permute-start | bytes 393224 | tf_op jit(solution)/shard_map/ppermute | solution.py:334
  75.4 11.2 %collective-permute-start.19 = (bf16[1024,128]{1,0:T(8,128)(2,1)S(1)}, bf16[1024,128]{1,0:T(8,128)(2,1)S(1)}, u32[]{:S(2)}, u32[]{:S(2)}) collective-permute-start(bf16[1024,128]{1,0:T(8,128)(2,1)S(1)} %get-tuple-element.92.refs_1_), channel_id=1, source_target_pairs={{0,16},{1,17},{2,18},{3,19},{4,20},{5,21},{6,22},{7,23},{8,24},{9,... | collective-permute-start | bytes 786440 | tf_op jit(solution)/shard_map/ppermute | solution.py:334
  77.7 13.4 %collective-permute-start.13 = (bf16[512,128]{1,0:T(8,128)(2,1)S(1)}, bf16[512,128]{1,0:T(8,128)(2,1)S(1)}, u32[]{:S(2)}, u32[]{:S(2)}) collective-permute-start(bf16[512,128]{1,0:T(8,128)(2,1)S(1)} %get-tuple-element.80), channel_id=1, source_target_pairs={{0,2},{1,3},{2,0},{3,1},{4,6},{5,7},{6,4},{7,5},{8,10},{9,11},{10,... | collective-permute-start | bytes 393224 | tf_op jit(solution)/shard_map/ppermute | solution.py:334
  80.1 11.4 %collective-permute-start.14 = (bf16[512,128]{1,0:T(8,128)(2,1)S(1)}, bf16[512,128]{1,0:T(8,128)(2,1)S(1)}, u32[]{:S(2)}, u32[]{:S(2)}) collective-permute-start(bf16[512,128]{1,0:T(8,128)(2,1)S(1)} %get-tuple-element.81), channel_id=1, source_target_pairs={{0,4},{1,5},{2,6},{3,7},{4,0},{5,1},{6,2},{7,3},{8,12},{9,13},{10,... | collective-permute-start | bytes 393224 | tf_op jit(solution)/shard_map/ppermute | solution.py:334
  82.2 9.4 %collective-permute-start.15 = (bf16[512,128]{1,0:T(8,128)(2,1)S(1)}, bf16[512,128]{1,0:T(8,128)(2,1)S(1)}, u32[]{:S(2)}, u32[]{:S(2)}) collective-permute-start(bf16[512,128]{1,0:T(8,128)(2,1)S(1)} %get-tuple-element.82), channel_id=1, source_target_pairs={{0,6},{1,7},{2,4},{3,5},{4,2},{5,3},{6,0},{7,1},{8,14},{9,15},{10,... | collective-permute-start | bytes 393224 | tf_op jit(solution)/shard_map/ppermute | solution.py:334
  91.0 5.9 %collective-permute-start.25 = (bf16[512,128]{1,0:T(8,128)(2,1)S(1)}, bf16[512,128]{1,0:T(8,128)(2,1)S(1)}, u32[]{:S(2)}, u32[]{:S(2)}) collective-permute-start(bf16[512,128]{1,0:T(8,128)(2,1)S(1)} %get-tuple-element.103), channel_id=1, source_target_pairs={{0,6},{1,7},{2,4},{3,5},{4,2},{5,3},{6,0},{7,1},{8,14},{9,15},{10,... | collective-permute-start | bytes 393224 | tf_op jit(solution)/shard_map/ppermute | solution.py:334
  91.8 5.8 %collective-permute-start.20 = (bf16[128,256]{1,0:T(8,128)(2,1)S(1)}, bf16[128,256]{1,0:T(8,128)(2,1)S(1)}, u32[]{:S(2)}, u32[]{:S(2)}) collective-permute-start(bf16[128,256]{1,0:T(8,128)(2,1)S(1)} %get-tuple-element.96), channel_id=1, source_target_pairs={{0,1},{1,0},{2,3},{3,2},{4,5},{5,4},{6,7},{7,6},{8,9},{9,8},{10,11... | collective-permute-start | bytes 196616 | tf_op jit(solution)/shard_map/ppermute | solution.py:334
  91.9 7.3 %collective-permute-start.21 = (bf16[128,256]{1,0:T(8,128)(2,1)S(1)}, bf16[128,256]{1,0:T(8,128)(2,1)S(1)}, u32[]{:S(2)}, u32[]{:S(2)}) collective-permute-start(bf16[128,256]{1,0:T(8,128)(2,1)S(1)} %get-tuple-element.97), channel_id=1, source_target_pairs={{0,8},{1,9},{2,10},{3,11},{4,12},{5,13},{6,14},{7,15},{8,0},{9,1},... | collective-permute-start | bytes 196616 | tf_op jit(solution)/shard_map/ppermute | solution.py:334
  93.0 6.2 %collective-permute-start.22 = (bf16[128,256]{1,0:T(8,128)(2,1)S(1)}, bf16[128,256]{1,0:T(8,128)(2,1)S(1)}, u32[]{:S(2)}, u32[]{:S(2)}) collective-permute-start(bf16[128,256]{1,0:T(8,128)(2,1)S(1)} %get-tuple-element.98), channel_id=1, source_target_pairs={{0,9},{1,8},{2,11},{3,10},{4,13},{5,12},{6,15},{7,14},{8,1},{9,0},... | collective-permute-start | bytes 196616 | tf_op jit(solution)/shard_map/ppermute | solution.py:334
  (9 other events, 45.1 us)

commit v6 on v5

--- a/solution.py
+++ b/solution.py
@@ -159,9 +159,9 @@
                         b * lay.slab : (b + 1) * lay.slab, g * CH : (g + 1) * CH
                     ]
                 out[d, lay.groups * lay.slab : lay.pay, :] = below[b]
-                pltpu.make_async_copy(out.at[d], out_far.at[d], gone.at[d]).start()
-    for d in range(lay.U):
-        pltpu.make_async_copy(out.at[d], out_far.at[d], gone.at[d]).wait()
+    send = pltpu.make_async_copy(out, out_far, gone)
+    send.start()
+    send.wait()
 
 
 def land_kernel(lay, first, many, got, out, ids=None):
@@ -192,21 +192,24 @@
             ids[2 * i : 2 * i + 2, :] = found[1:3, :].astype(jnp.int32)
 
 
-def dense_kernel(lay, turned, ids, far0, far2, v1, w1, v3, w3, near, far, v0, v2, arrived):
+def dense_kernel(lay, turned, *refs):
     here = Here(lay)
+    far_ids, sources, (near, far, ids), held, arrived = refs[0], refs[1:7], refs[7:10], refs[10:16], refs[16]
     fetch = [
-        pltpu.make_async_copy(a, b, arrived.at[i]) for i, (a, b) in enumerate(((far0, v0), (far2, v2)))
+        pltpu.make_async_copy(src, dst, arrived.at[i])
+        for i, (src, dst) in enumerate(zip((*sources, far_ids), (*held, ids)))
     ]
     for copy in fetch:
         copy.start()
     near[...] = jnp.zeros_like(near)
     far[...] = jnp.zeros_like(far)
+    fetch[-1].wait()
     spare = 2 * lay.chips
-    cut = v1.shape[0]
-    sets = ((1, 0, v1, far), (3, 0, v3, far), (0, 0, v0, near), (2, 0, v2, near), (1, cut, w1, far), (3, cut, w3, far))
-    for i, skip, values, to in sets:
-        if i % 2 == 0:
-            fetch[i // 2].wait()
+    cut = held[2].shape[0]
+    order = ((2, 1, 0, far), (4, 3, 0, far), (0, 0, 0, near), (1, 2, 0, near), (3, 1, cut, far), (5, 3, cut, far))
+    for n, i, skip, to in order:
+        values = held[n]
+        fetch[n].wait()
 
         def body(t, carry, i=i, skip=skip, values=values, to=to):
             rt, ct = ids[2 * i, skip + t], ids[2 * i + 1, skip + t]
@@ -306,7 +309,8 @@
     join_kernel(lay, done, None, *refs)
 
 
-GATHER = ((0, 1), (1, 2))
+GATHER = ((0, 1), (1, 1), (2, 1))
+RELAY = False
 SUMS = ((0, 1), (1, 1), (2, 1))
 BLOCK = 256
 AHEAD = 5
@@ -352,7 +356,7 @@
             pltpu.VMEM((1, lay.slots), jnp.int32),
             pltpu.VMEM(tile_ids.shape[::-1], jnp.int32),
             pltpu.SemaphoreType.DMA((4,)),
-            pltpu.SemaphoreType.DMA((lay.U,)),
+            pltpu.SemaphoreType.DMA(()),
         ],
         vmem=PACK_VMEM,
     )(unit_rows, node_map.reshape(1, lay.slots), tile_ids.T, ingest_features)
@@ -360,14 +364,20 @@
 
     _, token = call(seen_kernel, [], [VM], flops=SEEN_FLOPS)(val3[0])
 
-    def land(first, many, token, extra=()):
+    def land(first, many, token, extra=(), relay=False):
         (x, *more), token = call(
             functools.partial(land_kernel, lay, first, many),
             [array(lay.own, many * CH), *extra],
             [VM],
             behind=[token],
         )(got)
-        return [x] + [exchange(x, chip=s) for s in range(1, lay.chips)], more, token
+        if relay:
+            xs = [x]
+            while len(xs) < lay.chips:
+                xs += [exchange(y, chip=len(xs)) for y in list(xs)]
+        else:
+            xs = [x] + [exchange(x, chip=s) for s in range(1, lay.chips)]
+        return xs, more, token
 
     def dense(turned, token):
         depth = 2 * lay.chips * PIECE + TILE
@@ -375,18 +385,18 @@
         return call(
             functools.partial(dense_kernel, lay, turned),
             [array(*shape)] * 2,
-            [SM, HB, HB, VM, VM, VM, VM],
+            [HB] * 7,
             behind=[token],
-            scratch=[pltpu.VMEM(tile_values.shape, BF16)] * 2 + [pltpu.SemaphoreType.DMA((2,))],
+            scratch=[pltpu.SMEM((8, CH), jnp.int32)]
+            + [pltpu.VMEM(x.shape, BF16) for x in values]
+            + [pltpu.SemaphoreType.DMA((7,))],
         )(ids, *values)
 
     xs, (ids,), token = land(*GATHER[0], token, [array(8, CH, jnp.int32)])
     gathered = [xs]
     (at0, at1), token = dense(True, token)
-    for first, many in GATHER[1:]:
-        xs, _, token = land(first, many, token)
-        gathered.append(xs)
-    own = [xs[0] for xs in gathered]
+    xs, _, token = land(*GATHER[1], token, relay=True)
+    gathered.append(xs)
 
     def back(n, token, wait=()):
         first, many = SUMS[n]
@@ -437,6 +447,10 @@
 
     left, parts = [], []
     ready, token = back(0, token)
+    for first, many in GATHER[2:]:
+        xs, _, token = land(first, many, token, relay=RELAY)
+        gathered.append(xs)
+    own = [xs[0] for xs in gathered]
     coming, token = back(1, token)
     (a0, a1), token = dense(False, token)
     for n in range(len(SUMS)):

time: 103 us -> 101 us (0.981)
  starting transfers between devices: 39.6 us -> 37.5 us
    ppermute x29 -> x32, starting transfers between devices: 34.8 us -> 32.6 us  [exchange(): return lax.ppermute(x, ('row', 'col'), pairs)]
    pallas_call x20 -> x21, Pallas kernels: 24.6 us -> 24.8 us  [apply(): *outs, token = run(*args, *behind)]
    ppermute x29 -> x32, waiting for transfers between devices: 36.4 us -> 36.5 us  [exchange(): return lax.ppermute(x, ('row', 'col'), pairs)]
  transfers between devices with their start and end apart: 30 -> 33, of which waited for: 8 -> 9; matrix products, arithmetic and copies ran while one was open for 0% -> 0% of each run, Pallas kernels for 23% -> 23%
where the time goes in v6:
time: 101 us
  starting transfers between devices  37.5 us (37%)
  waiting for transfers between devices  36.5 us (36%)
  Pallas kernels  24.8 us (25%)
  local copies, waits for them, and re-layouts  1.17 us (1%)
  between operations  1.04 us (1%)
    ppermute x32, waiting for transfers between devices, exchange(): return lax.ppermute(x, ('row', 'col'), pairs)  36.5 us
    ppermute x32, starting transfers between devices, exchange(): return lax.ppermute(x, ('row', 'col'), pairs)  32.6 us
    pallas_call x21, Pallas kernels, apply(): *outs, token = run(*args, *behind)  24.8 us
    all_to_all x1, starting transfers between devices, local(): lax.all_to_all(outgoing, ('row', 'col'), split_axis=0, concat_axis=0, til...  4.84 us
  transfers between devices with their start and end apart: 33, of which 9 were waited for; matrix products, arithmetic and copies ran while one was open for 0% of the time, Pallas kernels for 23%

profile of v6, /device:TPU:0, one launch (start us, length us, event | category | flops | bytes accessed | tf_op | source)
XLA Modules:
  0.0 101.0 jit_solution(10490265540243522509)
XLA Ops:
  1.1 3.1 %collective-permute-start = (bf16[15,128,128]{2,1,0:T(8,128)(2,1)S(1)}, bf16[15,128,128]{2,1,0:T(8,128)(2,1)S(1)}, u32[]{:S(2)}, u32[]{:S(2)}) collective-permute-start(bf16[15,128,128]{2,1,0:T(8,128)(2,1)S(1)} %slice.6), channel_id=1, source_target_pairs={{0,8},{1,9},{2,10},{3,11},{4,12},{5,13},{6,14},{7,15},{8,0},{9,1},... | collective-permute-start | bytes 1474568 | tf_op jit(solution)/shard_map/ppermute | solution.py:338
  4.9 3.2 %shard_map.73 = (bf16[32,104,128]{2,1,0:T(8,128)(2,1)}, f32[8,128]{1,0:T(8,128)}) custom-call(s32[1]{0:T(128)S(6)} %copy.10.refs_0_, s32[1,256]{1,0:T(1,128)} %bitcast.2, s32[2,24]{1,0:T(2,128)} %bitcast.3, bf16[256,1536]{1,0:T(8,128)(2,1)} %refs_3_.1), custom_call_target="tpu_custom_call" | custom-call | tf_op jit(solution)/shard_map/pallas_call | solution.py:68
  8.1 4.8 %all-to-all-start = ((bf16[32,104,128]{2,1,0:T(8,128)(2,1)}), bf16[32,104,128]{2,1,0:T(8,128)(2,1)S(1)}, u32[]{:S(2)}, u32[]{:S(2)}) async-start(bf16[32,104,128]{2,1,0:T(8,128)(2,1)} %get-tuple-element.61), calls=%async_computation | async-start | bytes 1703936 | tf_op jit(solution)/shard_map/all_to_all | solution.py:363
  12.9 2.8 %collective-permute-done.refs_3_ = bf16[15,128,128]{2,1,0:T(8,128)(2,1)S(1)} collective-permute-done((bf16[15,128,128]{2,1,0:T(8,128)(2,1)S(1)}, bf16[15,128,128]{2,1,0:T(8,128)(2,1)S(1)}, u32[]{:S(2)}, u32[]{:S(2)}) %collective-permute-start) | collective-permute-done | bytes 491552 | tf_op jit(solution)/shard_map/ppermute | solution.py:338
  15.7 2.5 %collective-permute-start.3 = (bf16[9,128,128]{2,1,0:T(8,128)(2,1)S(1)}, bf16[9,128,128]{2,1,0:T(8,128)(2,1)}, u32[]{:S(2)}, u32[]{:S(2)}) collective-permute-start(bf16[9,128,128]{2,1,0:T(8,128)(2,1)S(1)} %slice.7), channel_id=1, source_target_pairs={{0,8},{1,9},{2,10},{3,11},{4,12},{5,13},{6,14},{7,15},{8,0},{9,1},... | collective-permute-start | bytes 884744 | tf_op jit(solution)/shard_map/ppermute | solution.py:338
  18.5 17.4 %collective-permute-done.3.refs_4_ = bf16[9,128,128]{2,1,0:T(8,128)(2,1)} collective-permute-done((bf16[9,128,128]{2,1,0:T(8,128)(2,1)S(1)}, bf16[9,128,128]{2,1,0:T(8,128)(2,1)}, u32[]{:S(2)}, u32[]{:S(2)}) %collective-permute-start.3) | collective-permute-done | bytes 294944 | tf_op jit(solution)/shard_map/ppermute | solution.py:338
  36.4 1.5 %collective-permute-start.5 = (bf16[512,128]{1,0:T(8,128)(2,1)S(1)}, bf16[512,128]{1,0:T(8,128)(2,1)S(1)}, u32[]{:S(2)}, u32[]{:S(2)}) collective-permute-start(bf16[512,128]{1,0:T(8,128)(2,1)S(1)} %get-tuple-element.62.refs_2_.refs_1_), channel_id=1, source_target_pairs={{0,2},{1,3},{2,0},{3,1},{4,6},{5,7},{6,4},{7,5},{8,10},{9,11},{10,... | collective-permute-start | bytes 393224 | tf_op jit(solution)/shard_map/ppermute | solution.py:338
  37.9 1.5 %collective-permute-start.6 = (bf16[512,128]{1,0:T(8,128)(2,1)S(1)}, bf16[512,128]{1,0:T(8,128)(2,1)S(1)}, u32[]{:S(2)}, u32[]{:S(2)}) collective-permute-start(bf16[512,128]{1,0:T(8,128)(2,1)S(1)} %get-tuple-element.62.refs_2_.refs_1_), channel_id=1, source_target_pairs={{0,4},{1,5},{2,6},{3,7},{4,0},{5,1},{6,2},{7,3},{8,12},{9,13},{10,... | collective-permute-start | bytes 393224 | tf_op jit(solution)/shard_map/ppermute | solution.py:338
  39.9 3.9 %shard_map.76 = (bf16[1024,1152]{1,0:T(8,128)(2,1)S(1)}, bf16[1024,1152]{1,0:T(8,128)(2,1)S(1)}, f32[8,128]{1,0:T(8,128)S(1)}) custom-call(s32[8,128]{1,0:T(8,128)S(1)} %get-tuple-element.63.refs_0_, bf16[24,128,128]{2,1,0:T(8,128)(2,1)S(1)} %copy-done, bf16[24,128,128]{2,1,0:T(8,128)(2,1)S(1)} %collective-permute-done.2.refs_2_, ...), custom_call_target="tpu_custom_call" | custom-call | tf_op jit(solution)/shard_map/pallas_call | solution.py:68
  44.3 1.5 %collective-permute-start.8 = (bf16[512,128]{1,0:T(8,128)(2,1)S(1)}, bf16[512,128]{1,0:T(8,128)(2,1)S(1)}, u32[]{:S(2)}, u32[]{:S(2)}) collective-permute-start(bf16[512,128]{1,0:T(8,128)(2,1)S(1)} %get-tuple-element.66.refs_2_), channel_id=1, source_target_pairs={{0,2},{1,3},{2,0},{3,1},{4,6},{5,7},{6,4},{7,5},{8,10},{9,11},{10,... | collective-permute-start | bytes 393224 | tf_op jit(solution)/shard_map/ppermute | solution.py:338
  45.9 1.5 %collective-permute-start.9 = (bf16[512,128]{1,0:T(8,128)(2,1)S(1)}, bf16[512,128]{1,0:T(8,128)(2,1)S(1)}, u32[]{:S(2)}, u32[]{:S(2)}) collective-permute-start(bf16[512,128]{1,0:T(8,128)(2,1)S(1)} %get-tuple-element.66.refs_2_), channel_id=1, source_target_pairs={{0,4},{1,5},{2,6},{3,7},{4,0},{5,1},{6,2},{7,3},{8,12},{9,13},{10,... | collective-permute-start | bytes 393224 | tf_op jit(solution)/shard_map/ppermute | solution.py:338
  48.7 2.5 %collective-permute-start.12 = (bf16[1024,128]{1,0:T(8,128)(2,1)S(1)}, bf16[1024,128]{1,0:T(8,128)(2,1)S(1)}, u32[]{:S(2)}, u32[]{:S(2)}) collective-permute-start(bf16[1024,128]{1,0:T(8,128)(2,1)S(1)} %get-tuple-element.77.refs_1_), channel_id=1, source_target_pairs={{0,16},{1,17},{2,18},{3,19},{4,20},{5,21},{6,22},{7,23},{8,24},{9,... | collective-permute-start | bytes 786440 | tf_op jit(solution)/shard_map/ppermute | solution.py:338
  54.3 1.4 %collective-permute-start.15 = (bf16[512,128]{1,0:T(8,128)(2,1)S(1)}, bf16[512,128]{1,0:T(8,128)(2,1)S(1)}, u32[]{:S(2)}, u32[]{:S(2)}) collective-permute-start(bf16[512,128]{1,0:T(8,128)(2,1)S(1)} %get-tuple-element.71.refs_2_.refs_3_), channel_id=1, source_target_pairs={{0,6},{1,7},{2,4},{3,5},{4,2},{5,3},{6,0},{7,1},{8,14},{9,15},{10,... | collective-permute-start | bytes 393224 | tf_op jit(solution)/shard_map/ppermute | solution.py:338
  55.7 2.5 %collective-permute-done.10.refs_5_ = bf16[512,128]{1,0:T(8,128)(2,1)S(1)} collective-permute-done((bf16[512,128]{1,0:T(8,128)(2,1)S(1)}, bf16[512,128]{1,0:T(8,128)(2,1)S(1)}, u32[]{:S(2)}, u32[]{:S(2)}) %collective-permute-start.10) | collective-permute-done | bytes 131104 | tf_op jit(solution)/shard_map/ppermute | solution.py:338
  59.6 2.7 %shard_map.81 = (bf16[1152,1024]{1,0:T(8,128)(2,1)S(1)}, bf16[1152,1024]{1,0:T(8,128)(2,1)S(1)}, f32[8,128]{1,0:T(8,128)S(1)}) custom-call(s32[8,128]{1,0:T(8,128)S(1)} %get-tuple-element.63.refs_0_, bf16[24,128,128]{2,1,0:T(8,128)(2,1)S(1)} %copy-done, bf16[24,128,128]{2,1,0:T(8,128)(2,1)S(1)} %collective-permute-done.2.refs_2_, ...), custom_call_target="tpu_custom_call" | custom-call | tf_op jit(solution)/shard_map/pallas_call | solution.py:68
  62.3 6.9 %collective-permute-done.12.refs_7_.refs_2_ = bf16[1024,128]{1,0:T(8,128)(2,1)S(1)} collective-permute-done((bf16[1024,128]{1,0:T(8,128)(2,1)S(1)}, bf16[1024,128]{1,0:T(8,128)(2,1)S(1)}, u32[]{:S(2)}, u32[]{:S(2)}) %collective-permute-start.12) | collective-permute-done | bytes 262176 | tf_op jit(solution)/shard_map/ppermute | solution.py:338
  70.5 1.3 %shard_map.83 = (bf16[1024,128]{1,0:T(8,128)(2,1)S(1)}, bf16[512,128]{1,0:T(8,128)(2,1)S(1)}, bf16[512,128]{1,0:T(8,128)(2,1)S(1)}, bf16[512,128]{1,0:T(8,128)(2,1)S(1)}, f32[8,128]{1,0:T(8,128)S(1)}) custom-call(bf16[128,128]{1,0:T(8,128)(2,1)S(1)} %copy-done.1, bf16[1024,128]{1,0:T(8,128)(2,1)S(1)} %get-tuple-element.77.refs_1_, ...), custom_call_target="tpu_custom_call" | custom-call | tf_op jit(solution)/shard_map/pallas_call | solution.py:68
  73.3 2.1 %collective-permute-start.21 = (bf16[512,128]{1,0:T(8,128)(2,1)S(1)}, bf16[512,128]{1,0:T(8,128)(2,1)S(1)}, u32[]{:S(2)}, u32[]{:S(2)}) collective-permute-start(bf16[512,128]{1,0:T(8,128)(2,1)S(1)} %get-tuple-element.91), channel_id=1, source_target_pairs={{0,6},{1,7},{2,4},{3,5},{4,2},{5,3},{6,0},{7,1},{8,14},{9,15},{10,... | collective-permute-start | bytes 393224 | tf_op jit(solution)/shard_map/ppermute | solution.py:338
  76.3 1.3 %shard_map.84 = (bf16[1024,128]{1,0:T(8,128)(2,1)S(1)}, bf16[512,128]{1,0:T(8,128)(2,1)S(1)}, bf16[512,128]{1,0:T(8,128)(2,1)S(1)}, bf16[512,128]{1,0:T(8,128)(2,1)S(1)}, f32[8,128]{1,0:T(8,128)S(1)}) custom-call(bf16[128,128]{1,0:T(8,128)(2,1)S(1)} %copy-done.1, bf16[1024,128]{1,0:T(8,128)(2,1)S(1)} %get-tuple-element.76.refs_1_, ...), custom_call_target="tpu_custom_call" | custom-call | tf_op jit(solution)/shard_map/pallas_call | solution.py:68
  79.1 2.1 %collective-permute-start.18 = (bf16[512,128]{1,0:T(8,128)(2,1)S(1)}, bf16[512,128]{1,0:T(8,128)(2,1)S(1)}, u32[]{:S(2)}, u32[]{:S(2)}) collective-permute-start(bf16[512,128]{1,0:T(8,128)(2,1)S(1)} %get-tuple-element.86), channel_id=1, source_target_pairs={{0,6},{1,7},{2,4},{3,5},{4,2},{5,3},{6,0},{7,1},{8,14},{9,15},{10,... | collective-permute-start | bytes 393224 | tf_op jit(solution)/shard_map/ppermute | solution.py:338
  82.5 3.7 %collective-permute-done.22.refs_2_ = bf16[1024,128]{1,0:T(8,128)(2,1)S(1)} collective-permute-done((bf16[1024,128]{1,0:T(8,128)(2,1)S(1)}, bf16[1024,128]{1,0:T(8,128)(2,1)S(1)}, u32[]{:S(2)}, u32[]{:S(2)}) %collective-permute-start.22) | collective-permute-done | bytes 262176 | tf_op jit(solution)/shard_map/ppermute | solution.py:338
  86.2 1.3 %shard_map.88 = (bf16[1024,128]{1,0:T(8,128)(2,1)S(1)}, bf16[512,128]{1,0:T(8,128)(2,1)S(1)}, bf16[512,128]{1,0:T(8,128)(2,1)S(1)}, bf16[512,128]{1,0:T(8,128)(2,1)S(1)}, f32[8,128]{1,0:T(8,128)S(1)}) custom-call(bf16[128,128]{1,0:T(8,128)(2,1)S(1)} %copy-done.1, bf16[1024,128]{1,0:T(8,128)(2,1)S(1)} %get-tuple-element.96.refs_1_, ...), custom_call_target="tpu_custom_call" | custom-call | tf_op jit(solution)/shard_map/pallas_call | solution.py:68
  88.9 2.1 %collective-permute-start.28 = (bf16[512,128]{1,0:T(8,128)(2,1)S(1)}, bf16[512,128]{1,0:T(8,128)(2,1)S(1)}, u32[]{:S(2)}, u32[]{:S(2)}) collective-permute-start(bf16[512,128]{1,0:T(8,128)(2,1)S(1)} %get-tuple-element.107), channel_id=1, source_target_pairs={{0,6},{1,7},{2,4},{3,5},{4,2},{5,3},{6,0},{7,1},{8,14},{9,15},{10,... | collective-permute-start | bytes 393224 | tf_op jit(solution)/shard_map/ppermute | solution.py:338
  99.5 1.3 %shard_map.93 = (f32[128,1536]{1,0:T(8,128)}, f32[8,128]{1,0:T(8,128)}) custom-call(f32[128,1536]{1,0:T(8,128)} %get-tuple-element.110.refs_0_, f32[128,128]{1,0:T(8,128)S(1)} %get-tuple-element.111.refs_1_, bf16[128,128]{1,0:T(8,128)(2,1)S(1)} %collective-permute-done.29.refs_2_, ...), custom_call_target="tpu_custom_call", output_to_operand_aliasing={{0}: (0, {})} | custom-call | tf_op jit(solution)/shard_map/pallas_call | solution.py:68
  (71 shorter events, 24.8 us)
Async XLA Ops:
  1.1 14.5 %collective-permute-start = (bf16[15,128,128]{2,1,0:T(8,128)(2,1)S(1)}, bf16[15,128,128]{2,1,0:T(8,128)(2,1)S(1)}, u32[]{:S(2)}, u32[]{:S(2)}) collective-permute-start(bf16[15,128,128]{2,1,0:T(8,128)(2,1)S(1)} %slice.6), channel_id=1, source_target_pairs={{0,8},{1,9},{2,10},{3,11},{4,12},{5,13},{6,14},{7,15},{8,0},{9,1},... | collective-permute-start | bytes 1474568 | tf_op jit(solution)/shard_map/ppermute | solution.py:338
  8.1 27.8 %all-to-all-start = ((bf16[32,104,128]{2,1,0:T(8,128)(2,1)}), bf16[32,104,128]{2,1,0:T(8,128)(2,1)S(1)}, u32[]{:S(2)}, u32[]{:S(2)}) async-start(bf16[32,104,128]{2,1,0:T(8,128)(2,1)} %get-tuple-element.61), calls=%async_computation | async-start | bytes 1703936 | tf_op jit(solution)/shard_map/all_to_all | solution.py:363
  15.7 20.2 %collective-permute-start.1 = (bf16[15,128,128]{2,1,0:T(8,128)(2,1)S(1)}, bf16[15,128,128]{2,1,0:T(8,128)(2,1)S(1)}, u32[]{:S(2)}, u32[]{:S(2)}) collective-permute-start(bf16[15,128,128]{2,1,0:T(8,128)(2,1)S(1)} %collective-permute-done.refs_3_), channel_id=1, source_target_pairs={{0,1},{1,0},{2,3},{3,2},{4,5},{5,4},{6,7},{7,6},{8,9},{9,8},{10,11... | collective-permute-start | bytes 1474568 | tf_op jit(solution)/shard_map/ppermute | solution.py:338
  15.7 20.2 %collective-permute-start.3 = (bf16[9,128,128]{2,1,0:T(8,128)(2,1)S(1)}, bf16[9,128,128]{2,1,0:T(8,128)(2,1)}, u32[]{:S(2)}, u32[]{:S(2)}) collective-permute-start(bf16[9,128,128]{2,1,0:T(8,128)(2,1)S(1)} %slice.7), channel_id=1, source_target_pairs={{0,8},{1,9},{2,10},{3,11},{4,12},{5,13},{6,14},{7,15},{8,0},{9,1},... | collective-permute-start | bytes 884744 | tf_op jit(solution)/shard_map/ppermute | solution.py:338
  18.3 21.7 %collective-permute-start.2 = (bf16[24,128,128]{2,1,0:T(8,128)(2,1)S(1)}, bf16[24,128,128]{2,1,0:T(8,128)(2,1)S(1)}, u32[]{:S(2)}, u32[]{:S(2)}) collective-permute-start(bf16[24,128,128]{2,1,0:T(8,128)(2,1)S(1)} %copy-done), channel_id=1, source_target_pairs={{0,1},{1,0},{2,3},{3,2},{4,5},{5,4},{6,7},{7,6},{8,9},{9,8},{10,11... | collective-permute-start | bytes 2359304 | tf_op jit(solution)/shard_map/ppermute | solution.py:338
  36.4 11.0 %collective-permute-start.5 = (bf16[512,128]{1,0:T(8,128)(2,1)S(1)}, bf16[512,128]{1,0:T(8,128)(2,1)S(1)}, u32[]{:S(2)}, u32[]{:S(2)}) collective-permute-start(bf16[512,128]{1,0:T(8,128)(2,1)S(1)} %get-tuple-element.62.refs_2_.refs_1_), channel_id=1, source_target_pairs={{0,2},{1,3},{2,0},{3,1},{4,6},{5,7},{6,4},{7,5},{8,10},{9,11},{10,... | collective-permute-start | bytes 393224 | tf_op jit(solution)/shard_map/ppermute | solution.py:338
  37.9 9.5 %collective-permute-start.6 = (bf16[512,128]{1,0:T(8,128)(2,1)S(1)}, bf16[512,128]{1,0:T(8,128)(2,1)S(1)}, u32[]{:S(2)}, u32[]{:S(2)}) collective-permute-start(bf16[512,128]{1,0:T(8,128)(2,1)S(1)} %get-tuple-element.62.refs_2_.refs_1_), channel_id=1, source_target_pairs={{0,4},{1,5},{2,6},{3,7},{4,0},{5,1},{6,2},{7,3},{8,12},{9,13},{10,... | collective-permute-start | bytes 393224 | tf_op jit(solution)/shard_map/ppermute | solution.py:338
  39.4 8.0 %collective-permute-start.7 = (bf16[512,128]{1,0:T(8,128)(2,1)S(1)}, bf16[512,128]{1,0:T(8,128)(2,1)S(1)}, u32[]{:S(2)}, u32[]{:S(2)}) collective-permute-start(bf16[512,128]{1,0:T(8,128)(2,1)S(1)} %get-tuple-element.62.refs_2_.refs_1_), channel_id=1, source_target_pairs={{0,6},{1,7},{2,4},{3,5},{4,2},{5,3},{6,0},{7,1},{8,14},{9,15},{10,... | collective-permute-start | bytes 393224 | tf_op jit(solution)/shard_map/ppermute | solution.py:338
  44.3 6.8 %collective-permute-start.8 = (bf16[512,128]{1,0:T(8,128)(2,1)S(1)}, bf16[512,128]{1,0:T(8,128)(2,1)S(1)}, u32[]{:S(2)}, u32[]{:S(2)}) collective-permute-start(bf16[512,128]{1,0:T(8,128)(2,1)S(1)} %get-tuple-element.66.refs_2_), channel_id=1, source_target_pairs={{0,2},{1,3},{2,0},{3,1},{4,6},{5,7},{6,4},{7,5},{8,10},{9,11},{10,... | collective-permute-start | bytes 393224 | tf_op jit(solution)/shard_map/ppermute | solution.py:338
  45.9 8.4 %collective-permute-start.9 = (bf16[512,128]{1,0:T(8,128)(2,1)S(1)}, bf16[512,128]{1,0:T(8,128)(2,1)S(1)}, u32[]{:S(2)}, u32[]{:S(2)}) collective-permute-start(bf16[512,128]{1,0:T(8,128)(2,1)S(1)} %get-tuple-element.66.refs_2_), channel_id=1, source_target_pairs={{0,4},{1,5},{2,6},{3,7},{4,0},{5,1},{6,2},{7,3},{8,12},{9,13},{10,... | collective-permute-start | bytes 393224 | tf_op jit(solution)/shard_map/ppermute | solution.py:338
  48.7 20.5 %collective-permute-start.12 = (bf16[1024,128]{1,0:T(8,128)(2,1)S(1)}, bf16[1024,128]{1,0:T(8,128)(2,1)S(1)}, u32[]{:S(2)}, u32[]{:S(2)}) collective-permute-start(bf16[1024,128]{1,0:T(8,128)(2,1)S(1)} %get-tuple-element.77.refs_1_), channel_id=1, source_target_pairs={{0,16},{1,17},{2,18},{3,19},{4,20},{5,21},{6,22},{7,23},{8,24},{9,... | collective-permute-start | bytes 786440 | tf_op jit(solution)/shard_map/ppermute | solution.py:338
  51.2 7.0 %collective-permute-start.10 = (bf16[512,128]{1,0:T(8,128)(2,1)S(1)}, bf16[512,128]{1,0:T(8,128)(2,1)S(1)}, u32[]{:S(2)}, u32[]{:S(2)}) collective-permute-start(bf16[512,128]{1,0:T(8,128)(2,1)S(1)} %collective-permute-done.8.refs_3_), channel_id=1, source_target_pairs={{0,4},{1,5},{2,6},{3,7},{4,0},{5,1},{6,2},{7,3},{8,12},{9,13},{10,... | collective-permute-start | bytes 393224 | tf_op jit(solution)/shard_map/ppermute | solution.py:338
  52.1 10.2 %collective-permute-start.13 = (bf16[512,128]{1,0:T(8,128)(2,1)S(1)}, bf16[512,128]{1,0:T(8,128)(2,1)S(1)}, u32[]{:S(2)}, u32[]{:S(2)}) collective-permute-start(bf16[512,128]{1,0:T(8,128)(2,1)S(1)} %get-tuple-element.71.refs_2_.refs_3_), channel_id=1, source_target_pairs={{0,2},{1,3},{2,0},{3,1},{4,6},{5,7},{6,4},{7,5},{8,10},{9,11},{10,... | collective-permute-start | bytes 393224 | tf_op jit(solution)/shard_map/ppermute | solution.py:338
  52.9 9.4 %collective-permute-start.14 = (bf16[512,128]{1,0:T(8,128)(2,1)S(1)}, bf16[512,128]{1,0:T(8,128)(2,1)S(1)}, u32[]{:S(2)}, u32[]{:S(2)}) collective-permute-start(bf16[512,128]{1,0:T(8,128)(2,1)S(1)} %get-tuple-element.71.refs_2_.refs_3_), channel_id=1, source_target_pairs={{0,4},{1,5},{2,6},{3,7},{4,0},{5,1},{6,2},{7,3},{8,12},{9,13},{10,... | collective-permute-start | bytes 393224 | tf_op jit(solution)/shard_map/ppermute | solution.py:338
  54.3 8.1 %collective-permute-start.15 = (bf16[512,128]{1,0:T(8,128)(2,1)S(1)}, bf16[512,128]{1,0:T(8,128)(2,1)S(1)}, u32[]{:S(2)}, u32[]{:S(2)}) collective-permute-start(bf16[512,128]{1,0:T(8,128)(2,1)S(1)} %get-tuple-element.71.refs_2_.refs_3_), channel_id=1, source_target_pairs={{0,6},{1,7},{2,4},{3,5},{4,2},{5,3},{6,0},{7,1},{8,14},{9,15},{10,... | collective-permute-start | bytes 393224 | tf_op jit(solution)/shard_map/ppermute | solution.py:338
  59.5 16.8 %collective-permute-start.11 = (bf16[1024,128]{1,0:T(8,128)(2,1)S(1)}, bf16[1024,128]{1,0:T(8,128)(2,1)S(1)}, u32[]{:S(2)}, u32[]{:S(2)}) collective-permute-start(bf16[1024,128]{1,0:T(8,128)(2,1)S(1)} %get-tuple-element.76.refs_1_), channel_id=1, source_target_pairs={{0,16},{1,17},{2,18},{3,19},{4,20},{5,21},{6,22},{7,23},{8,24},{9,... | collective-permute-start | bytes 786440 | tf_op jit(solution)/shard_map/ppermute | solution.py:338
  71.8 6.7 %collective-permute-start.19 = (bf16[512,128]{1,0:T(8,128)(2,1)S(1)}, bf16[512,128]{1,0:T(8,128)(2,1)S(1)}, u32[]{:S(2)}, u32[]{:S(2)}) collective-permute-start(bf16[512,128]{1,0:T(8,128)(2,1)S(1)} %get-tuple-element.89), channel_id=1, source_target_pairs={{0,2},{1,3},{2,0},{3,1},{4,6},{5,7},{6,4},{7,5},{8,10},{9,11},{10,... | collective-permute-start | bytes 393224 | tf_op jit(solution)/shard_map/ppermute | solution.py:338
  72.7 6.5 %collective-permute-start.20 = (bf16[512,128]{1,0:T(8,128)(2,1)S(1)}, bf16[512,128]{1,0:T(8,128)(2,1)S(1)}, u32[]{:S(2)}, u32[]{:S(2)}) collective-permute-start(bf16[512,128]{1,0:T(8,128)(2,1)S(1)} %get-tuple-element.90), channel_id=1, source_target_pairs={{0,4},{1,5},{2,6},{3,7},{4,0},{5,1},{6,2},{7,3},{8,12},{9,13},{10,... | collective-permute-start | bytes 393224 | tf_op jit(solution)/shard_map/ppermute | solution.py:338
  73.3 7.9 %collective-permute-start.21 = (bf16[512,128]{1,0:T(8,128)(2,1)S(1)}, bf16[512,128]{1,0:T(8,128)(2,1)S(1)}, u32[]{:S(2)}, u32[]{:S(2)}) collective-permute-start(bf16[512,128]{1,0:T(8,128)(2,1)S(1)} %get-tuple-element.91), channel_id=1, source_target_pairs={{0,6},{1,7},{2,4},{3,5},{4,2},{5,3},{6,0},{7,1},{8,14},{9,15},{10,... | collective-permute-start | bytes 393224 | tf_op jit(solution)/shard_map/ppermute | solution.py:338
  75.4 10.8 %collective-permute-start.22 = (bf16[1024,128]{1,0:T(8,128)(2,1)S(1)}, bf16[1024,128]{1,0:T(8,128)(2,1)S(1)}, u32[]{:S(2)}, u32[]{:S(2)}) collective-permute-start(bf16[1024,128]{1,0:T(8,128)(2,1)S(1)} %get-tuple-element.96.refs_1_), channel_id=1, source_target_pairs={{0,16},{1,17},{2,18},{3,19},{4,20},{5,21},{6,22},{7,23},{8,24},{9,... | collective-permute-start | bytes 786440 | tf_op jit(solution)/shard_map/ppermute | solution.py:338
  77.7 11.2 %collective-permute-start.16 = (bf16[512,128]{1,0:T(8,128)(2,1)S(1)}, bf16[512,128]{1,0:T(8,128)(2,1)S(1)}, u32[]{:S(2)}, u32[]{:S(2)}) collective-permute-start(bf16[512,128]{1,0:T(8,128)(2,1)S(1)} %get-tuple-element.84), channel_id=1, source_target_pairs={{0,2},{1,3},{2,0},{3,1},{4,6},{5,7},{6,4},{7,5},{8,10},{9,11},{10,... | collective-permute-start | bytes 393224 | tf_op jit(solution)/shard_map/ppermute | solution.py:338
  78.5 12.5 %collective-permute-start.17 = (bf16[512,128]{1,0:T(8,128)(2,1)S(1)}, bf16[512,128]{1,0:T(8,128)(2,1)S(1)}, u32[]{:S(2)}, u32[]{:S(2)}) collective-permute-start(bf16[512,128]{1,0:T(8,128)(2,1)S(1)} %get-tuple-element.85), channel_id=1, source_target_pairs={{0,4},{1,5},{2,6},{3,7},{4,0},{5,1},{6,2},{7,3},{8,12},{9,13},{10,... | collective-permute-start | bytes 393224 | tf_op jit(solution)/shard_map/ppermute | solution.py:338
  79.1 11.9 %collective-permute-start.18 = (bf16[512,128]{1,0:T(8,128)(2,1)S(1)}, bf16[512,128]{1,0:T(8,128)(2,1)S(1)}, u32[]{:S(2)}, u32[]{:S(2)}) collective-permute-start(bf16[512,128]{1,0:T(8,128)(2,1)S(1)} %get-tuple-element.86), channel_id=1, source_target_pairs={{0,6},{1,7},{2,4},{3,5},{4,2},{5,3},{6,0},{7,1},{8,14},{9,15},{10,... | collective-permute-start | bytes 393224 | tf_op jit(solution)/shard_map/ppermute | solution.py:338
  88.3 5.9 %collective-permute-start.27 = (bf16[512,128]{1,0:T(8,128)(2,1)S(1)}, bf16[512,128]{1,0:T(8,128)(2,1)S(1)}, u32[]{:S(2)}, u32[]{:S(2)}) collective-permute-start(bf16[512,128]{1,0:T(8,128)(2,1)S(1)} %get-tuple-element.106), channel_id=1, source_target_pairs={{0,4},{1,5},{2,6},{3,7},{4,0},{5,1},{6,2},{7,3},{8,12},{9,13},{10,... | collective-permute-start | bytes 393224 | tf_op jit(solution)/shard_map/ppermute | solution.py:338
  (12 other events, 61.8 us)

commit v7 on v6

--- a/solution.py
+++ b/solution.py
@@ -313,7 +313,7 @@
 RELAY = False
 SUMS = ((0, 1), (1, 1), (2, 1))
 BLOCK = 256
-AHEAD = 5
+AHEAD = 16
 PACK_VMEM = 58 * 1024 * 1024
 SEEN_FLOPS = 7_500_000_000
 FIRST_FLOPS = 5_000_000_000
@@ -337,7 +337,7 @@
                 pairs.append((zz * lay.C + cc, to))
         return lax.ppermute(x, ("row", "col"), pairs)
 
-    cut = tile_values.shape[0] * AHEAD // 8
+    cut = tile_values.shape[0] * AHEAD // 24
     val1 = [exchange(x, dh=1) for x in (tile_values[:cut], tile_values[cut:])]
     val2 = exchange(tile_values, core=1)
     val3 = [exchange(x, core=1) for x in val1]

time: 101 us -> 101 us (level)
  starting transfers between devices: 37.5 us -> 39 us
  Pallas kernels: 24.8 us -> 23.4 us
    ppermute x32, starting transfers between devices: 32.6 us -> 34.1 us  [exchange(): return lax.ppermute(x, ('row', 'col'), pairs)]
    pallas_call x21, Pallas kernels: 24.8 us -> 23.4 us  [apply(): *outs, token = run(*args, *behind)]
  transfers between devices with their start and end apart: 33 -> 33, of which waited for: 9 -> 10; matrix products, arithmetic and copies ran while one was open for 0% -> 0% of each run, Pallas kernels for 23% -> 22%
where the time goes in v7:
time: 101 us
  starting transfers between devices  39 us (39%)
  waiting for transfers between devices  36.4 us (36%)
  Pallas kernels  23.4 us (23%)
  local copies, waits for them, and re-layouts  1.18 us (1%)
  between operations  1.02 us (1%)
    ppermute x32, waiting for transfers between devices, exchange(): return lax.ppermute(x, ('row', 'col'), pairs)  36.4 us
    ppermute x32, starting transfers between devices, exchange(): return lax.ppermute(x, ('row', 'col'), pairs)  34.1 us
    pallas_call x21, Pallas kernels, apply(): *outs, token = run(*args, *behind)  23.4 us
    all_to_all x1, starting transfers between devices, local(): lax.all_to_all(outgoing, ('row', 'col'), split_axis=0, concat_axis=0, til...  4.84 us
  transfers between devices with their start and end apart: 33, of which 10 were waited for; matrix products, arithmetic and copies ran while one was open for 0% of the time, Pallas kernels for 22%

profile of v7, /device:TPU:0, one launch (start us, length us, event | category | flops | bytes accessed | tf_op | source)
XLA Modules:
  0.0 101.0 jit_solution(18053769846674438141)
XLA Ops:
  1.2 3.1 %collective-permute-start = (bf16[16,128,128]{2,1,0:T(8,128)(2,1)S(1)}, bf16[16,128,128]{2,1,0:T(8,128)(2,1)S(1)}, u32[]{:S(2)}, u32[]{:S(2)}) collective-permute-start(bf16[16,128,128]{2,1,0:T(8,128)(2,1)S(1)} %slice.6), channel_id=1, source_target_pairs={{0,8},{1,9},{2,10},{3,11},{4,12},{5,13},{6,14},{7,15},{8,0},{9,1},... | collective-permute-start | bytes 1572872 | tf_op jit(solution)/shard_map/ppermute | solution.py:338
  4.9 3.2 %shard_map.73 = (bf16[32,104,128]{2,1,0:T(8,128)(2,1)}, f32[8,128]{1,0:T(8,128)}) custom-call(s32[1]{0:T(128)S(6)} %copy.10.refs_0_, s32[1,256]{1,0:T(1,128)} %bitcast.2, s32[2,24]{1,0:T(2,128)} %bitcast.3, bf16[256,1536]{1,0:T(8,128)(2,1)} %refs_3_.1), custom_call_target="tpu_custom_call" | custom-call | tf_op jit(solution)/shard_map/pallas_call | solution.py:68
  8.1 4.8 %all-to-all-start = ((bf16[32,104,128]{2,1,0:T(8,128)(2,1)}), bf16[32,104,128]{2,1,0:T(8,128)(2,1)S(1)}, u32[]{:S(2)}, u32[]{:S(2)}) async-start(bf16[32,104,128]{2,1,0:T(8,128)(2,1)} %get-tuple-element.61), calls=%async_computation | async-start | bytes 1703936 | tf_op jit(solution)/shard_map/all_to_all | solution.py:363
  12.9 3.6 %collective-permute-done.refs_3_ = bf16[16,128,128]{2,1,0:T(8,128)(2,1)S(1)} collective-permute-done((bf16[16,128,128]{2,1,0:T(8,128)(2,1)S(1)}, bf16[16,128,128]{2,1,0:T(8,128)(2,1)S(1)}, u32[]{:S(2)}, u32[]{:S(2)}) %collective-permute-start) | collective-permute-done | bytes 524320 | tf_op jit(solution)/shard_map/ppermute | solution.py:338
  16.6 2.5 %collective-permute-start.3 = (bf16[8,128,128]{2,1,0:T(8,128)(2,1)S(1)}, bf16[8,128,128]{2,1,0:T(8,128)(2,1)}, u32[]{:S(2)}, u32[]{:S(2)}) collective-permute-start(bf16[8,128,128]{2,1,0:T(8,128)(2,1)S(1)} %slice.7), channel_id=1, source_target_pairs={{0,8},{1,9},{2,10},{3,11},{4,12},{5,13},{6,14},{7,15},{8,0},{9,1},... | collective-permute-start | bytes 786440 | tf_op jit(solution)/shard_map/ppermute | solution.py:338
  19.4 16.2 %collective-permute-done.3.refs_4_ = bf16[8,128,128]{2,1,0:T(8,128)(2,1)} collective-permute-done((bf16[8,128,128]{2,1,0:T(8,128)(2,1)S(1)}, bf16[8,128,128]{2,1,0:T(8,128)(2,1)}, u32[]{:S(2)}, u32[]{:S(2)}) %collective-permute-start.3) | collective-permute-done | bytes 262176 | tf_op jit(solution)/shard_map/ppermute | solution.py:338
  36.1 1.7 %collective-permute-start.5 = (bf16[512,128]{1,0:T(8,128)(2,1)S(1)}, bf16[512,128]{1,0:T(8,128)(2,1)S(1)}, u32[]{:S(2)}, u32[]{:S(2)}) collective-permute-start(bf16[512,128]{1,0:T(8,128)(2,1)S(1)} %get-tuple-element.62.refs_2_.refs_1_), channel_id=1, source_target_pairs={{0,2},{1,3},{2,0},{3,1},{4,6},{5,7},{6,4},{7,5},{8,10},{9,11},{10,... | collective-permute-start | bytes 393224 | tf_op jit(solution)/shard_map/ppermute | solution.py:338
  37.8 1.5 %collective-permute-start.6 = (bf16[512,128]{1,0:T(8,128)(2,1)S(1)}, bf16[512,128]{1,0:T(8,128)(2,1)S(1)}, u32[]{:S(2)}, u32[]{:S(2)}) collective-permute-start(bf16[512,128]{1,0:T(8,128)(2,1)S(1)} %get-tuple-element.62.refs_2_.refs_1_), channel_id=1, source_target_pairs={{0,4},{1,5},{2,6},{3,7},{4,0},{5,1},{6,2},{7,3},{8,12},{9,13},{10,... | collective-permute-start | bytes 393224 | tf_op jit(solution)/shard_map/ppermute | solution.py:338
  39.6 3.0 %shard_map.76 = (bf16[1024,1152]{1,0:T(8,128)(2,1)S(1)}, bf16[1024,1152]{1,0:T(8,128)(2,1)S(1)}, f32[8,128]{1,0:T(8,128)S(1)}) custom-call(s32[8,128]{1,0:T(8,128)S(1)} %get-tuple-element.63.refs_0_, bf16[24,128,128]{2,1,0:T(8,128)(2,1)S(1)} %copy-done, bf16[24,128,128]{2,1,0:T(8,128)(2,1)S(1)} %collective-permute-done.2.refs_2_, ...), custom_call_target="tpu_custom_call" | custom-call | tf_op jit(solution)/shard_map/pallas_call | solution.py:68
  43.1 1.7 %collective-permute-start.8 = (bf16[512,128]{1,0:T(8,128)(2,1)S(1)}, bf16[512,128]{1,0:T(8,128)(2,1)S(1)}, u32[]{:S(2)}, u32[]{:S(2)}) collective-permute-start(bf16[512,128]{1,0:T(8,128)(2,1)S(1)} %get-tuple-element.66.refs_2_), channel_id=1, source_target_pairs={{0,2},{1,3},{2,0},{3,1},{4,6},{5,7},{6,4},{7,5},{8,10},{9,11},{10,... | collective-permute-start | bytes 393224 | tf_op jit(solution)/shard_map/ppermute | solution.py:338
  44.8 1.5 %collective-permute-start.9 = (bf16[512,128]{1,0:T(8,128)(2,1)S(1)}, bf16[512,128]{1,0:T(8,128)(2,1)S(1)}, u32[]{:S(2)}, u32[]{:S(2)}) collective-permute-start(bf16[512,128]{1,0:T(8,128)(2,1)S(1)} %get-tuple-element.66.refs_2_), channel_id=1, source_target_pairs={{0,4},{1,5},{2,6},{3,7},{4,0},{5,1},{6,2},{7,3},{8,12},{9,13},{10,... | collective-permute-start | bytes 393224 | tf_op jit(solution)/shard_map/ppermute | solution.py:338
  47.7 2.7 %collective-permute-start.12 = (bf16[1024,128]{1,0:T(8,128)(2,1)S(1)}, bf16[1024,128]{1,0:T(8,128)(2,1)S(1)}, u32[]{:S(2)}, u32[]{:S(2)}) collective-permute-start(bf16[1024,128]{1,0:T(8,128)(2,1)S(1)} %get-tuple-element.77.refs_1_), channel_id=1, source_target_pairs={{0,16},{1,17},{2,18},{3,19},{4,20},{5,21},{6,22},{7,23},{8,24},{9,... | collective-permute-start | bytes 786440 | tf_op jit(solution)/shard_map/ppermute | solution.py:338
  50.3 1.4 %collective-permute-start.10 = (bf16[512,128]{1,0:T(8,128)(2,1)S(1)}, bf16[512,128]{1,0:T(8,128)(2,1)S(1)}, u32[]{:S(2)}, u32[]{:S(2)}) collective-permute-start(bf16[512,128]{1,0:T(8,128)(2,1)S(1)} %collective-permute-done.8.refs_3_), channel_id=1, source_target_pairs={{0,4},{1,5},{2,6},{3,7},{4,0},{5,1},{6,2},{7,3},{8,12},{9,13},{10,... | collective-permute-start | bytes 393224 | tf_op jit(solution)/shard_map/ppermute | solution.py:338
  53.9 1.7 %collective-permute-start.15 = (bf16[512,128]{1,0:T(8,128)(2,1)S(1)}, bf16[512,128]{1,0:T(8,128)(2,1)S(1)}, u32[]{:S(2)}, u32[]{:S(2)}) collective-permute-start(bf16[512,128]{1,0:T(8,128)(2,1)S(1)} %get-tuple-element.71.refs_2_.refs_3_), channel_id=1, source_target_pairs={{0,6},{1,7},{2,4},{3,5},{4,2},{5,3},{6,0},{7,1},{8,14},{9,15},{10,... | collective-permute-start | bytes 393224 | tf_op jit(solution)/shard_map/ppermute | solution.py:338
  55.7 1.6 %collective-permute-done.10.refs_5_ = bf16[512,128]{1,0:T(8,128)(2,1)S(1)} collective-permute-done((bf16[512,128]{1,0:T(8,128)(2,1)S(1)}, bf16[512,128]{1,0:T(8,128)(2,1)S(1)}, u32[]{:S(2)}, u32[]{:S(2)}) %collective-permute-start.10) | collective-permute-done | bytes 131104 | tf_op jit(solution)/shard_map/ppermute | solution.py:338
  58.6 2.2 %shard_map.81 = (bf16[1152,1024]{1,0:T(8,128)(2,1)S(1)}, bf16[1152,1024]{1,0:T(8,128)(2,1)S(1)}, f32[8,128]{1,0:T(8,128)S(1)}) custom-call(s32[8,128]{1,0:T(8,128)S(1)} %get-tuple-element.63.refs_0_, bf16[24,128,128]{2,1,0:T(8,128)(2,1)S(1)} %copy-done, bf16[24,128,128]{2,1,0:T(8,128)(2,1)S(1)} %collective-permute-done.2.refs_2_, ...), custom_call_target="tpu_custom_call" | custom-call | tf_op jit(solution)/shard_map/pallas_call | solution.py:68
  60.9 7.5 %collective-permute-done.12.refs_7_.refs_2_ = bf16[1024,128]{1,0:T(8,128)(2,1)S(1)} collective-permute-done((bf16[1024,128]{1,0:T(8,128)(2,1)S(1)}, bf16[1024,128]{1,0:T(8,128)(2,1)S(1)}, u32[]{:S(2)}, u32[]{:S(2)}) %collective-permute-start.12) | collective-permute-done | bytes 262176 | tf_op jit(solution)/shard_map/ppermute | solution.py:338
  71.0 1.7 %collective-permute-start.19 = (bf16[512,128]{1,0:T(8,128)(2,1)S(1)}, bf16[512,128]{1,0:T(8,128)(2,1)S(1)}, u32[]{:S(2)}, u32[]{:S(2)}) collective-permute-start(bf16[512,128]{1,0:T(8,128)(2,1)S(1)} %get-tuple-element.89), channel_id=1, source_target_pairs={{0,2},{1,3},{2,0},{3,1},{4,6},{5,7},{6,4},{7,5},{8,10},{9,11},{10,... | collective-permute-start | bytes 393224 | tf_op jit(solution)/shard_map/ppermute | solution.py:338
  76.9 1.7 %collective-permute-start.16 = (bf16[512,128]{1,0:T(8,128)(2,1)S(1)}, bf16[512,128]{1,0:T(8,128)(2,1)S(1)}, u32[]{:S(2)}, u32[]{:S(2)}) collective-permute-start(bf16[512,128]{1,0:T(8,128)(2,1)S(1)} %get-tuple-element.84), channel_id=1, source_target_pairs={{0,2},{1,3},{2,0},{3,1},{4,6},{5,7},{6,4},{7,5},{8,10},{9,11},{10,... | collective-permute-start | bytes 393224 | tf_op jit(solution)/shard_map/ppermute | solution.py:338
  79.2 1.6 %collective-permute-start.18 = (bf16[512,128]{1,0:T(8,128)(2,1)S(1)}, bf16[512,128]{1,0:T(8,128)(2,1)S(1)}, u32[]{:S(2)}, u32[]{:S(2)}) collective-permute-start(bf16[512,128]{1,0:T(8,128)(2,1)S(1)} %get-tuple-element.86), channel_id=1, source_target_pairs={{0,6},{1,7},{2,4},{3,5},{4,2},{5,3},{6,0},{7,1},{8,14},{9,15},{10,... | collective-permute-start | bytes 393224 | tf_op jit(solution)/shard_map/ppermute | solution.py:338
  82.0 3.3 %collective-permute-done.22.refs_2_ = bf16[1024,128]{1,0:T(8,128)(2,1)S(1)} collective-permute-done((bf16[1024,128]{1,0:T(8,128)(2,1)S(1)}, bf16[1024,128]{1,0:T(8,128)(2,1)S(1)}, u32[]{:S(2)}, u32[]{:S(2)}) %collective-permute-start.22) | collective-permute-done | bytes 262176 | tf_op jit(solution)/shard_map/ppermute | solution.py:338
  86.6 1.7 %collective-permute-start.26 = (bf16[512,128]{1,0:T(8,128)(2,1)S(1)}, bf16[512,128]{1,0:T(8,128)(2,1)S(1)}, u32[]{:S(2)}, u32[]{:S(2)}) collective-permute-start(bf16[512,128]{1,0:T(8,128)(2,1)S(1)} %get-tuple-element.105), channel_id=1, source_target_pairs={{0,2},{1,3},{2,0},{3,1},{4,6},{5,7},{6,4},{7,5},{8,10},{9,11},{10,... | collective-permute-start | bytes 393224 | tf_op jit(solution)/shard_map/ppermute | solution.py:338
  93.4 1.4 %collective-permute-done.28.refs_7_ = bf16[512,128]{1,0:T(8,128)(2,1)S(1)} collective-permute-done((bf16[512,128]{1,0:T(8,128)(2,1)S(1)}, bf16[512,128]{1,0:T(8,128)(2,1)S(1)}, u32[]{:S(2)}, u32[]{:S(2)}) %collective-permute-start.28) | collective-permute-done | bytes 131104 | tf_op jit(solution)/shard_map/ppermute | solution.py:338
  99.5 1.3 %shard_map.93 = (f32[128,1536]{1,0:T(8,128)}, f32[8,128]{1,0:T(8,128)}) custom-call(f32[128,1536]{1,0:T(8,128)} %get-tuple-element.110.refs_0_, f32[128,128]{1,0:T(8,128)S(1)} %get-tuple-element.111.refs_1_, bf16[128,128]{1,0:T(8,128)(2,1)S(1)} %collective-permute-done.29.refs_2_, ...), custom_call_target="tpu_custom_call", output_to_operand_aliasing={{0}: (0, {})} | custom-call | tf_op jit(solution)/shard_map/pallas_call | solution.py:68
  (71 shorter events, 27.1 us)
Async XLA Ops:
  1.2 15.4 %collective-permute-start = (bf16[16,128,128]{2,1,0:T(8,128)(2,1)S(1)}, bf16[16,128,128]{2,1,0:T(8,128)(2,1)S(1)}, u32[]{:S(2)}, u32[]{:S(2)}) collective-permute-start(bf16[16,128,128]{2,1,0:T(8,128)(2,1)S(1)} %slice.6), channel_id=1, source_target_pairs={{0,8},{1,9},{2,10},{3,11},{4,12},{5,13},{6,14},{7,15},{8,0},{9,1},... | collective-permute-start | bytes 1572872 | tf_op jit(solution)/shard_map/ppermute | solution.py:338
  8.1 27.5 %all-to-all-start = ((bf16[32,104,128]{2,1,0:T(8,128)(2,1)}), bf16[32,104,128]{2,1,0:T(8,128)(2,1)S(1)}, u32[]{:S(2)}, u32[]{:S(2)}) async-start(bf16[32,104,128]{2,1,0:T(8,128)(2,1)} %get-tuple-element.61), calls=%async_computation | async-start | bytes 1703936 | tf_op jit(solution)/shard_map/all_to_all | solution.py:363
  16.6 19.0 %collective-permute-start.1 = (bf16[16,128,128]{2,1,0:T(8,128)(2,1)S(1)}, bf16[16,128,128]{2,1,0:T(8,128)(2,1)S(1)}, u32[]{:S(2)}, u32[]{:S(2)}) collective-permute-start(bf16[16,128,128]{2,1,0:T(8,128)(2,1)S(1)} %collective-permute-done.refs_3_), channel_id=1, source_target_pairs={{0,1},{1,0},{2,3},{3,2},{4,5},{5,4},{6,7},{7,6},{8,9},{9,8},{10,11... | collective-permute-start | bytes 1572872 | tf_op jit(solution)/shard_map/ppermute | solution.py:338
  16.6 19.0 %collective-permute-start.3 = (bf16[8,128,128]{2,1,0:T(8,128)(2,1)S(1)}, bf16[8,128,128]{2,1,0:T(8,128)(2,1)}, u32[]{:S(2)}, u32[]{:S(2)}) collective-permute-start(bf16[8,128,128]{2,1,0:T(8,128)(2,1)S(1)} %slice.7), channel_id=1, source_target_pairs={{0,8},{1,9},{2,10},{3,11},{4,12},{5,13},{6,14},{7,15},{8,0},{9,1},... | collective-permute-start | bytes 786440 | tf_op jit(solution)/shard_map/ppermute | solution.py:338
  19.2 20.5 %collective-permute-start.2 = (bf16[24,128,128]{2,1,0:T(8,128)(2,1)S(1)}, bf16[24,128,128]{2,1,0:T(8,128)(2,1)S(1)}, u32[]{:S(2)}, u32[]{:S(2)}) collective-permute-start(bf16[24,128,128]{2,1,0:T(8,128)(2,1)S(1)} %copy-done), channel_id=1, source_target_pairs={{0,1},{1,0},{2,3},{3,2},{4,5},{5,4},{6,7},{7,6},{8,9},{9,8},{10,11... | collective-permute-start | bytes 2359304 | tf_op jit(solution)/shard_map/ppermute | solution.py:338
  36.1 10.3 %collective-permute-start.5 = (bf16[512,128]{1,0:T(8,128)(2,1)S(1)}, bf16[512,128]{1,0:T(8,128)(2,1)S(1)}, u32[]{:S(2)}, u32[]{:S(2)}) collective-permute-start(bf16[512,128]{1,0:T(8,128)(2,1)S(1)} %get-tuple-element.62.refs_2_.refs_1_), channel_id=1, source_target_pairs={{0,2},{1,3},{2,0},{3,1},{4,6},{5,7},{6,4},{7,5},{8,10},{9,11},{10,... | collective-permute-start | bytes 393224 | tf_op jit(solution)/shard_map/ppermute | solution.py:338
  37.8 8.6 %collective-permute-start.6 = (bf16[512,128]{1,0:T(8,128)(2,1)S(1)}, bf16[512,128]{1,0:T(8,128)(2,1)S(1)}, u32[]{:S(2)}, u32[]{:S(2)}) collective-permute-start(bf16[512,128]{1,0:T(8,128)(2,1)S(1)} %get-tuple-element.62.refs_2_.refs_1_), channel_id=1, source_target_pairs={{0,4},{1,5},{2,6},{3,7},{4,0},{5,1},{6,2},{7,3},{8,12},{9,13},{10,... | collective-permute-start | bytes 393224 | tf_op jit(solution)/shard_map/ppermute | solution.py:338
  39.3 7.1 %collective-permute-start.7 = (bf16[512,128]{1,0:T(8,128)(2,1)S(1)}, bf16[512,128]{1,0:T(8,128)(2,1)S(1)}, u32[]{:S(2)}, u32[]{:S(2)}) collective-permute-start(bf16[512,128]{1,0:T(8,128)(2,1)S(1)} %get-tuple-element.62.refs_2_.refs_1_), channel_id=1, source_target_pairs={{0,6},{1,7},{2,4},{3,5},{4,2},{5,3},{6,0},{7,1},{8,14},{9,15},{10,... | collective-permute-start | bytes 393224 | tf_op jit(solution)/shard_map/ppermute | solution.py:338
  43.1 7.2 %collective-permute-start.8 = (bf16[512,128]{1,0:T(8,128)(2,1)S(1)}, bf16[512,128]{1,0:T(8,128)(2,1)S(1)}, u32[]{:S(2)}, u32[]{:S(2)}) collective-permute-start(bf16[512,128]{1,0:T(8,128)(2,1)S(1)} %get-tuple-element.66.refs_2_), channel_id=1, source_target_pairs={{0,2},{1,3},{2,0},{3,1},{4,6},{5,7},{6,4},{7,5},{8,10},{9,11},{10,... | collective-permute-start | bytes 393224 | tf_op jit(solution)/shard_map/ppermute | solution.py:338
  44.8 9.1 %collective-permute-start.9 = (bf16[512,128]{1,0:T(8,128)(2,1)S(1)}, bf16[512,128]{1,0:T(8,128)(2,1)S(1)}, u32[]{:S(2)}, u32[]{:S(2)}) collective-permute-start(bf16[512,128]{1,0:T(8,128)(2,1)S(1)} %get-tuple-element.66.refs_2_), channel_id=1, source_target_pairs={{0,4},{1,5},{2,6},{3,7},{4,0},{5,1},{6,2},{7,3},{8,12},{9,13},{10,... | collective-permute-start | bytes 393224 | tf_op jit(solution)/shard_map/ppermute | solution.py:338
  47.7 20.7 %collective-permute-start.12 = (bf16[1024,128]{1,0:T(8,128)(2,1)S(1)}, bf16[1024,128]{1,0:T(8,128)(2,1)S(1)}, u32[]{:S(2)}, u32[]{:S(2)}) collective-permute-start(bf16[1024,128]{1,0:T(8,128)(2,1)S(1)} %get-tuple-element.77.refs_1_), channel_id=1, source_target_pairs={{0,16},{1,17},{2,18},{3,19},{4,20},{5,21},{6,22},{7,23},{8,24},{9,... | collective-permute-start | bytes 786440 | tf_op jit(solution)/shard_map/ppermute | solution.py:338
  50.3 6.9 %collective-permute-start.10 = (bf16[512,128]{1,0:T(8,128)(2,1)S(1)}, bf16[512,128]{1,0:T(8,128)(2,1)S(1)}, u32[]{:S(2)}, u32[]{:S(2)}) collective-permute-start(bf16[512,128]{1,0:T(8,128)(2,1)S(1)} %collective-permute-done.8.refs_3_), channel_id=1, source_target_pairs={{0,4},{1,5},{2,6},{3,7},{4,0},{5,1},{6,2},{7,3},{8,12},{9,13},{10,... | collective-permute-start | bytes 393224 | tf_op jit(solution)/shard_map/ppermute | solution.py:338
  52.1 8.7 %collective-permute-start.13 = (bf16[512,128]{1,0:T(8,128)(2,1)S(1)}, bf16[512,128]{1,0:T(8,128)(2,1)S(1)}, u32[]{:S(2)}, u32[]{:S(2)}) collective-permute-start(bf16[512,128]{1,0:T(8,128)(2,1)S(1)} %get-tuple-element.71.refs_2_.refs_3_), channel_id=1, source_target_pairs={{0,2},{1,3},{2,0},{3,1},{4,6},{5,7},{6,4},{7,5},{8,10},{9,11},{10,... | collective-permute-start | bytes 393224 | tf_op jit(solution)/shard_map/ppermute | solution.py:338
  52.7 8.2 %collective-permute-start.14 = (bf16[512,128]{1,0:T(8,128)(2,1)S(1)}, bf16[512,128]{1,0:T(8,128)(2,1)S(1)}, u32[]{:S(2)}, u32[]{:S(2)}) collective-permute-start(bf16[512,128]{1,0:T(8,128)(2,1)S(1)} %get-tuple-element.71.refs_2_.refs_3_), channel_id=1, source_target_pairs={{0,4},{1,5},{2,6},{3,7},{4,0},{5,1},{6,2},{7,3},{8,12},{9,13},{10,... | collective-permute-start | bytes 393224 | tf_op jit(solution)/shard_map/ppermute | solution.py:338
  53.9 7.0 %collective-permute-start.15 = (bf16[512,128]{1,0:T(8,128)(2,1)S(1)}, bf16[512,128]{1,0:T(8,128)(2,1)S(1)}, u32[]{:S(2)}, u32[]{:S(2)}) collective-permute-start(bf16[512,128]{1,0:T(8,128)(2,1)S(1)} %get-tuple-element.71.refs_2_.refs_3_), channel_id=1, source_target_pairs={{0,6},{1,7},{2,4},{3,5},{4,2},{5,3},{6,0},{7,1},{8,14},{9,15},{10,... | collective-permute-start | bytes 393224 | tf_op jit(solution)/shard_map/ppermute | solution.py:338
  58.5 17.0 %collective-permute-start.11 = (bf16[1024,128]{1,0:T(8,128)(2,1)S(1)}, bf16[1024,128]{1,0:T(8,128)(2,1)S(1)}, u32[]{:S(2)}, u32[]{:S(2)}) collective-permute-start(bf16[1024,128]{1,0:T(8,128)(2,1)S(1)} %get-tuple-element.76.refs_1_), channel_id=1, source_target_pairs={{0,16},{1,17},{2,18},{3,19},{4,20},{5,21},{6,22},{7,23},{8,24},{9,... | collective-permute-start | bytes 786440 | tf_op jit(solution)/shard_map/ppermute | solution.py:338
  71.0 7.6 %collective-permute-start.19 = (bf16[512,128]{1,0:T(8,128)(2,1)S(1)}, bf16[512,128]{1,0:T(8,128)(2,1)S(1)}, u32[]{:S(2)}, u32[]{:S(2)}) collective-permute-start(bf16[512,128]{1,0:T(8,128)(2,1)S(1)} %get-tuple-element.89), channel_id=1, source_target_pairs={{0,2},{1,3},{2,0},{3,1},{4,6},{5,7},{6,4},{7,5},{8,10},{9,11},{10,... | collective-permute-start | bytes 393224 | tf_op jit(solution)/shard_map/ppermute | solution.py:338
  72.7 6.4 %collective-permute-start.20 = (bf16[512,128]{1,0:T(8,128)(2,1)S(1)}, bf16[512,128]{1,0:T(8,128)(2,1)S(1)}, u32[]{:S(2)}, u32[]{:S(2)}) collective-permute-start(bf16[512,128]{1,0:T(8,128)(2,1)S(1)} %get-tuple-element.90), channel_id=1, source_target_pairs={{0,4},{1,5},{2,6},{3,7},{4,0},{5,1},{6,2},{7,3},{8,12},{9,13},{10,... | collective-permute-start | bytes 393224 | tf_op jit(solution)/shard_map/ppermute | solution.py:338
  73.3 7.4 %collective-permute-start.21 = (bf16[512,128]{1,0:T(8,128)(2,1)S(1)}, bf16[512,128]{1,0:T(8,128)(2,1)S(1)}, u32[]{:S(2)}, u32[]{:S(2)}) collective-permute-start(bf16[512,128]{1,0:T(8,128)(2,1)S(1)} %get-tuple-element.91), channel_id=1, source_target_pairs={{0,6},{1,7},{2,4},{3,5},{4,2},{5,3},{6,0},{7,1},{8,14},{9,15},{10,... | collective-permute-start | bytes 393224 | tf_op jit(solution)/shard_map/ppermute | solution.py:338
  74.6 10.7 %collective-permute-start.22 = (bf16[1024,128]{1,0:T(8,128)(2,1)S(1)}, bf16[1024,128]{1,0:T(8,128)(2,1)S(1)}, u32[]{:S(2)}, u32[]{:S(2)}) collective-permute-start(bf16[1024,128]{1,0:T(8,128)(2,1)S(1)} %get-tuple-element.96.refs_1_), channel_id=1, source_target_pairs={{0,16},{1,17},{2,18},{3,19},{4,20},{5,21},{6,22},{7,23},{8,24},{9,... | collective-permute-start | bytes 786440 | tf_op jit(solution)/shard_map/ppermute | solution.py:338
  76.9 12.0 %collective-permute-start.16 = (bf16[512,128]{1,0:T(8,128)(2,1)S(1)}, bf16[512,128]{1,0:T(8,128)(2,1)S(1)}, u32[]{:S(2)}, u32[]{:S(2)}) collective-permute-start(bf16[512,128]{1,0:T(8,128)(2,1)S(1)} %get-tuple-element.84), channel_id=1, source_target_pairs={{0,2},{1,3},{2,0},{3,1},{4,6},{5,7},{6,4},{7,5},{8,10},{9,11},{10,... | collective-permute-start | bytes 393224 | tf_op jit(solution)/shard_map/ppermute | solution.py:338
  78.6 11.6 %collective-permute-start.17 = (bf16[512,128]{1,0:T(8,128)(2,1)S(1)}, bf16[512,128]{1,0:T(8,128)(2,1)S(1)}, u32[]{:S(2)}, u32[]{:S(2)}) collective-permute-start(bf16[512,128]{1,0:T(8,128)(2,1)S(1)} %get-tuple-element.85), channel_id=1, source_target_pairs={{0,4},{1,5},{2,6},{3,7},{4,0},{5,1},{6,2},{7,3},{8,12},{9,13},{10,... | collective-permute-start | bytes 393224 | tf_op jit(solution)/shard_map/ppermute | solution.py:338
  79.2 11.0 %collective-permute-start.18 = (bf16[512,128]{1,0:T(8,128)(2,1)S(1)}, bf16[512,128]{1,0:T(8,128)(2,1)S(1)}, u32[]{:S(2)}, u32[]{:S(2)}) collective-permute-start(bf16[512,128]{1,0:T(8,128)(2,1)S(1)} %get-tuple-element.86), channel_id=1, source_target_pairs={{0,6},{1,7},{2,4},{3,5},{4,2},{5,3},{6,0},{7,1},{8,14},{9,15},{10,... | collective-permute-start | bytes 393224 | tf_op jit(solution)/shard_map/ppermute | solution.py:338
  90.6 6.5 %collective-permute-start.24 = (bf16[128,256]{1,0:T(8,128)(2,1)S(1)}, bf16[128,256]{1,0:T(8,128)(2,1)S(1)}, u32[]{:S(2)}, u32[]{:S(2)}) collective-permute-start(bf16[128,256]{1,0:T(8,128)(2,1)S(1)} %get-tuple-element.101), channel_id=1, source_target_pairs={{0,8},{1,9},{2,10},{3,11},{4,12},{5,13},{6,14},{7,15},{8,0},{9,1},... | collective-permute-start | bytes 196616 | tf_op jit(solution)/shard_map/ppermute | solution.py:338
  (12 other events, 64.2 us)
